TPU v7x, 128 devices: a whole 4x4x4 slice. The times are simulated.
128 devices in a mesh: az: 16 (over z_hi, x, core), gz: 8 (over y, z_lo).
Axes of the slice: x: 4, y: 4, z: 4 (z_hi: 2, z_lo: 2; z = z_hi * 2 + z_lo), core: 2. Of those that a mesh axis runs over, the one named last changes fastest.
Arguments:
- pressure: float32 [512, 64, 512], P('az', 'gz'), may hold values from -6 to 6
- divergence: float32 [512, 64, 512], P('az', 'gz'), may hold values from -6 to 6
- void_fraction: float32 [512, 64, 512], P('az', 'gz'), may hold values from 0 to 0.8
- bubble_volume: float32 [16384], P(('az', 'gz')), may hold values from 0.5 to 5
- bubble_count: int32 [128], P(('az', 'gz')), may hold values from 16 to 128, as said below
- bubble_cell: int32 [16384], P(('az', 'gz')), may hold values from 0 to 131071
Outputs:
- pressure_out: float32 [512, 64, 512], P('az', 'gz')
- scaled_residual: float32 [512, 64, 512], P('az', 'gz')
Inputs may be any that keep to these rules, and one draw needn't show every extreme that they name: `bubble_count`: bubble slots below the count are live; the devices of three neighbouring azimuth owners have all 128 slots live in every draw.
All inputs are finite; a program needn't handle non-finite values.
Results may differ from a plain program's by a relative error of at most 0.0003.
Values sent between devices are 32-bit elements; how exact they have to be, the bound alone decides.
No kernel may reach another device: no remote copies, remote signals or barrier semaphores. Data moves between devices by JAX's collectives and lax.ppermute only.
A program may use at most 256 MiB of HBM per device.

v0:
```python
import math

import jax
import jax.numpy as jnp
from jax import lax
from jax.sharding import PartitionSpec as P

LEVELS = 4
SWEEPS = 1
COARSE_SWEEPS = 32
GATHER_LEVEL = 2


SIGMA = 0.02
OMEGA = 0.8


def padded_2(x, sides, width):
    for axis, dim in sides:
        count, length = (lax.axis_size(axis), x.shape[dim])
        up = [(i, (i + 1) % count) for i in range(count)]
        down = [(j, i) for i, j in up]
        last = lax.slice_in_dim(x, length - width, length, axis=dim)
        initial = lax.slice_in_dim(x, 0, width, axis=dim)
        before = lax.ppermute(last, axis, up)
        after = lax.ppermute(initial, axis, down)
        x = jnp.concatenate([before, x, after], axis=dim)
    return x


def passed_along(value, axis, steps):
    count = lax.axis_size(axis)
    pairs = [(source, (source + steps) % count) for source in range(count)]
    return lax.ppermute(value, axis, pairs)


def radial_ratios(size):
    positions = jnp.arange(1, size, dtype=jnp.float32)
    return (positions / (positions + 0.5), positions / (positions - 0.5))


def shrink_all(weights):
    return tuple((member for member in weights))


def face_weights(extended, margin, level_no, z_first, z_total, a_total):
    ext_az, ext_ht, rad_n = extended.shape
    angle_step = 2.0 * math.pi / a_total
    radius = jnp.arange(rad_n, dtype=jnp.float32) + 0.5
    metric = (radius * angle_step) ** 2
    az_face = 0.5 * (extended[:-1] + extended[1:]) / metric
    heights = z_first - margin + jnp.arange(ext_ht, dtype=jnp.int32)
    inside = ((heights[:-1] >= 0) & (heights[1:] <= z_total - 1)).astype(jnp.float32)
    z_face = 0.5 * (extended[:, :-1] + extended[:, 1:]) * inside[None, :, None]
    r_face = 0.5 * (extended[:, :, :-1] + extended[:, :, 1:])
    inward, outward = radial_ratios(rad_n)
    zero_r = jnp.zeros((ext_az, ext_ht, 1), jnp.float32)
    wr_inner = jnp.concatenate([zero_r, r_face * inward], 2)[1:-1, 1:-1]
    wr_outer = jnp.concatenate([r_face * outward, zero_r], 2)[1:-1, 1:-1]
    wa_minus = az_face[:-1, 1:-1]
    wa_plus = az_face[1:, 1:-1]
    wz_minus = z_face[1:-1, :-1]
    wz_plus = z_face[1:-1, 1:]
    diagonal = wa_minus + wa_plus + wz_minus + wz_plus + wr_inner + wr_outer + SIGMA * 4.0**level_no
    return (wa_minus, wa_plus, wz_minus, wz_plus, wr_inner, wr_outer, diagonal)


def apply_ext(padded, weights):
    wa_minus, wa_plus, wz_minus, wz_plus, wr_inner, wr_outer, diagonal = weights
    center = padded[1:-1, 1:-1]
    zero_r = jnp.zeros(center.shape[:2] + (1,), jnp.float32)
    inner = jnp.concatenate([zero_r, center[:, :, :-1]], 2)
    outer = jnp.concatenate([center[:, :, 1:], zero_r], 2)
    neighbours = (
        wa_minus * padded[:-2, 1:-1]
        + wa_plus * padded[2:, 1:-1]
        + wz_minus * padded[1:-1, :-2]
        + wz_plus * padded[1:-1, 2:]
        + wr_inner * inner
        + wr_outer * outer
    )
    return diagonal * center - neighbours


def jacobi_sweep(padded, source_part, weights):
    center = padded[1:-1, 1:-1]
    return center + OMEGA * (source_part - apply_ext(padded, weights)) / weights[6]


def smooth(iterate, source_ext, weights, margin, sweep_count, widen):
    finished = 0
    while finished < sweep_count:
        padded = widen(iterate)
        current = margin
        taken = min(margin, sweep_count - finished)
        padded = jacobi_sweep(padded, source_ext, shrink_all(weights))
        current = current - 1
        iterate = padded
        finished = finished + taken
    return iterate


def residual(iterate, source_term, weights, widen):
    applied = apply_ext(widen(iterate), weights)
    return source_term - applied


def coarsen(array_in):
    az_n, ht_n, rad_n = array_in.shape
    return array_in.reshape(az_n // 2, 2, ht_n // 2, 2, rad_n // 2, 2).sum(axis=(1, 3, 5))


def refine(correction):
    return jnp.repeat(jnp.repeat(jnp.repeat(correction, 2, 0), 2, 1), 2, 2)


def extend_dist(array_in):
    return padded_2(array_in, (("az", 0), ("gz", 1)), 1)


def extend_circle(array_in):
    extended = padded_2(array_in, (("az", 0),), 1)
    zero_z = jnp.zeros((extended.shape[0], 1, extended.shape[2]), jnp.float32)
    return jnp.concatenate([zero_z, extended, zero_z], 1)


def consolidate(array_in):
    gathered = lax.all_gather(array_in, "gz", axis=1, tiled=True)
    return gathered


def own_piece(array_in, ht_own):
    piece = lax.dynamic_slice_in_dim(array_in, lax.axis_index("gz") * ht_own, ht_own, 1)
    return piece


def body(pressure, divergence, void_fraction, bubble_volume, bubble_count, bubble_cell):
    slot_total = bubble_volume.shape[0]
    az_cells, ht_cells, radial_n = pressure.shape
    az_devices = lax.axis_size("az")
    gz_devices = lax.axis_size("gz")
    gz_index = lax.axis_index("gz")
    live_mask = (jnp.arange(slot_total, dtype=jnp.int32) < bubble_count[0]).astype(jnp.float32)
    arrived = passed_along(bubble_volume * live_mask, "az", 1)
    planes = bubble_cell // radial_n
    radial_idx = bubble_cell % radial_n
    plane_hot = (
        planes[:, None] == jnp.arange(az_cells * ht_cells, dtype=jnp.int32)[None, :]
    ).astype(jnp.float32)
    radius_hot = (radial_idx[:, None] == jnp.arange(radial_n, dtype=jnp.int32)[None, :]).astype(
        jnp.float32
    ) * arrived[:, None]
    deposit = lax.dot_general(
        plane_hot, radius_hot, (((0,), (0,)), ((), ())), precision=lax.Precision.HIGHEST
    )
    rhs_zero = divergence + deposit.reshape(az_cells, ht_cells, radial_n)
    margin = 1
    mobility = 1.0 / (1.0 - void_fraction)
    dist_weights = []
    for level_no in range(GATHER_LEVEL):
        if level_no > 0:
            mobility = 0.125 * coarsen(mobility)
        ht_level = mobility.shape[1]
        dist_weights.append(
            face_weights(
                extend_dist(mobility),
                margin,
                level_no,
                gz_index * ht_level,
                ht_level * gz_devices,
                mobility.shape[0] * az_devices,
            )
        )
    mobility = 0.125 * coarsen(mobility)
    az_own, ht_own = (mobility.shape[0], mobility.shape[1])
    mobility = consolidate(mobility)
    circle_weights = {}
    for level_no in range(GATHER_LEVEL, LEVELS):
        if level_no > GATHER_LEVEL:
            mobility = 0.125 * coarsen(mobility)
        circle_weights[level_no] = face_weights(
            extend_circle(mobility),
            1,
            level_no,
            0,
            mobility.shape[1],
            mobility.shape[0] * az_devices,
        )

    def cycle(level_no, iterate, source_term):
        if level_no < GATHER_LEVEL:
            weights = dist_weights[level_no]
            iterate = smooth(iterate, source_term, weights, margin, SWEEPS, extend_dist)
            remainder = residual(iterate, source_term, weights, extend_dist)
            coarse_rhs = 0.5 * coarsen(remainder)
            if level_no + 1 == GATHER_LEVEL:
                coarse_rhs = consolidate(coarse_rhs)
            correction = cycle(level_no + 1, jnp.zeros_like(coarse_rhs), coarse_rhs)
            if level_no + 1 == GATHER_LEVEL:
                correction = own_piece(correction, ht_own)
            iterate = iterate + refine(correction)
            return smooth(iterate, source_term, weights, margin, SWEEPS, extend_dist)
        weights = circle_weights[level_no]
        if level_no == LEVELS - 1:
            return smooth(iterate, source_term, weights, 1, COARSE_SWEEPS, extend_circle)
        iterate = smooth(iterate, source_term, weights, 1, SWEEPS, extend_circle)
        remainder = residual(iterate, source_term, weights, extend_circle)
        coarse_rhs = 0.5 * coarsen(remainder)
        correction = cycle(level_no + 1, jnp.zeros_like(coarse_rhs), coarse_rhs)
        iterate = iterate + refine(correction)
        return smooth(iterate, source_term, weights, 1, SWEEPS, extend_circle)

    pressure_out = cycle(0, pressure, rhs_zero)
    final_rest = residual(pressure_out, rhs_zero, dist_weights[0], extend_dist)
    scaled_residual = final_rest / dist_weights[0][6]
    return (pressure_out, scaled_residual)


def solution(mesh):
    return jax.shard_map(
        body,
        mesh=mesh,
        in_specs=(
            P("az", "gz", None),
            P("az", "gz", None),
            P("az", "gz", None),
            P(("az", "gz")),
            P(("az", "gz")),
            P(("az", "gz")),
        ),
        out_specs=(P("az", "gz", None), P("az", "gz", None)),
        check_vma=False,
    )
```

profile of v0, /device:TPU:0, one launch (start us, length us, event | category | flops | bytes accessed | tf_op | source)
XLA Modules:
  0.0 755.9 jit_solution(14099833745717370731)
XLA Ops:
  0.7 5.7 collective-permute-start.18
  8.8 34.9 %reshape.134 = f32[16,2,4,2,256,2]{5,4,3,2,1,0:T(8,128)} reshape(f32[32,8,512]{2,1,0:T(8,128)S(1)} %subtract_divide_fusion) | data formatting | bytes 1048576 | tf_op jit(solution)/shard_map/reshape | solution.py:110
  43.7 12.2 %reduce_sum.55 = f32[16,4,256]{2,1,0:T(4,128)S(1)} reduce(f32[16,2,4,2,256,2]{5,4,3,2,1,0:T(8,128)} %reshape.134, f32[]{:T(128)} %constant.43.clone.1), dimensions={1,3,5}, to_apply=%region_1.2 | reduce | flops 114688 | bytes 589828 | tf_op jit(solution)/shard_map/reduce_sum | solution.py:110
  56.0 5.5 mul.1341
  64.1 28.5 %all_gather.7 = f32[8,16,128]{2,0,1:T(8,128)S(1)} all-gather(f32[8,2,128]{2,0,1:T(8,128)S(1)} %broadcast_multiply_fusion.11), channel_id=1, replica_groups=mesh['az'=16,'gz'=8] {'gz'}, dimensions={1}, use_global_device_ids=true | all-gather | bytes 73728 | tf_op jit(solution)/shard_map/all_gather | solution.py:128
  93.2 5.5 reshape.137
  128.6 5.4 collective-permute-start.14
  147.2 6.0 collective-permute-done.25
  190.3 6.2 collective-permute-done.3
  214.2 14.1 %fusion.48 = (f32[32,8,512]{0,1,2:T(8,128)S(1)}, f32[32,8,512]{0,1,2:T(8,128)}) fusion(f32[32,8,512]{0,1,2:T(8,128)S(1)} %copy-done.4, f32[34,1,512]{0,1,2:T(1,128)} %copy-done.17, f32[34,8,512]{0,1,2:T(8,128)} %copy.278, f32[34,1,512]{0,1,2:T(1,128)} %copy-done.16, f32[32,8,511]{0,1,2:T(8,128)} %get-tuple-element.37, f32[32,8,511]{0,1,2:T(8,128)} %get-tuple-element.36, ...), kind=kLoop, calls=%fused_computation.79 | loop fusion | flops 3407872 | bytes 8899936 | tf_op jit(solution)/shard_map/add | solution.py:87
  235.4 5.8 collective-permute-start.10
  246.6 5.7 pad_maximum_fusion.39
  262.6 19.8 %fusion.34 = f32[32,8,512]{0,1,2:T(8,128)} fusion(f32[32,8,512]{0,1,2:T(8,128)} %get-tuple-element.13, f32[34,1,512]{0,1,2:T(1,128)} %copy-done.19, f32[1,8,512]{0,1,2:T(8,128)} %copy.288, f32[32,8,512]{0,1,2:T(8,128)S(1)} %get-tuple-element.12, f32[1,8,512]{0,1,2:T(8,128)} %copy.286, f32[34,1,512]{0,1,2:T(1,128)} %copy-done.18, ...), kind=kLoop, calls=%fused_computation.57 | loop fusion | flops 3670016 | bytes 6278496 | tf_op jit(solution)/shard_map/sub | solution.py:105
  284.8 34.9 %reshape.133 = f32[16,2,4,2,256,2]{5,4,3,2,1,0:T(8,128)} reshape(f32[32,8,512]{2,1,0:T(8,128)S(1)} %copy.291) | data formatting | bytes 1048576 | tf_op jit(solution)/shard_map/reshape | solution.py:110
  319.7 12.2 %reduce_sum.54 = f32[16,4,256]{2,1,0:T(4,128)S(1)} reduce(f32[16,2,4,2,256,2]{5,4,3,2,1,0:T(8,128)} %reshape.133, f32[]{:T(128)} %constant.43.clone.1), dimensions={1,3,5}, to_apply=%region_0.1 | reduce | flops 114688 | bytes 589828 | tf_op jit(solution)/shard_map/reduce_sum | solution.py:110
  333.1 5.9 collective-permute-start.22
  346.5 5.5 reshape.135
  354.7 28.2 %all_gather.6 = f32[8,16,128]{2,0,1:T(8,128)S(1)} all-gather(f32[8,2,128]{2,0,1:T(8,128)S(1)} %broadcast_multiply_fusion.12), channel_id=1, replica_groups=mesh['az'=16,'gz'=8] {'gz'}, dimensions={1}, use_global_device_ids=true | all-gather | bytes 73728 | tf_op jit(solution)/shard_map/all_gather | solution.py:128
  391.2 5.5 reshape.136
  447.8 5.6 collective-permute-start.50
  661.9 5.7 pad_maximum_fusion.36
  677.8 23.1 %fusion.23 = f32[32,8,512]{0,1,2:T(8,128)S(1)} fusion(f32[32,8,512]{0,1,2:T(8,128)} %copy-done.1, f32[32,8,512]{0,1,2:T(8,128)} %get-tuple-element.13, f32[34,1,512]{0,1,2:T(1,128)S(1)} %collective-permute-done.106, f32[1,8,512]{0,1,2:T(8,128)} %copy.311, f32[1,8,512]{0,1,2:T(8,128)} %copy.309, f32[34,1,512]{0,1,2:T(1,128)S(1)} %collective-permute-done.105, ...), kind=kLoop, calls=%fused_computation.38 | loop fusion | flops 4063232 | bytes 6278496 | tf_op jit(solution)/shard_map/add | solution.py:87
  717.4 5.7 pad_maximum_fusion.33
  732.6 19.7 %fusion.9 = f32[32,8,512]{0,1,2:T(8,128)} fusion(f32[32,8,512]{0,1,2:T(8,128)} %get-tuple-element.13, f32[34,1,512]{0,1,2:T(1,128)S(1)} %collective-permute-done.110, f32[1,8,512]{0,1,2:T(8,128)} %copy.317, f32[32,8,512]{0,1,2:T(8,128)S(1)} %fusion.23, f32[1,8,512]{0,1,2:T(8,128)} %copy.315, f32[34,1,512]{0,1,2:T(1,128)S(1)} %collective-permute-done.109, ...), kind=kLoop, calls=%fused_computation.16 | loop fusion | flops 3801088 | bytes 6278496 | tf_op jit(solution)/shard_map/div | solution.py:215
  (576 shorter events, 445.3 us)
Async XLA Ops:
  0.6 140.4 %collective-permute-start.17 = (f32[1,4,256]{2,1,0:T(4,128)S(1)}, f32[1,4,256]{2,1,0:T(4,128)S(1)}, u32[]{:S(2)}, u32[]{:S(2)}) collective-permute-start(f32[1,4,256]{2,1,0:T(4,128)S(1)} %broadcast.582), channel_id=1, source_target_pairs={{0,8},{8,16},{16,24},{24,32},{32,40},{40,48},{48,56},{56,64},{64,7... | collective-permute-start | bytes 12296 | tf_op jit(solution)/shard_map/ppermute | solution.py:25
  0.7 145.7 %collective-permute-start.18 = (f32[1,4,256]{2,1,0:T(4,128)S(1)}, f32[1,4,256]{2,1,0:T(4,128)S(1)}, u32[]{:S(2)}, u32[]{:S(2)}) collective-permute-start(f32[1,4,256]{2,1,0:T(4,128)S(1)} %broadcast.582), channel_id=1, source_target_pairs={{8,0},{16,8},{24,16},{32,24},{40,32},{48,40},{56,48},{64,56},{72,6... | collective-permute-start | bytes 12296 | tf_op jit(solution)/shard_map/ppermute | solution.py:26
  7.7 112.6 %collective-permute-start = (f32[128]{0:T(128)S(1)}, f32[128]{0:T(128)S(1)}, u32[]{:S(2)}, u32[]{:S(2)}) collective-permute-start(f32[128]{0:T(128)S(1)} %compare_select_fusion), channel_id=1, source_target_pairs={{0,8},{8,16},{16,24},{24,32},{32,40},{40,48},{48,56},{56,64},{64,7... | collective-permute-start | bytes 1544 | tf_op jit(solution)/shard_map/ppermute | solution.py:34
  101.3 21.7 %collective-permute-start.31 = (f32[1,8,64]{2,1,0:T(8,128)S(1)}, f32[1,8,64]{2,1,0:T(8,128)S(1)}, u32[]{:S(2)}, u32[]{:S(2)}) collective-permute-start(f32[1,8,64]{2,1,0:T(8,128)S(1)} %get-tuple-element.207), channel_id=1, source_target_pairs={{0,8},{8,16},{16,24},{24,32},{32,40},{40,48},{48,56},{56,64},{64,7... | collective-permute-start | bytes 6152 | tf_op jit(solution)/shard_map/ppermute | solution.py:25
  101.4 27.0 %collective-permute-start.32 = (f32[1,8,64]{2,1,0:T(8,128)S(1)}, f32[1,8,64]{2,1,0:T(8,128)S(1)}, u32[]{:S(2)}, u32[]{:S(2)}) collective-permute-start(f32[1,8,64]{2,1,0:T(8,128)S(1)} %get-tuple-element.208), channel_id=1, source_target_pairs={{8,0},{16,8},{24,16},{32,24},{40,32},{48,40},{56,48},{64,56},{72,6... | collective-permute-start | bytes 6152 | tf_op jit(solution)/shard_map/ppermute | solution.py:26
  123.0 11.0 %collective-permute-start.34 = (f32[1,8,64]{2,1,0:T(8,128)S(1)}, f32[1,8,64]{2,1,0:T(8,128)S(1)}, u32[]{:S(2)}, u32[]{:S(2)}) collective-permute-start(f32[1,8,64]{2,1,0:T(8,128)S(1)} %broadcast.596), channel_id=1, source_target_pairs={{8,0},{16,8},{24,16},{32,24},{40,32},{48,40},{56,48},{64,56},{72,6... | collective-permute-start | bytes 6152 | tf_op jit(solution)/shard_map/ppermute | solution.py:26
  128.6 11.6 %collective-permute-start.14 = (f32[1,4,256]{2,1,0:T(4,128)}, f32[1,4,256]{2,1,0:T(4,128)S(1)}, u32[]{:S(2)}, u32[]{:S(2)}) collective-permute-start(f32[1,4,256]{2,1,0:T(4,128)} %get-tuple-element.80), channel_id=1, source_target_pairs={{8,0},{16,8},{24,16},{32,24},{40,32},{48,40},{56,48},{64,56},{72,6... | collective-permute-start | bytes 12296 | tf_op jit(solution)/shard_map/ppermute | solution.py:26
  134.7 204.3 %collective-permute-start.27 = (f32[1,16,128]{2,1,0:T(8,128)}, f32[1,16,128]{2,1,0:T(8,128)}, u32[]{:S(2)}, u32[]{:S(2)}) collective-permute-start(f32[1,16,128]{2,1,0:T(8,128)} %broadcast.590), channel_id=1, source_target_pairs={{0,8},{8,16},{16,24},{24,32},{32,40},{40,48},{48,56},{56,64},{64,7... | collective-permute-start | bytes 24584 | tf_op jit(solution)/shard_map/ppermute | solution.py:25
  135.2 203.7 %collective-permute-start.28 = (f32[1,16,128]{2,1,0:T(8,128)}, f32[1,16,128]{2,1,0:T(8,128)}, u32[]{:S(2)}, u32[]{:S(2)}) collective-permute-start(f32[1,16,128]{2,1,0:T(8,128)} %broadcast.590), channel_id=1, source_target_pairs={{8,0},{16,8},{24,16},{32,24},{40,32},{48,40},{56,48},{64,56},{72,6... | collective-permute-start | bytes 24584 | tf_op jit(solution)/shard_map/ppermute | solution.py:26
  140.3 16.0 %collective-permute-start.1 = (f32[1,8,512]{2,1,0:T(8,128)S(1)}, f32[1,8,512]{2,1,0:T(8,128)S(1)}, u32[]{:S(2)}, u32[]{:S(2)}) collective-permute-start(f32[1,8,512]{2,1,0:T(8,128)S(1)} %copy-done.34), channel_id=1, source_target_pairs={{0,8},{8,16},{16,24},{24,32},{32,40},{40,48},{48,56},{56,64},{64,7... | collective-permute-start | bytes 49160 | tf_op jit(solution)/shard_map/ppermute | solution.py:25
  141.0 20.6 %collective-permute-start.2 = (f32[1,8,512]{2,1,0:T(8,128)S(1)}, f32[1,8,512]{2,1,0:T(8,128)S(1)}, u32[]{:S(2)}, u32[]{:S(2)}) collective-permute-start(f32[1,8,512]{2,1,0:T(8,128)S(1)} %copy-done.33), channel_id=1, source_target_pairs={{8,0},{16,8},{24,16},{32,24},{40,32},{48,40},{56,48},{64,56},{72,6... | collective-permute-start | bytes 49160 | tf_op jit(solution)/shard_map/ppermute | solution.py:26
  154.6 12.7 %collective-permute-start.5 = (f32[1,8,512]{2,1,0:T(8,128)}, f32[1,8,512]{2,1,0:T(8,128)}, u32[]{:S(2)}, u32[]{:S(2)}) collective-permute-start(f32[1,8,512]{2,1,0:T(8,128)} %get-tuple-element.44), channel_id=1, source_target_pairs={{0,8},{8,16},{16,24},{24,32},{32,40},{40,48},{48,56},{56,64},{64,7... | collective-permute-start | bytes 49160 | tf_op jit(solution)/shard_map/ppermute | solution.py:25
  156.2 13.5 %collective-permute-start.6 = (f32[1,8,512]{2,1,0:T(8,128)}, f32[1,8,512]{2,1,0:T(8,128)}, u32[]{:S(2)}, u32[]{:S(2)}) collective-permute-start(f32[1,8,512]{2,1,0:T(8,128)} %get-tuple-element.45), channel_id=1, source_target_pairs={{8,0},{16,8},{24,16},{32,24},{40,32},{48,40},{56,48},{64,56},{72,6... | collective-permute-start | bytes 49160 | tf_op jit(solution)/shard_map/ppermute | solution.py:26
  161.6 22.9 %collective-permute-start.15 = (f32[18,1,256]{2,1,0:T(1,128)}, f32[18,1,256]{2,1,0:T(1,128)S(1)}, u32[]{:S(2)}, u32[]{:S(2)}) collective-permute-start(f32[18,1,256]{2,1,0:T(1,128)} %get-tuple-element.57), channel_id=1, source_target_pairs={{0,1},{1,2},{2,3},{3,4},{4,5},{5,6},{6,7},{7,0},{8,9},{9,10},{10,1... | collective-permute-start | bytes 55304 | tf_op jit(solution)/shard_map/ppermute | solution.py:25
  167.2 17.7 %collective-permute-start.16 = (f32[18,1,256]{2,1,0:T(1,128)}, f32[18,1,256]{2,1,0:T(1,128)}, u32[]{:S(2)}, u32[]{:S(2)}) collective-permute-start(f32[18,1,256]{2,1,0:T(1,128)} %get-tuple-element.56), channel_id=1, source_target_pairs={{1,0},{2,1},{3,2},{4,3},{5,4},{6,5},{7,6},{0,7},{9,8},{10,9},{11,1... | collective-permute-start | bytes 55304 | tf_op jit(solution)/shard_map/ppermute | solution.py:26
  169.7 162.3 %collective-permute-start.19 = (f32[18,1,256]{2,1,0:T(1,128)}, f32[18,1,256]{2,1,0:T(1,128)}, u32[]{:S(2)}, u32[]{:S(2)}) collective-permute-start(f32[18,1,256]{2,1,0:T(1,128)} %get-tuple-element.58), channel_id=1, source_target_pairs={{0,1},{1,2},{2,3},{3,4},{4,5},{5,6},{6,7},{7,0},{8,9},{9,10},{10,1... | collective-permute-start | bytes 55304 | tf_op jit(solution)/shard_map/ppermute | solution.py:25
  184.5 12.0 %collective-permute-start.3 = (f32[34,1,512]{0,1,2:T(1,128)}, f32[34,1,512]{0,1,2:T(1,128)S(1)}, u32[]{:S(2)}, u32[]{:S(2)}) collective-permute-start(f32[34,1,512]{0,1,2:T(1,128)} %get-tuple-element.35), channel_id=1, source_target_pairs={{0,1},{1,2},{2,3},{3,4},{4,5},{5,6},{6,7},{7,0},{8,9},{9,10},{10,1... | collective-permute-start | bytes 208904 | tf_op jit(solution)/shard_map/ppermute | solution.py:25
  185.0 13.9 %collective-permute-start.4 = (f32[34,1,512]{0,1,2:T(1,128)}, f32[34,1,512]{0,1,2:T(1,128)S(1)}, u32[]{:S(2)}, u32[]{:S(2)}) collective-permute-start(f32[34,1,512]{0,1,2:T(1,128)} %get-tuple-element.34), channel_id=1, source_target_pairs={{1,0},{2,1},{3,2},{4,3},{5,4},{6,5},{7,6},{0,7},{9,8},{10,9},{11,1... | collective-permute-start | bytes 208904 | tf_op jit(solution)/shard_map/ppermute | solution.py:26
  196.5 16.9 %collective-permute-start.7 = (f32[34,1,512]{0,1,2:T(1,128)}, f32[34,1,512]{0,1,2:T(1,128)S(1)}, u32[]{:S(2)}, u32[]{:S(2)}) collective-permute-start(f32[34,1,512]{0,1,2:T(1,128)} %get-tuple-element.38), channel_id=1, source_target_pairs={{0,1},{1,2},{2,3},{3,4},{4,5},{5,6},{6,7},{7,0},{8,9},{9,10},{10,1... | collective-permute-start | bytes 208904 | tf_op jit(solution)/shard_map/ppermute | solution.py:25
  198.8 14.5 %collective-permute-start.8 = (f32[34,1,512]{0,1,2:T(1,128)}, f32[34,1,512]{0,1,2:T(1,128)S(1)}, u32[]{:S(2)}, u32[]{:S(2)}) collective-permute-start(f32[34,1,512]{0,1,2:T(1,128)} %get-tuple-element.39), channel_id=1, source_target_pairs={{1,0},{2,1},{3,2},{4,3},{5,4},{6,5},{7,6},{0,7},{9,8},{10,9},{11,1... | collective-permute-start | bytes 208904 | tf_op jit(solution)/shard_map/ppermute | solution.py:26
  233.1 9.5 %collective-permute-start.9 = (f32[1,8,512]{2,1,0:T(8,128)S(1)}, f32[1,8,512]{2,1,0:T(8,128)S(1)}, u32[]{:S(2)}, u32[]{:S(2)}) collective-permute-start(f32[1,8,512]{2,1,0:T(8,128)S(1)} %copy.285), channel_id=1, source_target_pairs={{0,8},{8,16},{16,24},{24,32},{32,40},{40,48},{48,56},{56,64},{64,7... | collective-permute-start | bytes 49160 | tf_op jit(solution)/shard_map/ppermute | solution.py:25
  252.4 9.5 %collective-permute-start.12 = (f32[34,1,512]{0,1,2:T(1,128)S(1)}, f32[34,1,512]{0,1,2:T(1,128)S(1)}, u32[]{:S(2)}, u32[]{:S(2)}) collective-permute-start(f32[34,1,512]{0,1,2:T(1,128)S(1)} %get-tuple-element.19), channel_id=1, source_target_pairs={{1,0},{2,1},{3,2},{4,3},{5,4},{6,5},{7,6},{0,7},{9,8},{10,9},{11,1... | collective-permute-start | bytes 208904 | tf_op jit(solution)/shard_map/ppermute | solution.py:26
  261.0 71.0 %collective-permute-start.20 = (f32[18,1,256]{2,1,0:T(1,128)S(1)}, f32[18,1,256]{2,1,0:T(1,128)S(1)}, u32[]{:S(2)}, u32[]{:S(2)}) collective-permute-start(f32[18,1,256]{2,1,0:T(1,128)S(1)} %copy-done.24), channel_id=1, source_target_pairs={{1,0},{2,1},{3,2},{4,3},{5,4},{6,5},{7,6},{0,7},{9,8},{10,9},{11,1... | collective-permute-start | bytes 55304 | tf_op jit(solution)/shard_map/ppermute | solution.py:26
  723.1 9.5 %collective-permute-start.110 = (f32[34,1,512]{0,1,2:T(1,128)S(1)}, f32[34,1,512]{0,1,2:T(1,128)S(1)}, u32[]{:S(2)}, u32[]{:S(2)}) collective-permute-start(f32[34,1,512]{0,1,2:T(1,128)S(1)} %get-tuple-element.15), channel_id=1, source_target_pairs={{1,0},{2,1},{3,2},{4,3},{5,4},{6,5},{7,6},{0,7},{9,8},{10,9},{11,1... | collective-permute-start | bytes 208904 | tf_op jit(solution)/shard_map/ppermute | solution.py:26
  (135 other events, 1196.6 us)
where the time goes:
time: 768 us; the launch traced here: 756 us
  starting transfers between devices  284 us (37%)
  local copies, waits for them, and re-layouts  173 us (23%)
  other arithmetic  165 us (21%)
  waiting for transfers between devices  73.4 us (10%)
  blocking collectives  56.6 us (7%)
    ppermute x55, starting transfers between devices, padded_2(): after = lax.ppermute(initial, axis, down)  272 us
    reshape x5, local copies, waits for them, and re-layouts, coarsen(): array_in.reshape(az_n // 2, 2, ht_n // 2, 2, rad_n // 2, 2)  86.3 us
    ppermute x55, waiting for transfers between devices, padded_2(): before = lax.ppermute(last, axis, up)  64.7 us
    all_gather x2, blocking collectives, consolidate(): gathered = lax.all_gather(array_in, 'gz', axis=1, tiled=True)  56.6 us
    add x35, other arithmetic, jacobi_sweep(): center + OMEGA * (source_part - apply_ext(padded, weights)) / weights[6]  42.1 us
    reduce_sum x6, other arithmetic, coarsen(): array_in.reshape(az_n // 2, 2, ht_n // 2, 2, rad_n // 2, 2)  34.7 us
    sub x3, other arithmetic, residual(): return source_term - applied  20.2 us
    div x1, other arithmetic, body(): scaled_residual = final_rest / dist_weights[0][6]  19.7 us
  transfers between devices with their start and end apart: 111, of which 82 were waited for; matrix products, arithmetic and copies ran while one was open for 31% of the time, Pallas kernels for 0%

commit v1 on v0

v1 whole, which is shorter than its diff:
```python
import functools
import math

import jax
import jax.numpy as jnp
from jax import lax
from jax.experimental import pallas as pl
from jax.experimental.pallas import tpu as pltpu
from jax.sharding import PartitionSpec as P

SIGMA = 0.02
OMEGA = 0.8
COARSE_SWEEPS = 32
F32 = jnp.float32

NA, NH, NR = 32, 8, 512
A1, H1, R1 = 16, 4, 256
A2, H2, R2 = 8, 2, 128
AZ2, G2 = 128, 8
AZ3 = 64
N_AZ, N_GZ = 16, 8
SLOTS = 128


def struct(*shape):
    return jax.ShapeDtypeStruct(shape, F32)


def call(kernel, outs, ins, scratch=(), smem=(), limit=48):
    specs = [
        pl.BlockSpec(memory_space=pltpu.SMEM if i in smem else pltpu.VMEM) for i in range(len(ins))
    ]
    return pl.pallas_call(
        kernel,
        out_shape=outs,
        in_specs=specs,
        out_specs=[pl.BlockSpec(memory_space=pltpu.VMEM) for _ in outs],
        scratch_shapes=list(scratch),
        compiler_params=pltpu.CompilerParams(vmem_limit_bytes=limit * 1024 * 1024),
    )(*ins)


def iota(shape, dim):
    return lax.broadcasted_iota(jnp.int32, shape, dim)


def dot(a, b):
    return jnp.dot(a, b, precision=lax.Precision.HIGHEST, preferred_element_type=F32)


def radial_consts(shape, size, step, rad):
    i = rad.astype(F32)
    metric = ((i + 0.5) * step) ** 2
    ca = 0.5 / metric
    ri = jnp.where(rad > 0, 0.5 * i / (i + 0.5), 0.0)
    ro = jnp.where(rad < size - 1, 0.5 * (i + 1.0) / (i + 0.5), 0.0)
    return ca, ri, ro


def pair_cols(n):
    return (iota((n, n // 2), 0) // 2 == iota((n, n // 2), 1)).astype(F32)


def dup_cols(n):
    return (iota((n, 2 * n), 0) == iota((n, 2 * n), 1) // 2).astype(F32)


def pair_rows_h(rows):
    return (iota((rows // 2, rows), 1) // 2 == iota((rows // 2, rows), 0)).astype(F32)


def block_rows(az, ht):
    out = (az // 2) * (ht // 2)
    r = iota((out, az * ht), 1)
    o = iota((out, az * ht), 0)
    target = (r // (2 * ht)) * (ht // 2) + (r % ht) // 2
    return (target == o).astype(F32)


def position():
    return lax.axis_index("az"), lax.axis_index("gz")


def pick(par, even, odd):
    return jnp.where(par == 0, even, odd)


class Halo:
    def __init__(self, x_ref, c_ref, z_ref, y_ref):
        a, g = position()
        self.pa, self.pg = a % 2, g % 2
        self.x, self.c, self.z, self.y = x_ref, c_ref, z_ref, y_ref

    def prev(self, rows, lanes):
        return pick(self.pa, self.x[rows, lanes], self.c[rows, lanes])

    def next(self, rows, lanes):
        return pick(self.pa, self.c[rows, lanes], self.x[rows, lanes])

    def below(self, rows, lanes):
        return pick(self.pg, self.y[rows, lanes], self.z[rows, lanes])

    def above(self, rows, lanes):
        return pick(self.pg, self.z[rows, lanes], self.y[rows, lanes])


def fine_walk(m_of, v_of, mb, ma, vb, va, emit):
    a, g = position()
    sub = iota((NH, NR), 0)
    lane = iota((NH, NR), 1)
    ca, ri, ro = radial_consts((NH, NR), NR, 2.0 * math.pi / (NA * N_AZ), lane)
    zlo = jnp.where((sub == 0) & (g == 0), 0.0, 0.5)
    zhi = jnp.where((sub == NH - 1) & (g == N_GZ - 1), 0.0, 0.5)
    first, final = sub == 0, sub == NH - 1
    mp, mc = m_of(-1), m_of(0)
    vp, vc = v_of(-1), v_of(0)
    wa = ca * (mp + mc)
    for i in range(NA):
        mn, vn = m_of(i + 1), v_of(i + 1)
        wan = ca * (mc + mn)
        m_lo = jnp.where(first, mb(i), pltpu.roll(mc, 1, 0))
        m_hi = jnp.where(final, ma(i), pltpu.roll(mc, NH - 1, 0))
        v_lo = jnp.where(first, vb(i), pltpu.roll(vc, 1, 0))
        v_hi = jnp.where(final, va(i), pltpu.roll(vc, NH - 1, 0))
        wl, wh = zlo * (mc + m_lo), zhi * (mc + m_hi)
        wi = ri * (mc + pltpu.roll(mc, 1, 1))
        wo = ro * (mc + pltpu.roll(mc, NR - 1, 1))
        diagonal = (wa + wan) + (wl + wh) + (wi + wo) + SIGMA
        around = (wa * vp + wan * vn) + (wl * v_lo + wh * v_hi)
        around = around + (wi * pltpu.roll(vc, 1, 1) + wo * pltpu.roll(vc, NR - 1, 1))
        emit(i, diagonal, around, vc)
        mp, mc, vp, vc, wa = mc, mn, vc, vn, wan


def level1_weights(m, prev, nxt, below, above, buf):
    a, g = position()
    rows = A1 * H1
    sub = iota((rows, R1), 0)
    lane = iota((rows, R1), 1)
    ht = sub % H1
    ca, ri, ro = radial_consts((rows, R1), R1, 2.0 * math.pi / (A1 * N_AZ), lane)
    zlo = jnp.where((ht == 0) & (g == 0), 0.0, 0.5)
    zhi = jnp.where((ht == H1 - 1) & (g == N_GZ - 1), 0.0, 0.5)
    mp, mn, ml, mh, mi, mo = level1_around(m, prev, nxt, below, above, buf)
    w = (ca * (m + mp), ca * (m + mn), zlo * (m + ml), zhi * (m + mh), ri * (m + mi), ro * (m + mo))
    diagonal = (w[0] + w[1]) + (w[2] + w[3]) + (w[4] + w[5]) + SIGMA * 4.0
    return w, diagonal


def level1_around(x, prev, nxt, below, above, buf):
    rows = A1 * H1
    ht = iota((rows, R1), 0) % H1
    spread = (iota((rows, A1), 0) // H1 == iota((rows, A1), 1)).astype(F32)
    buf[8 : 8 + rows, :] = x
    buf[8 - H1 : 8, :] = prev
    buf[8 + rows : 8 + rows + H1, :] = nxt
    xp = buf[8 - H1 : 8 - H1 + rows, :]
    xn = buf[8 + H1 : 8 + H1 + rows, :]
    xl = jnp.where(ht == 0, dot(spread, below), pltpu.roll(x, 1, 0))
    xh = jnp.where(ht == H1 - 1, dot(spread, above), pltpu.roll(x, rows - 1, 0))
    return xp, xn, xl, xh, pltpu.roll(x, 1, 1), pltpu.roll(x, R1 - 1, 1)


def weighted(w, n):
    return (w[0] * n[0] + w[1] * n[1]) + (w[2] * n[2] + w[3] * n[3]) + (w[4] * n[4] + w[5] * n[5])


ALL = slice(None)


def store_faces(ref, x_ref, c_ref, z_ref, y_ref, planes_at=0, rows_at=0):
    a, g = position()
    pa, pg = a % 2, g % 2
    c_plane = jnp.where(pa == 0, NA - 1, 0)
    x_plane = NA - 1 - c_plane
    c_ref[planes_at : planes_at + NH, :] = ref[c_plane]
    x_ref[planes_at : planes_at + NH, :] = ref[x_plane]
    z_row = jnp.where(pg == 0, NH - 1, 0)
    y_row = NH - 1 - z_row
    for i in range(NA):
        z_ref[rows_at + i : rows_at + i + 1, :] = ref[i, pl.ds(z_row, 1), :]
        y_ref[rows_at + i : rows_at + i + 1, :] = ref[i, pl.ds(y_row, 1), :]


def store_faces1(ref, x_ref, c_ref, z_ref, y_ref, planes_at=0, rows_at=0):
    a, g = position()
    pa, pg = a % 2, g % 2
    rows = A1 * H1
    lo, hi = ref[0:H1, :], ref[rows - H1 : rows, :]
    c_ref[planes_at : planes_at + H1, 0:R1] = pick(pa, hi, lo)
    x_ref[planes_at : planes_at + H1, 0:R1] = pick(pa, lo, hi)
    for i in range(A1):
        low, high = ref[H1 * i : H1 * i + 1, :], ref[H1 * i + H1 - 1 : H1 * i + H1, :]
        z_ref[rows_at + i : rows_at + i + 1, 0:R1] = pick(pg, high, low)
        y_ref[rows_at + i : rows_at + i + 1, 0:R1] = pick(pg, low, high)


def prepare(p_ref, void_ref, vol_ref, cnt_ref, m0_ref, m1_ref, m2_ref, sx, sc, sz, sy, pairs):
    for i in range(0, NA, 2):
        u = 1.0 / (1.0 - void_ref[i])
        v = 1.0 / (1.0 - void_ref[i + 1])
        m0_ref[i] = u
        m0_ref[i + 1] = v
        pairs[(i // 2) * NH : (i // 2 + 1) * NH, :] = u + v
    m1 = 0.125 * dot(pair_rows_h(A1 * NH), dot(pairs[...], pair_cols(NR)))
    m1_ref[...] = m1
    m2_ref[...] = 0.125 * dot(block_rows(A1, H1), dot(m1, pair_cols(R1)))
    store_faces(p_ref, sx, sc, sz, sy, 0, 0)
    store_faces(m0_ref, sx, sc, sz, sy, NH, NA)
    zero = jnp.zeros((NH, NR), F32)
    sx[2 * NH : 3 * NH, :] = zero
    sc[2 * NH : 3 * NH, :] = zero
    for ref in (sz, sy):
        ref[2 * NA : 2 * NA + A1, R1:NR] = jnp.zeros((A1, NR - R1), F32)
    store_faces1(m1_ref, sx, sc, sz, sy, 2 * NH, 2 * NA)
    live = jnp.where(iota((1, SLOTS), 1) < cnt_ref[0], vol_ref[...], 0.0)
    sx[2 * NH + H1 : 2 * NH + H1 + 1, 0:SLOTS] = live
    sc[2 * NH + H1 : 2 * NH + H1 + 1, 0:SLOTS] = live


def fine_mobility(m_ref, ah):
    def m_of(i):
        if i < 0:
            return ah.prev(slice(NH, 2 * NH), ALL)
        if i >= NA:
            return ah.next(slice(NH, 2 * NH), ALL)
        return m_ref[i]

    return (
        m_of,
        lambda i: ah.below(slice(NA + i, NA + i + 1), ALL),
        lambda i: ah.above(slice(NA + i, NA + i + 1), ALL),
    )


def fine_values(v_ref, vh):
    def v_of(i):
        if i < 0:
            return vh.prev(slice(0, NH), ALL)
        if i >= NA:
            return vh.next(slice(0, NH), ALL)
        return v_ref[i]

    return (
        v_of,
        lambda i: vh.below(slice(i, i + 1), ALL),
        lambda i: vh.above(slice(i, i + 1), ALL),
    )


def presmooth(p_ref, div_ref, m_ref, cell_ref, ax, ac, az, ay, rhs_ref, v_ref, sx, sc, sz, sy):
    ah = Halo(ax, ac, az, ay)
    arrived = ah.prev(slice(2 * NH + H1, 2 * NH + H1 + 1), slice(0, SLOTS))
    cell = cell_ref[...]
    plane_hot = (iota((NA * NH, SLOTS), 0) == lax.shift_right_logical(cell, 9)).astype(F32)
    radius_hot = jnp.where(iota((NR, SLOTS), 0) == (cell & (NR - 1)), arrived, 0.0)
    deposit = lax.dot_general(
        plane_hot,
        radius_hot,
        (((1,), (1,)), ((), ())),
        precision=lax.Precision.HIGHEST,
        preferred_element_type=F32,
    )
    rhs_ref[...] = div_ref[...] + deposit.reshape(NA, NH, NR)
    m_of, mb, ma = fine_mobility(m_ref, ah)
    v_of, vb, va = fine_values(p_ref, ah)

    def emit(i, diagonal, around, centre):
        v_ref[i] = centre + OMEGA * (rhs_ref[i] - diagonal * centre + around) / diagonal

    fine_walk(m_of, v_of, mb, ma, vb, va, emit)
    store_faces(v_ref, sx, sc, sz, sy)


def mobility1(m1_ref, ah):
    return (
        m1_ref[...],
        ah.prev(slice(2 * NH, 2 * NH + H1), slice(0, R1)),
        ah.next(slice(2 * NH, 2 * NH + H1), slice(0, R1)),
        ah.below(slice(2 * NA, 2 * NA + A1), slice(0, R1)),
        ah.above(slice(2 * NA, 2 * NA + A1), slice(0, R1)),
    )


def restrict(
    rhs_ref, v_ref, m_ref, m1_ref, ax, ac, az, ay, bx, bc, bz, by, b1_ref, v1_ref, sx, sc, sz, sy, pairs, buf
):
    ah, bh = Halo(ax, ac, az, ay), Halo(bx, bc, bz, by)
    m_of, mb, ma = fine_mobility(m_ref, ah)
    v_of, vb, va = fine_values(v_ref, bh)
    kept = []

    def emit(i, diagonal, around, centre):
        r = rhs_ref[i] - diagonal * centre + around
        if i % 2 == 0:
            kept.append(r)
        else:
            pairs[(i // 2) * NH : (i // 2 + 1) * NH, :] = kept.pop() + r

    fine_walk(m_of, v_of, mb, ma, vb, va, emit)
    b1 = 0.5 * dot(pair_rows_h(A1 * NH), dot(pairs[...], pair_cols(NR)))
    b1_ref[...] = b1
    _, diagonal = level1_weights(*mobility1(m1_ref, ah), buf)
    v1_ref[...] = OMEGA * b1 / diagonal
    store_faces1(v1_ref, sx, sc, sz, sy)


def halo1(h):
    return (
        h.prev(slice(0, H1), ALL),
        h.next(slice(0, H1), ALL),
        h.below(slice(0, A1), ALL),
        h.above(slice(0, A1), ALL),
    )


def restrict1(b1_ref, v1_ref, m1_ref, m2_ref, ax, ac, az, ay, cx, cc, cz, cy, out_ref, buf):
    ah, ch = Halo(ax, ac, az, ay), Halo(cx, cc, cz, cy)
    w, diagonal = level1_weights(*mobility1(m1_ref, ah), buf)
    v1 = v1_ref[...]
    n = level1_around(v1, *halo1(ch), buf)
    r1 = b1_ref[...] - diagonal * v1 + weighted(w, n)
    b2 = 0.5 * dot(block_rows(A1, H1), dot(r1, pair_cols(R1)))
    m2 = m2_ref[...]
    rows = A2 * H2
    for k in range(out_ref.shape[0]):
        out_ref[k, 0:rows, :] = b2
        out_ref[k, rows : 2 * rows, :] = m2


def level2_plane(ca, ri, ro, zlo, zhi, mp, mc, mn):
    mid = 0.5 * (mc[0] + mc[1])
    lows = (zlo * (mc[0] + pltpu.roll(mc[1], 1, 0)), mid)
    highs = (mid, zhi * (mc[1] + pltpu.roll(mc[0], G2 - 1, 0)))
    out = []
    for p in range(2):
        m = mc[p]
        w = (
            ca * (m + mp[p]),
            ca * (m + mn[p]),
            lows[p],
            highs[p],
            ri * (m + pltpu.roll(m, 1, 1)),
            ro * (m + pltpu.roll(m, R2 - 1, 1)),
        )
        out.append((w, (w[0] + w[1]) + (w[2] + w[3]) + (w[4] + w[5]) + SIGMA * 16.0))
    return out


def level2_around(vp, vc, vn):
    lows = (pltpu.roll(vc[1], 1, 0), vc[0])
    highs = (vc[1], pltpu.roll(vc[0], G2 - 1, 0))
    return [
        (vp[p], vn[p], lows[p], highs[p], pltpu.roll(vc[p], 1, 1), pltpu.roll(vc[p], R2 - 1, 1))
        for p in range(2)
    ]


def coarse(
    own, oth, b1_ref, v1_ref, m1_ref, ax, ac, az, ay, cx, cc, cz, cy,
    v1_out, sx, sc, sz, sy,
    m2, b2, v2, sum_m, sum_r, m3, w3, va, vb, e2, v2f, src, buf,
):
    a, g = position()
    pa = a % 2
    rows = A2 * H2

    for k in range(N_AZ):
        base = (k // 2) * N_GZ * 2 * rows
        for i in range(A2):
            total = None
            for p in range(2):
                at_b = pl.ds(base + i * 2 + p, G2, stride=2 * rows)
                at_m = pl.ds(base + rows + i * 2 + p, G2, stride=2 * rows)
                first, second = (own, oth) if k % 2 == 0 else (oth, own)
                b2[k * A2 + i + 2, p] = pick(pa, first[at_b, :], second[at_b, :])
                m2[k * A2 + i + 2, p] = pick(pa, first[at_m, :], second[at_m, :])
    for ref in (m2, b2):
        ref[0:2] = ref[AZ2 : AZ2 + 2]
        ref[AZ2 + 2 : AZ2 + 4] = ref[2:4]

    sub = iota((G2, R2), 0)
    lane = iota((G2, R2), 1)
    ca, ri, ro = radial_consts((G2, R2), R2, 2.0 * math.pi / AZ2, lane)
    zlo = jnp.where(sub == 0, 0.0, 0.5)
    zhi = jnp.where(sub == G2 - 1, 0.0, 0.5)
    plane = functools.partial(level2_plane, ca, ri, ro, zlo, zhi)

    def both(ref, s):
        return (ref[s, 0], ref[s, 1])

    def first_sweep(j, carry):
        s = 2 * j + 2
        planes = [both(m2, s + d) for d in (-1, 0, 1, 2)]
        for d in range(2):
            for p, (_, diagonal) in enumerate(plane(*planes[d : d + 3])):
                v2[s + d, p] = OMEGA * b2[s + d, p] / diagonal
        sum_m[j] = (planes[1][0] + planes[1][1]) + (planes[2][0] + planes[2][1])
        return carry

    lax.fori_loop(0, AZ3, first_sweep, 0)
    v2[0:2] = v2[AZ2 : AZ2 + 2]
    v2[AZ2 + 2 : AZ2 + 4] = v2[2:4]

    def residuals(j, carry):
        s = 2 * j + 2
        planes = [both(m2, s + d) for d in (-1, 0, 1, 2)]
        values = [both(v2, s + d) for d in (-1, 0, 1, 2)]
        total = None
        for d in range(2):
            around = level2_around(*values[d : d + 3])
            for p, (w, diagonal) in enumerate(plane(*planes[d : d + 3])):
                r = b2[s + d, p] - diagonal * values[d + 1][p] + weighted(w, around[p])
                total = r if total is None else total + r
        sum_r[j] = total
        return carry

    lax.fori_loop(0, AZ3, residuals, 0)

    half = AZ3 // 2
    row_i, col_i = iota((R2, R2), 0), iota((R2, R2), 1)
    left = (row_i // 2 == col_i).astype(F32)
    right = (row_i // 2 + R2 // 2 == col_i).astype(F32)

    def packed(ref):
        lower = ref[0:half].reshape(half * G2, R2)
        upper = ref[half:AZ3].reshape(half * G2, R2)
        return (dot(lower, left) + dot(upper, right)).reshape(half, G2, R2)

    def wrap(ref):
        ref[0] = pltpu.roll(ref[half], R2 // 2, 1)
        ref[half + 1] = pltpu.roll(ref[1], R2 // 2, 1)

    m3[1 : half + 1] = 0.125 * packed(sum_m)
    wrap(m3)
    b3 = 0.5 * packed(sum_r)
    va[1 : half + 1] = b3
    ca, ri, ro = radial_consts((G2, R2), R2 // 2, 2.0 * math.pi / AZ3, lane % (R2 // 2))
    mp, mc = m3[0], m3[1]
    for i in range(half):
        mn = m3[i + 2]
        w = (
            ca * (mc + mp),
            ca * (mc + mn),
            zlo * (mc + pltpu.roll(mc, 1, 0)),
            zhi * (mc + pltpu.roll(mc, G2 - 1, 0)),
            ri * (mc + pltpu.roll(mc, 1, 1)),
            ro * (mc + pltpu.roll(mc, R2 - 1, 1)),
        )
        diagonal = (w[0] + w[1]) + (w[2] + w[3]) + (w[4] + w[5]) + SIGMA * 64.0
        scale = OMEGA / diagonal
        for f in range(6):
            w3[f, i] = w[f] * scale
        start = va[i + 1] * scale
        w3[6, i] = start
        va[i + 1] = start
        mp, mc = mc, mn
    wrap(va)

    def sweep(src_ref, dst_ref):
        vp, vc = src_ref[0], src_ref[1]
        for i in range(half):
            vn = src_ref[i + 2]
            n = (
                vp,
                vn,
                pltpu.roll(vc, 1, 0),
                pltpu.roll(vc, G2 - 1, 0),
                pltpu.roll(vc, 1, 1),
                pltpu.roll(vc, R2 - 1, 1),
            )
            w = [w3[f, i] for f in range(6)]
            dst_ref[i + 1] = ((1.0 - OMEGA) * vc + w3[6, i]) + weighted(w, n)
            vp, vc = vc, vn
        wrap(dst_ref)

    def two(k, carry):
        sweep(va, vb)
        sweep(vb, va)
        return carry

    lax.fori_loop(0, (COARSE_SWEEPS - 2) // 2, two, 0)
    sweep(va, vb)

    solved = vb[1 : half + 1].reshape(half * G2, R2)
    e2[0:half] = dot(solved, (row_i == col_i // 2).astype(F32)).reshape(half, G2, R2)
    e2[half:AZ3] = dot(solved, (row_i == col_i // 2 + R2 // 2).astype(F32)).reshape(half, G2, R2)

    at = a * A2
    ca, ri, ro = radial_consts((G2, R2), R2, 2.0 * math.pi / AZ2, lane)
    plane = functools.partial(level2_plane, ca, ri, ro, zlo, zhi)
    values = []
    for k in range(A2 + 4):
        e = e2[(a * (A2 // 2) - 1 + k // 2 + AZ3) % AZ3]
        values.append((v2[at + k, 0] + e, v2[at + k, 1] + e))
    for k in range(1, A2 + 3):
        around = level2_around(*values[k - 1 : k + 2])
        for p, (w, diagonal) in enumerate(plane(both(m2, at + k - 1), both(m2, at + k), both(m2, at + k + 1))):
            v = values[k][p]
            r = b2[at + k, p] - diagonal * v + weighted(w, around[p])
            v2f[k - 1, p] = v + OMEGA * r / diagonal

    low, high = jnp.maximum(g - 1, 0), jnp.minimum(g + 1, N_GZ - 1)
    for j in range(A2):
        src[2 * j : 2 * j + 1, :] = v2f[j + 1, 0, pl.ds(g, 1), :]
        src[2 * j + 1 : 2 * j + 2, :] = v2f[j + 1, 1, pl.ds(g, 1), :]
        src[16 + j : 17 + j, :] = v2f[j + 1, 1, pl.ds(low, 1), :]
        src[24 + j : 25 + j, :] = v2f[j + 1, 0, pl.ds(high, 1), :]
    for p in range(2):
        src[32 + p : 33 + p, :] = v2f[0, p, pl.ds(g, 1), :]
        src[34 + p : 35 + p, :] = v2f[A2 + 1, p, pl.ds(g, 1), :]
    src[36:40, :] = jnp.zeros((4, R2), F32)
    o, c = iota((112, 40), 0), iota((112, 40), 1)
    target = jnp.where(
        o < 64,
        (o // 8) * 2 + (o % 4) // 2,
        jnp.where(
            o < 96,
            16 + (o - 64) // 2,
            jnp.where(o < 100, 32 + (o - 96) // 2, 34 + (o - 104) // 2),
        ),
    )
    e1 = dot((target == c).astype(F32), dot(src[...], dup_cols(R2)))

    ah, ch = Halo(ax, ac, az, ay), Halo(cx, cc, cz, cy)
    w, diagonal = level1_weights(*mobility1(m1_ref, ah), buf)
    prev, nxt, below, above = halo1(ch)
    v1 = v1_ref[...] + e1[0:64]
    n = level1_around(
        v1, prev + e1[96:100], nxt + e1[104:108], below + e1[64:80], above + e1[80:96], buf
    )
    v1_out[...] = v1 + OMEGA * (b1_ref[...] - diagonal * v1 + weighted(w, n)) / diagonal
    store_faces1(v1_out, sx, sc, sz, sy)


def postsmooth(
    rhs_ref, v_ref, m_ref, v1_ref, ax, ac, az, ay, bx, bc, bz, by, fx, fc, fz, fy, out_ref, sx, sc, sz, sy, e_ref, er
):
    ah, bh, fh = Halo(ax, ac, az, ay), Halo(bx, bc, bz, by), Halo(fx, fc, fz, fy)
    dup = dup_cols(R1)
    rows = A1 * NH
    tall = (iota((rows, A1 * H1), 0) // 2 == iota((rows, A1 * H1), 1)).astype(F32)
    e_ref[...] = dot(tall, dot(v1_ref[...], dup)).reshape(A1, NH, NR)
    prev, nxt, below, above = halo1(fh)
    er[0:A1, :] = dot(below, dup)
    er[A1 : 2 * A1, :] = dot(above, dup)
    tall = (iota((NH, H1), 0) // 2 == iota((NH, H1), 1)).astype(F32)
    er[2 * A1 : 2 * A1 + NH, :] = dot(tall, dot(prev, dup))
    er[2 * A1 + NH : 2 * A1 + 2 * NH, :] = dot(tall, dot(nxt, dup))
    m_of, mb, ma = fine_mobility(m_ref, ah)
    old, ob, oa = fine_values(v_ref, bh)

    def v_of(i):
        if i < 0:
            return old(i) + er[2 * A1 : 2 * A1 + NH, :]
        if i >= NA:
            return old(i) + er[2 * A1 + NH : 2 * A1 + 2 * NH, :]
        return old(i) + e_ref[i // 2]

    def emit(i, diagonal, around, centre):
        out_ref[i] = centre + OMEGA * (rhs_ref[i] - diagonal * centre + around) / diagonal

    fine_walk(
        m_of,
        v_of,
        mb,
        ma,
        lambda i: ob(i) + er[i // 2 : i // 2 + 1, :],
        lambda i: oa(i) + er[A1 + i // 2 : A1 + i // 2 + 1, :],
        emit,
    )
    store_faces(out_ref, sx, sc, sz, sy)


def final(rhs_ref, v_ref, m_ref, ax, ac, az, ay, gx, gc, gz, gy, out_ref):
    ah, gh = Halo(ax, ac, az, ay), Halo(gx, gc, gz, gy)
    m_of, mb, ma = fine_mobility(m_ref, ah)
    v_of, vb, va = fine_values(v_ref, gh)

    def emit(i, diagonal, around, centre):
        out_ref[i] = (rhs_ref[i] - diagonal * centre + around) / diagonal

    fine_walk(m_of, v_of, mb, ma, vb, va, emit)


def swap(x, axis, odd):
    n = lax.axis_size(axis)
    pairs = []
    for i in range(n):
        partner = i ^ 1 if odd == 0 else ((i + 1) % n if i % 2 else (i - 1) % n)
        pairs.append((i, partner))
    return lax.ppermute(x, axis, pairs)


def exchange(sx, sc, sz, sy):
    return swap(sx, "az", 1), swap(sc, "az", 0), swap(sz, "gz", 0), swap(sy, "gz", 1)


def gathered(x):
    groups = [[a * N_GZ + g for a in range(c, N_AZ, 2) for g in range(N_GZ)] for c in range(2)]
    own = lax.all_to_all(x, ("az", "gz"), 0, 0, tiled=True, axis_index_groups=groups)
    own = own.reshape(own.shape[0] * own.shape[1], own.shape[2])
    return own, swap(own, "az", 0)


def faces(planes, rows, width):
    return [struct(planes, width)] * 2 + [struct(rows, width)] * 2


def vmem(*shape):
    return pltpu.VMEM(shape, F32)


def body(pressure, divergence, void_fraction, bubble_volume, bubble_count, bubble_cell):
    block = struct(NA, NH, NR)
    flat1 = struct(A1 * H1, R1)
    cell = bubble_cell.reshape(1, SLOTS)
    volume = bubble_volume.reshape(1, SLOTS)
    pairs = vmem(A1 * NH, NR)
    buf = vmem(A1 * H1 + 16, R1)

    m0, m1, m2, *send = call(
        prepare,
        [block, flat1, struct(A2 * H2, R2)] + faces(3 * NH, 2 * NA + A1, NR),
        (pressure, void_fraction, volume, bubble_count),
        [pairs],
        smem=(3,),
    )
    ha = exchange(*send)
    rhs, v0, *send = call(
        presmooth, [block, block] + faces(NH, NA, NR), (pressure, divergence, m0, cell, *ha)
    )
    hb = exchange(*send)
    b1, v1, *send = call(
        restrict, [flat1, flat1] + faces(H1, A1, R1), (rhs, v0, m0, m1, *ha, *hb), [pairs, buf]
    )
    hc = exchange(*send)
    (copies,) = call(
        restrict1, [struct(64, 2 * A2 * H2, R2)], (b1, v1, m1, m2, *ha, *hc), [buf]
    )
    own, oth = gathered(copies)
    ring = vmem(AZ2 + 4, 2, G2, R2)
    half = AZ3 // 2
    v1, *send = call(
        coarse,
        [flat1] + faces(H1, A1, R1),
        (own, oth, b1, v1, m1, *ha, *hc),
        [
            ring,
            ring,
            ring,
            vmem(AZ3, G2, R2),
            vmem(AZ3, G2, R2),
            vmem(half + 2, G2, R2),
            vmem(7, half, G2, R2),
            vmem(half + 2, G2, R2),
            vmem(half + 2, G2, R2),
            vmem(AZ3, G2, R2),
            vmem(A2 + 2, 2, G2, R2),
            vmem(40, R2),
            buf,
        ],
    )
    hf = exchange(*send)
    out, *send = call(
        postsmooth,
        [block] + faces(NH, NA, NR),
        (rhs, v0, m0, v1, *ha, *hb, *hf),
        [vmem(A1, NH, NR), vmem(2 * A1 + 2 * NH, NR)],
    )
    hg = exchange(*send)
    (scaled,) = call(final, [block], (rhs, out, m0, *ha, *hg))
    return out, scaled


def solution(mesh):
    return jax.shard_map(
        body,
        mesh=mesh,
        in_specs=(
            P("az", "gz", None),
            P("az", "gz", None),
            P("az", "gz", None),
            P(("az", "gz")),
            P(("az", "gz")),
            P(("az", "gz")),
        ),
        out_specs=(P("az", "gz", None), P("az", "gz", None)),
        check_vma=False,
    )
```

time: 768 us -> 113 us (0.15); the launches traced: 756 us -> 113 us
  starting transfers between devices: 284 us -> 31.1 us
  local copies, waits for them, and re-layouts: 173 us -> 4.41 us
  other arithmetic: 165 us -> 0 us
  waiting for transfers between devices: 73.4 us -> 21.7 us
  blocking collectives: 56.6 us -> 25.1 us
  Pallas kernels: 0 us -> 29.1 us
    ppermute x111 -> x21, starting transfers between devices: 284 us -> 31.1 us  [swap(): return lax.ppermute(x, axis, pairs)]
    reshape x11 -> x0, local copies, waits for them, and re-layouts: 91 us -> none  [the longest x5 86.3 us: coarsen(): array_in.reshape(az_n // 2, 2, ht_n // 2, 2, rad_n // 2, 2)]
    all_gather x2 -> x0, blocking collectives: 56.6 us -> none  [consolidate(): gathered = lax.all_gather(array_in, 'gz', axis=1, tiled=True)]
    ppermute x111 -> x21, waiting for transfers between devices: 73.4 us -> 21.7 us  [swap(): return lax.ppermute(x, axis, pairs)]
    add x44 -> x0, other arithmetic: 44 us -> none  [the longest x35 42.1 us: jacobi_sweep(): center + OMEGA * (source_part - apply_ext(padded, weights)) / weights[6]]
    slice x90 -> x0, local copies, waits for them, and re-layouts: 37.8 us -> none  [the longest x46 19.1 us: padded_2(): last = lax.slice_in_dim(x, length - width, length, axis=dim)]
    reduce_sum x6 -> x0, other arithmetic: 34.7 us -> none  [coarsen(): array_in.reshape(az_n // 2, 2, ht_n // 2, 2, rad_n // 2, 2)]
    pallas_call x0 -> x7, Pallas kernels: none -> 29.1 us  [call(): pl.pallas_call(kernel, out_shape=outs, in_specs=specs, out_specs=[pl.Bloc...]
  transfers between devices with their start and end apart: 111 -> 21, of which waited for: 82 -> 6; matrix products, arithmetic and copies ran while one was open for 31% -> 0% of each run, Pallas kernels for 0% -> 0%
where the time goes in v1:
time: 113 us
  starting transfers between devices  31.1 us (28%)
  Pallas kernels  29.1 us (26%)
  blocking collectives  25.1 us (22%)
  waiting for transfers between devices  21.7 us (19%)
  local copies, waits for them, and re-layouts  4.41 us (4%)
  between operations  1.37 us (1%)
    ppermute x21, starting transfers between devices, swap(): return lax.ppermute(x, axis, pairs)  31.1 us
    pallas_call x7, Pallas kernels, call(): pl.pallas_call(kernel, out_shape=outs, in_specs=specs, out_specs=[pl.Bloc...  29.1 us
    all_to_all x1, blocking collectives, gathered(): lax.all_to_all(x, ('az', 'gz'), 0, 0, tiled=True, axis_index_groups=groups)  25.1 us
    ppermute x21, waiting for transfers between devices, swap(): return lax.ppermute(x, axis, pairs)  21.7 us
    unnamed x12, local copies, waits for them, and re-layouts  4.41 us
  transfers between devices with their start and end apart: 21, of which 6 were waited for; matrix products, arithmetic and copies ran while one was open for 0% of the time, Pallas kernels for 0%

profile of v1, /device:TPU:0, one launch (start us, length us, event | category | flops | bytes accessed | tf_op | source)
XLA Modules:
  0.0 112.7 jit_solution(12855691656334650235)
XLA Ops:
  1.9 1.0 copy-done
  4.0 1.2 %shard_map.77 = (f32[32,8,512]{2,1,0:T(8,128)S(1)}, f32[64,256]{1,0:T(8,128)S(1)}, f32[16,128]{1,0:T(8,128)S(1)}, f32[24,512]{1,0:T(8,128)S(1)}, f32[24,512]{1,0...) custom-call(f32[32,8,512]{2,1,0:T(8,128)S(1)} %copy-done, f32[32,8,512]{2,1,0:T(8,128)S(1)} %copy-done.2, ...), custom_call_target="tpu_custom_call" | custom-call | tf_op jit(solution)/shard_map/pallas_call | solution.py:33
  5.2 2.0 %collective-permute-start.2 = (f32[80,512]{1,0:T(8,128)S(1)}, f32[80,512]{1,0:T(8,128)S(1)}, u32[]{:S(2)}, u32[]{:S(2)}) collective-permute-start(f32[80,512]{1,0:T(8,128)S(1)} %get-tuple-element.34), channel_id=1, source_target_pairs={{0,1},{1,0},{2,3},{3,2},{4,5},{5,4},{6,7},{7,6},{8,9},{9,8},{10,11... | collective-permute-start | bytes 491528 | tf_op jit(solution)/shard_map/ppermute | solution.py:592
  7.2 2.6 %collective-permute-start.3 = (f32[80,512]{1,0:T(8,128)S(1)}, f32[80,512]{1,0:T(8,128)S(1)}, u32[]{:S(2)}, u32[]{:S(2)}) collective-permute-start(f32[80,512]{1,0:T(8,128)S(1)} %get-tuple-element.35), channel_id=1, source_target_pairs={{0,7},{1,2},{2,1},{3,4},{4,3},{5,6},{6,5},{7,0},{8,15},{9,10},{10,... | collective-permute-start | bytes 491528 | tf_op jit(solution)/shard_map/ppermute | solution.py:592
  9.7 5.0 %collective-permute-start = (f32[24,512]{1,0:T(8,128)S(1)}, f32[24,512]{1,0:T(8,128)S(1)}, u32[]{:S(2)}, u32[]{:S(2)}) collective-permute-start(f32[24,512]{1,0:T(8,128)S(1)} %get-tuple-element.32), channel_id=1, source_target_pairs={{0,120},{8,16},{16,8},{24,32},{32,24},{40,48},{48,40},{56,64},{64,... | collective-permute-start | bytes 147464 | tf_op jit(solution)/shard_map/ppermute | solution.py:592
  14.7 2.3 %collective-permute-done.ax = f32[24,512]{1,0:T(8,128)S(1)} collective-permute-done((f32[24,512]{1,0:T(8,128)S(1)}, f32[24,512]{1,0:T(8,128)S(1)}, u32[]{:S(2)}, u32[]{:S(2)}) %collective-permute-start) | collective-permute-done | bytes 49184 | tf_op jit(solution)/shard_map/ppermute | solution.py:592
  17.7 1.3 %shard_map.78 = (f32[32,8,512]{2,1,0:T(8,128)S(1)}, f32[32,8,512]{2,1,0:T(8,128)S(1)}, f32[8,512]{1,0:T(8,128)S(1)}, f32[8,512]{1,0:T(8,128)S(1)}, f32[32,512]{1,0:T(8,128)S(1)}, /*index=5*/f32[32,512]{1,0:T(8,128)S(1)}) custom-call(f32[32,8,512]{2,1,0:T(8,128)S(1)} %copy-done, f32[32,8,512]{2,1,0:T(8,128)S(1)} %copy-done.1, ...), custom_call_target="tpu_custom_call" | custom-call | tf_op jit(solution)/shard_map/pallas_call | solution.py:33
  20.0 1.8 %collective-permute-start.7 = (f32[32,512]{1,0:T(8,128)S(1)}, f32[32,512]{1,0:T(8,128)S(1)}, u32[]{:S(2)}, u32[]{:S(2)}) collective-permute-start(f32[32,512]{1,0:T(8,128)S(1)} %get-tuple-element.42), channel_id=1, source_target_pairs={{0,7},{1,2},{2,1},{3,4},{4,3},{5,6},{6,5},{7,0},{8,15},{9,10},{10,... | collective-permute-start | bytes 196616 | tf_op jit(solution)/shard_map/ppermute | solution.py:592
  21.8 4.1 %collective-permute-start.4 = (f32[8,512]{1,0:T(8,128)S(1)}, f32[8,512]{1,0:T(8,128)S(1)}, u32[]{:S(2)}, u32[]{:S(2)}) collective-permute-start(f32[8,512]{1,0:T(8,128)S(1)} %get-tuple-element.39), channel_id=1, source_target_pairs={{0,120},{8,16},{16,8},{24,32},{32,24},{40,48},{48,40},{56,64},{64,... | collective-permute-start | bytes 49160 | tf_op jit(solution)/shard_map/ppermute | solution.py:592
  25.9 2.7 %collective-permute-done.4.bx = f32[8,512]{1,0:T(8,128)S(1)} collective-permute-done((f32[8,512]{1,0:T(8,128)S(1)}, f32[8,512]{1,0:T(8,128)S(1)}, u32[]{:S(2)}, u32[]{:S(2)}) %collective-permute-start.4) | collective-permute-done | bytes 16416 | tf_op jit(solution)/shard_map/ppermute | solution.py:592
  28.6 1.8 %shard_map.79 = (f32[64,256]{1,0:T(8,128)S(1)}, f32[64,256]{1,0:T(8,128)S(1)}, f32[4,256]{1,0:T(4,128)S(1)}, f32[4,256]{1,0:T(4,128)S(1)}, f32[16,256]{1,0:T(8,128)S(1)}, /*index=5*/f32[16,256]{1,0:T(8,128)S(1)}) custom-call(f32[32,8,512]{2,1,0:T(8,128)S(1)} %get-tuple-element.36.rhs_ref, f32[32,8,512]{2,1,0:T(8,128)S(1)} %get-tuple-element.37.v_ref, ...), custom_call_target="tpu_custom_call" | custom-call | tf_op jit(solution)/shard_map/pallas_call | solution.py:33
  31.2 1.7 %collective-permute-start.11 = (f32[16,256]{1,0:T(8,128)S(1)}, f32[16,256]{1,0:T(8,128)S(1)}, u32[]{:S(2)}, u32[]{:S(2)}) collective-permute-start(f32[16,256]{1,0:T(8,128)S(1)} %get-tuple-element.49), channel_id=1, source_target_pairs={{0,7},{1,2},{2,1},{3,4},{4,3},{5,6},{6,5},{7,0},{8,15},{9,10},{10,... | collective-permute-start | bytes 49160 | tf_op jit(solution)/shard_map/ppermute | solution.py:592
  32.9 3.5 %collective-permute-start.8 = (f32[4,256]{1,0:T(4,128)S(1)}, f32[4,256]{1,0:T(4,128)S(1)}, u32[]{:S(2)}, u32[]{:S(2)}) collective-permute-start(f32[4,256]{1,0:T(4,128)S(1)} %get-tuple-element.46), channel_id=1, source_target_pairs={{0,120},{8,16},{16,8},{24,32},{32,24},{40,48},{48,40},{56,64},{64,... | collective-permute-start | bytes 12296 | tf_op jit(solution)/shard_map/ppermute | solution.py:592
  36.4 3.2 %collective-permute-done.8.cx = f32[4,256]{1,0:T(4,128)S(1)} collective-permute-done((f32[4,256]{1,0:T(4,128)S(1)}, f32[4,256]{1,0:T(4,128)S(1)}, u32[]{:S(2)}, u32[]{:S(2)}) %collective-permute-start.8) | collective-permute-done | bytes 4128 | tf_op jit(solution)/shard_map/ppermute | solution.py:592
  40.4 25.1 %all_to_all.5 = f32[64,32,128]{2,1,0:T(8,128)S(1)} all-to-all(f32[64,32,128]{2,1,0:T(8,128)S(1)} %shard_map.80), channel_id=1, replica_groups={{0,1,2,3,4,5,6,7,16,17,18,19,20,21,22,23,32,33,34,35,36,37,38,39,48,49,..., dimensions={0} | all-to-all | bytes 2097152 | tf_op jit(solution)/shard_map/all_to_all | solution.py:601
  65.5 2.7 %collective-permute-done.12.oth = f32[2048,128]{1,0:T(8,128)S(1)} collective-permute-done((f32[2048,128]{1,0:T(8,128)S(1)}, f32[2048,128]{1,0:T(8,128)S(1)}, u32[]{:S(2)}, u32[]{:S(2)}) %collective-permute-start.12) | collective-permute-done | bytes 1048608 | tf_op jit(solution)/shard_map/ppermute | solution.py:592
  68.2 19.1 %shard_map.81 = (f32[64,256]{1,0:T(8,128)S(1)}, f32[4,256]{1,0:T(4,128)S(1)}, f32[4,256]{1,0:T(4,128)S(1)}, f32[16,256]{1,0:T(8,128)S(1)}, f32[16,256]{1,0:T(8,128)S(1)}) custom-call(f32[2048,128]{1,0:T(8,128)S(1)} %bitcast.4, f32[2048,128]{1,0:T(8,128)S(1)} %collective-permute-done.12.oth, f32[64,256]{1,0:T(8,128)S(1)} %get-tuple-element.43.b1_ref, ...), custom_call_target="tpu_custom_call" | custom-call | tf_op jit(solution)/shard_map/pallas_call | solution.py:33
  88.3 3.3 %collective-permute-start.16 = (f32[16,256]{1,0:T(8,128)S(1)}, f32[16,256]{1,0:T(8,128)S(1)}, u32[]{:S(2)}, u32[]{:S(2)}) collective-permute-start(f32[16,256]{1,0:T(8,128)S(1)} %get-tuple-element.54), channel_id=1, source_target_pairs={{0,7},{1,2},{2,1},{3,4},{4,3},{5,6},{6,5},{7,0},{8,15},{9,10},{10,... | collective-permute-start | bytes 49160 | tf_op jit(solution)/shard_map/ppermute | solution.py:592
  92.6 5.6 %collective-permute-done.13.fx = f32[4,256]{1,0:T(4,128)S(1)} collective-permute-done((f32[4,256]{1,0:T(4,128)S(1)}, f32[4,256]{1,0:T(4,128)S(1)}, u32[]{:S(2)}, u32[]{:S(2)}) %collective-permute-start.13) | collective-permute-done | bytes 4128 | tf_op jit(solution)/shard_map/ppermute | solution.py:592
  98.3 3.2 %shard_map.82 = (f32[32,8,512]{2,1,0:T(8,128)}, f32[8,512]{1,0:T(8,128)S(1)}, f32[8,512]{1,0:T(8,128)S(1)}, f32[32,512]{1,0:T(8,128)S(1)}, f32[32,512]{1,0:T(8,128)S(1)}) custom-call(f32[32,8,512]{2,1,0:T(8,128)S(1)} %get-tuple-element.36.rhs_ref, f32[32,8,512]{2,1,0:T(8,128)S(1)} %get-tuple-element.37.v_ref, f32[32,8,512]{2,1,0:T(8,128)S(1)} %get-tuple-element.31.m_ref, ...), custom_call_target="tpu_custom_call" | custom-call | tf_op jit(solution)/shard_map/pallas_call | solution.py:33
  101.4 1.7 %collective-permute-start.20 = (f32[32,512]{1,0:T(8,128)S(1)}, f32[32,512]{1,0:T(8,128)S(1)}, u32[]{:S(2)}, u32[]{:S(2)}) collective-permute-start(f32[32,512]{1,0:T(8,128)S(1)} %get-tuple-element.59), channel_id=1, source_target_pairs={{0,7},{1,2},{2,1},{3,4},{4,3},{5,6},{6,5},{7,0},{8,15},{9,10},{10,... | collective-permute-start | bytes 196616 | tf_op jit(solution)/shard_map/ppermute | solution.py:592
  103.2 1.6 %collective-permute-start.17 = (f32[8,512]{1,0:T(8,128)S(1)}, f32[8,512]{1,0:T(8,128)S(1)}, u32[]{:S(2)}, u32[]{:S(2)}) collective-permute-start(f32[8,512]{1,0:T(8,128)S(1)} %get-tuple-element.56), channel_id=1, source_target_pairs={{0,120},{8,16},{16,8},{24,32},{32,24},{40,48},{48,40},{56,64},{64,... | collective-permute-start | bytes 49160 | tf_op jit(solution)/shard_map/ppermute | solution.py:592
  104.8 5.2 %collective-permute-done.17.gx = f32[8,512]{1,0:T(8,128)S(1)} collective-permute-done((f32[8,512]{1,0:T(8,128)S(1)}, f32[8,512]{1,0:T(8,128)S(1)}, u32[]{:S(2)}, u32[]{:S(2)}) %collective-permute-start.17) | collective-permute-done | bytes 16416 | tf_op jit(solution)/shard_map/ppermute | solution.py:592
  111.0 1.7 %shard_map.83 = f32[32,8,512]{2,1,0:T(8,128)} custom-call(f32[32,8,512]{2,1,0:T(8,128)S(1)} %get-tuple-element.36.rhs_ref, f32[32,8,512]{2,1,0:T(8,128)S(1)} %copy-done.3, f32[32,8,512]{2,1,0:T(8,128)S(1)} %get-tuple-element.31.m_ref, f32[24,512]{1,0:T(8,128)S(1)} %collective-permute-done.ax, f32[24,512]{1,0:T(8,128)S(1)} %collective-permute-done.1.ac, ...), custom_call_target="tpu_custom_call" | custom-call | tf_op jit(solution)/shard_map/pallas_call | solution.py:33
  (38 shorter events, 8.1 us)
Async XLA Ops:
  1.9 1.0 copy-start
  4.0 13.0 %copy-start.1 = (f32[32,8,512]{2,1,0:T(8,128)S(1)}, f32[32,8,512]{2,1,0:T(8,128)}, u32[]{:S(2)}) copy-start(f32[32,8,512]{2,1,0:T(8,128)} %div_ref.1) | copy-start | bytes 1572868
  5.2 11.8 %collective-permute-start.2 = (f32[80,512]{1,0:T(8,128)S(1)}, f32[80,512]{1,0:T(8,128)S(1)}, u32[]{:S(2)}, u32[]{:S(2)}) collective-permute-start(f32[80,512]{1,0:T(8,128)S(1)} %get-tuple-element.34), channel_id=1, source_target_pairs={{0,1},{1,0},{2,3},{3,2},{4,5},{5,4},{6,7},{7,6},{8,9},{9,8},{10,11... | collective-permute-start | bytes 491528 | tf_op jit(solution)/shard_map/ppermute | solution.py:592
  7.2 9.8 %collective-permute-start.3 = (f32[80,512]{1,0:T(8,128)S(1)}, f32[80,512]{1,0:T(8,128)S(1)}, u32[]{:S(2)}, u32[]{:S(2)}) collective-permute-start(f32[80,512]{1,0:T(8,128)S(1)} %get-tuple-element.35), channel_id=1, source_target_pairs={{0,7},{1,2},{2,1},{3,4},{4,3},{5,6},{6,5},{7,0},{8,15},{9,10},{10,... | collective-permute-start | bytes 491528 | tf_op jit(solution)/shard_map/ppermute | solution.py:592
  9.7 7.2 %collective-permute-start = (f32[24,512]{1,0:T(8,128)S(1)}, f32[24,512]{1,0:T(8,128)S(1)}, u32[]{:S(2)}, u32[]{:S(2)}) collective-permute-start(f32[24,512]{1,0:T(8,128)S(1)} %get-tuple-element.32), channel_id=1, source_target_pairs={{0,120},{8,16},{16,8},{24,32},{32,24},{40,48},{48,40},{56,64},{64,... | collective-permute-start | bytes 147464 | tf_op jit(solution)/shard_map/ppermute | solution.py:592
  14.7 2.3 %collective-permute-start.1 = (f32[24,512]{1,0:T(8,128)S(1)}, f32[24,512]{1,0:T(8,128)S(1)}, u32[]{:S(2)}, u32[]{:S(2)}) collective-permute-start(f32[24,512]{1,0:T(8,128)S(1)} %get-tuple-element.33), channel_id=1, source_target_pairs={{0,8},{8,0},{16,24},{24,16},{32,40},{40,32},{48,56},{56,48},{64,72... | collective-permute-start | bytes 147464 | tf_op jit(solution)/shard_map/ppermute | solution.py:592
  19.0 9.6 %collective-permute-start.6 = (f32[32,512]{1,0:T(8,128)S(1)}, f32[32,512]{1,0:T(8,128)S(1)}, u32[]{:S(2)}, u32[]{:S(2)}) collective-permute-start(f32[32,512]{1,0:T(8,128)S(1)} %get-tuple-element.41), channel_id=1, source_target_pairs={{0,1},{1,0},{2,3},{3,2},{4,5},{5,4},{6,7},{7,6},{8,9},{9,8},{10,11... | collective-permute-start | bytes 196616 | tf_op jit(solution)/shard_map/ppermute | solution.py:592
  20.0 8.6 %collective-permute-start.7 = (f32[32,512]{1,0:T(8,128)S(1)}, f32[32,512]{1,0:T(8,128)S(1)}, u32[]{:S(2)}, u32[]{:S(2)}) collective-permute-start(f32[32,512]{1,0:T(8,128)S(1)} %get-tuple-element.42), channel_id=1, source_target_pairs={{0,7},{1,2},{2,1},{3,4},{4,3},{5,6},{6,5},{7,0},{8,15},{9,10},{10,... | collective-permute-start | bytes 196616 | tf_op jit(solution)/shard_map/ppermute | solution.py:592
  21.8 6.8 %collective-permute-start.4 = (f32[8,512]{1,0:T(8,128)S(1)}, f32[8,512]{1,0:T(8,128)S(1)}, u32[]{:S(2)}, u32[]{:S(2)}) collective-permute-start(f32[8,512]{1,0:T(8,128)S(1)} %get-tuple-element.39), channel_id=1, source_target_pairs={{0,120},{8,16},{16,8},{24,32},{32,24},{40,48},{48,40},{56,64},{64,... | collective-permute-start | bytes 49160 | tf_op jit(solution)/shard_map/ppermute | solution.py:592
  25.9 2.7 %collective-permute-start.5 = (f32[8,512]{1,0:T(8,128)S(1)}, f32[8,512]{1,0:T(8,128)S(1)}, u32[]{:S(2)}, u32[]{:S(2)}) collective-permute-start(f32[8,512]{1,0:T(8,128)S(1)} %get-tuple-element.40), channel_id=1, source_target_pairs={{0,8},{8,0},{16,24},{24,16},{32,40},{40,32},{48,56},{56,48},{64,72... | collective-permute-start | bytes 49160 | tf_op jit(solution)/shard_map/ppermute | solution.py:592
  30.4 9.2 %collective-permute-start.10 = (f32[16,256]{1,0:T(8,128)S(1)}, f32[16,256]{1,0:T(8,128)S(1)}, u32[]{:S(2)}, u32[]{:S(2)}) collective-permute-start(f32[16,256]{1,0:T(8,128)S(1)} %get-tuple-element.48), channel_id=1, source_target_pairs={{0,1},{1,0},{2,3},{3,2},{4,5},{5,4},{6,7},{7,6},{8,9},{9,8},{10,11... | collective-permute-start | bytes 49160 | tf_op jit(solution)/shard_map/ppermute | solution.py:592
  31.2 8.4 %collective-permute-start.11 = (f32[16,256]{1,0:T(8,128)S(1)}, f32[16,256]{1,0:T(8,128)S(1)}, u32[]{:S(2)}, u32[]{:S(2)}) collective-permute-start(f32[16,256]{1,0:T(8,128)S(1)} %get-tuple-element.49), channel_id=1, source_target_pairs={{0,7},{1,2},{2,1},{3,4},{4,3},{5,6},{6,5},{7,0},{8,15},{9,10},{10,... | collective-permute-start | bytes 49160 | tf_op jit(solution)/shard_map/ppermute | solution.py:592
  32.9 6.6 %collective-permute-start.8 = (f32[4,256]{1,0:T(4,128)S(1)}, f32[4,256]{1,0:T(4,128)S(1)}, u32[]{:S(2)}, u32[]{:S(2)}) collective-permute-start(f32[4,256]{1,0:T(4,128)S(1)} %get-tuple-element.46), channel_id=1, source_target_pairs={{0,120},{8,16},{16,8},{24,32},{32,24},{40,48},{48,40},{56,64},{64,... | collective-permute-start | bytes 12296 | tf_op jit(solution)/shard_map/ppermute | solution.py:592
  36.4 3.2 %collective-permute-start.9 = (f32[4,256]{1,0:T(4,128)S(1)}, f32[4,256]{1,0:T(4,128)S(1)}, u32[]{:S(2)}, u32[]{:S(2)}) collective-permute-start(f32[4,256]{1,0:T(4,128)S(1)} %get-tuple-element.47), channel_id=1, source_target_pairs={{0,8},{8,0},{16,24},{24,16},{32,40},{40,32},{48,56},{56,48},{64,72... | collective-permute-start | bytes 12296 | tf_op jit(solution)/shard_map/ppermute | solution.py:592
  65.5 2.7 %collective-permute-start.12 = (f32[2048,128]{1,0:T(8,128)S(1)}, f32[2048,128]{1,0:T(8,128)S(1)}, u32[]{:S(2)}, u32[]{:S(2)}) collective-permute-start(f32[2048,128]{1,0:T(8,128)S(1)} %bitcast.3), channel_id=1, source_target_pairs={{0,8},{8,0},{16,24},{24,16},{32,40},{40,32},{48,56},{56,48},{64,72... | collective-permute-start | bytes 3145736 | tf_op jit(solution)/shard_map/ppermute | solution.py:592
  87.3 10.9 %collective-permute-start.15 = (f32[16,256]{1,0:T(8,128)S(1)}, f32[16,256]{1,0:T(8,128)S(1)}, u32[]{:S(2)}, u32[]{:S(2)}) collective-permute-start(f32[16,256]{1,0:T(8,128)S(1)} %get-tuple-element.53), channel_id=1, source_target_pairs={{0,1},{1,0},{2,3},{3,2},{4,5},{5,4},{6,7},{7,6},{8,9},{9,8},{10,11... | collective-permute-start | bytes 49160 | tf_op jit(solution)/shard_map/ppermute | solution.py:592
  88.3 10.0 %collective-permute-start.16 = (f32[16,256]{1,0:T(8,128)S(1)}, f32[16,256]{1,0:T(8,128)S(1)}, u32[]{:S(2)}, u32[]{:S(2)}) collective-permute-start(f32[16,256]{1,0:T(8,128)S(1)} %get-tuple-element.54), channel_id=1, source_target_pairs={{0,7},{1,2},{2,1},{3,4},{4,3},{5,6},{6,5},{7,0},{8,15},{9,10},{10,... | collective-permute-start | bytes 49160 | tf_op jit(solution)/shard_map/ppermute | solution.py:592
  91.6 6.6 %collective-permute-start.13 = (f32[4,256]{1,0:T(4,128)S(1)}, f32[4,256]{1,0:T(4,128)S(1)}, u32[]{:S(2)}, u32[]{:S(2)}) collective-permute-start(f32[4,256]{1,0:T(4,128)S(1)} %get-tuple-element.51), channel_id=1, source_target_pairs={{0,120},{8,16},{16,8},{24,32},{32,24},{40,48},{48,40},{56,64},{64,... | collective-permute-start | bytes 12296 | tf_op jit(solution)/shard_map/ppermute | solution.py:592
  92.6 5.6 %collective-permute-start.14 = (f32[4,256]{1,0:T(4,128)S(1)}, f32[4,256]{1,0:T(4,128)S(1)}, u32[]{:S(2)}, u32[]{:S(2)}) collective-permute-start(f32[4,256]{1,0:T(4,128)S(1)} %get-tuple-element.52), channel_id=1, source_target_pairs={{0,8},{8,0},{16,24},{24,16},{32,40},{40,32},{48,56},{56,48},{64,72... | collective-permute-start | bytes 12296 | tf_op jit(solution)/shard_map/ppermute | solution.py:592
  101.4 8.5 %collective-permute-start.19 = (f32[32,512]{1,0:T(8,128)S(1)}, f32[32,512]{1,0:T(8,128)S(1)}, u32[]{:S(2)}, u32[]{:S(2)}) collective-permute-start(f32[32,512]{1,0:T(8,128)S(1)} %get-tuple-element.58), channel_id=1, source_target_pairs={{0,1},{1,0},{2,3},{3,2},{4,5},{5,4},{6,7},{7,6},{8,9},{9,8},{10,11... | collective-permute-start | bytes 196616 | tf_op jit(solution)/shard_map/ppermute | solution.py:592
  101.4 8.5 %collective-permute-start.20 = (f32[32,512]{1,0:T(8,128)S(1)}, f32[32,512]{1,0:T(8,128)S(1)}, u32[]{:S(2)}, u32[]{:S(2)}) collective-permute-start(f32[32,512]{1,0:T(8,128)S(1)} %get-tuple-element.59), channel_id=1, source_target_pairs={{0,7},{1,2},{2,1},{3,4},{4,3},{5,6},{6,5},{7,0},{8,15},{9,10},{10,... | collective-permute-start | bytes 196616 | tf_op jit(solution)/shard_map/ppermute | solution.py:592
  103.2 6.8 %collective-permute-start.17 = (f32[8,512]{1,0:T(8,128)S(1)}, f32[8,512]{1,0:T(8,128)S(1)}, u32[]{:S(2)}, u32[]{:S(2)}) collective-permute-start(f32[8,512]{1,0:T(8,128)S(1)} %get-tuple-element.56), channel_id=1, source_target_pairs={{0,120},{8,16},{16,8},{24,32},{32,24},{40,48},{48,40},{56,64},{64,... | collective-permute-start | bytes 49160 | tf_op jit(solution)/shard_map/ppermute | solution.py:592
  104.8 5.2 %collective-permute-start.18 = (f32[8,512]{1,0:T(8,128)S(1)}, f32[8,512]{1,0:T(8,128)S(1)}, u32[]{:S(2)}, u32[]{:S(2)}) collective-permute-start(f32[8,512]{1,0:T(8,128)S(1)} %get-tuple-element.57), channel_id=1, source_target_pairs={{0,8},{8,0},{16,24},{24,16},{32,40},{40,32},{48,56},{56,48},{64,72... | collective-permute-start | bytes 49160 | tf_op jit(solution)/shard_map/ppermute | solution.py:592
  110.0 1.0 copy-start.3
  (3 other events, 2.4 us)

commit v2 on v1

--- a/solution.py
+++ b/solution.py
@@ -26,15 +26,19 @@
     return jax.ShapeDtypeStruct(shape, F32)
 
 
-def call(kernel, outs, ins, scratch=(), smem=(), limit=48):
-    specs = [
-        pl.BlockSpec(memory_space=pltpu.SMEM if i in smem else pltpu.VMEM) for i in range(len(ins))
-    ]
+def call(kernel, outs, ins, scratch=(), smem=(), hbm=(), hbm_out=(), limit=48):
+    def space(i, far):
+        return pltpu.HBM if i in far else pltpu.SMEM if i in smem else pltpu.VMEM
+
+    specs = [pl.BlockSpec(memory_space=space(i, hbm)) for i in range(len(ins))]
     return pl.pallas_call(
         kernel,
         out_shape=outs,
         in_specs=specs,
-        out_specs=[pl.BlockSpec(memory_space=pltpu.VMEM) for _ in outs],
+        out_specs=[
+            pl.BlockSpec(memory_space=pltpu.HBM if i in hbm_out else pltpu.VMEM)
+            for i in range(len(outs))
+        ],
         scratch_shapes=list(scratch),
         compiler_params=pltpu.CompilerParams(vmem_limit_bytes=limit * 1024 * 1024),
     )(*ins)
@@ -195,8 +199,31 @@
         y_ref[rows_at + i : rows_at + i + 1, 0:R1] = pick(pg, low, high)
 
 
-def prepare(p_ref, void_ref, vol_ref, cnt_ref, m0_ref, m1_ref, m2_ref, sx, sc, sz, sy, pairs):
+def prepare(
+    p_hbm, void_hbm, vol_hbm, cell_hbm, cnt_ref,
+    m0_ref, m1_ref, m2_ref, cell_ref, sx, sc, sz, sy,
+    p_ref, void_ref, vol_ref, pairs, sems,
+):
+    part = NA // 4
+    copies = [
+        pltpu.make_async_copy(
+            src.at[pl.ds(k * part, part)], dst.at[pl.ds(k * part, part)], sems.at[4 * n + k]
+        )
+        for n, (src, dst) in enumerate(((void_hbm, void_ref), (p_hbm, p_ref)))
+        for k in range(4)
+    ]
+    copies.append(pltpu.make_async_copy(vol_hbm, vol_ref, sems.at[8]))
+    copies.append(pltpu.make_async_copy(cell_hbm, cell_ref, sems.at[9]))
+    for copy in copies:
+        copy.start()
+    zero = jnp.zeros((NH, NR), F32)
+    sx[2 * NH : 3 * NH, :] = zero
+    sc[2 * NH : 3 * NH, :] = zero
+    for ref in (sz, sy):
+        ref[2 * NA : 2 * NA + A1, R1:NR] = jnp.zeros((A1, NR - R1), F32)
     for i in range(0, NA, 2):
+        if i % part == 0:
+            copies[i // part].wait()
         u = 1.0 / (1.0 - void_ref[i])
         v = 1.0 / (1.0 - void_ref[i + 1])
         m0_ref[i] = u
@@ -204,14 +231,13 @@
         pairs[(i // 2) * NH : (i // 2 + 1) * NH, :] = u + v
     m1 = 0.125 * dot(pair_rows_h(A1 * NH), dot(pairs[...], pair_cols(NR)))
     m1_ref[...] = m1
-    m2_ref[...] = 0.125 * dot(block_rows(A1, H1), dot(m1, pair_cols(R1)))
+    m2 = 0.125 * dot(block_rows(A1, H1), dot(m1, pair_cols(R1)))
+    for k in range(m2_ref.shape[0]):
+        m2_ref[k] = m2
+    for copy in copies[4:]:
+        copy.wait()
     store_faces(p_ref, sx, sc, sz, sy, 0, 0)
     store_faces(m0_ref, sx, sc, sz, sy, NH, NA)
-    zero = jnp.zeros((NH, NR), F32)
-    sx[2 * NH : 3 * NH, :] = zero
-    sc[2 * NH : 3 * NH, :] = zero
-    for ref in (sz, sy):
-        ref[2 * NA : 2 * NA + A1, R1:NR] = jnp.zeros((A1, NR - R1), F32)
     store_faces1(m1_ref, sx, sc, sz, sy, 2 * NH, 2 * NA)
     live = jnp.where(iota((1, SLOTS), 1) < cnt_ref[0], vol_ref[...], 0.0)
     sx[2 * NH + H1 : 2 * NH + H1 + 1, 0:SLOTS] = live
@@ -266,7 +292,7 @@
     v_of, vb, va = fine_values(p_ref, ah)
 
     def emit(i, diagonal, around, centre):
-        v_ref[i] = centre + OMEGA * (rhs_ref[i] - diagonal * centre + around) / diagonal
+        v_ref[i] = (1.0 - OMEGA) * centre + OMEGA * (rhs_ref[i] + around) / diagonal
 
     fine_walk(m_of, v_of, mb, ma, vb, va, emit)
     store_faces(v_ref, sx, sc, sz, sy)
@@ -314,37 +340,32 @@
     )
 
 
-def restrict1(b1_ref, v1_ref, m1_ref, m2_ref, ax, ac, az, ay, cx, cc, cz, cy, out_ref, buf):
+def restrict1(b1_ref, v1_ref, m1_ref, ax, ac, az, ay, cx, cc, cz, cy, out_ref, buf):
     ah, ch = Halo(ax, ac, az, ay), Halo(cx, cc, cz, cy)
-    w, diagonal = level1_weights(*mobility1(m1_ref, ah), buf)
-    v1 = v1_ref[...]
-    n = level1_around(v1, *halo1(ch), buf)
-    r1 = b1_ref[...] - diagonal * v1 + weighted(w, n)
+    w, _ = level1_weights(*mobility1(m1_ref, ah), buf)
+    n = level1_around(v1_ref[...], *halo1(ch), buf)
+    r1 = (1.0 - OMEGA) * b1_ref[...] + weighted(w, n)
     b2 = 0.5 * dot(block_rows(A1, H1), dot(r1, pair_cols(R1)))
-    m2 = m2_ref[...]
-    rows = A2 * H2
     for k in range(out_ref.shape[0]):
-        out_ref[k, 0:rows, :] = b2
-        out_ref[k, rows : 2 * rows, :] = m2
-
-
-def level2_plane(ca, ri, ro, zlo, zhi, mp, mc, mn):
+        out_ref[k] = b2
+
+
+def level2_plane(consts, face, mc, mn):
+    ca, ri, ro, zlo, zhi = consts
     mid = 0.5 * (mc[0] + mc[1])
     lows = (zlo * (mc[0] + pltpu.roll(mc[1], 1, 0)), mid)
     highs = (mid, zhi * (mc[1] + pltpu.roll(mc[0], G2 - 1, 0)))
+    nxt = level2_face(consts, mc, mn)
     out = []
     for p in range(2):
         m = mc[p]
-        w = (
-            ca * (m + mp[p]),
-            ca * (m + mn[p]),
-            lows[p],
-            highs[p],
-            ri * (m + pltpu.roll(m, 1, 1)),
-            ro * (m + pltpu.roll(m, R2 - 1, 1)),
-        )
-        out.append((w, (w[0] + w[1]) + (w[2] + w[3]) + (w[4] + w[5]) + SIGMA * 16.0))
-    return out
+        wi, wo = ri * (m + pltpu.roll(m, 1, 1)), ro * (m + pltpu.roll(m, R2 - 1, 1))
+        out.append((face[p], nxt[p], lows[p], highs[p], wi, wo))
+    return out, nxt
+
+
+def level2_face(consts, mp, mc):
+    return (consts[0] * (mp[0] + mc[0]), consts[0] * (mp[1] + mc[1]))
 
 
 def level2_around(vp, vc, vn):
@@ -356,88 +377,86 @@
     ]
 
 
-def coarse(
-    own, oth, b1_ref, v1_ref, m1_ref, ax, ac, az, ay, cx, cc, cz, cy,
-    v1_out, sx, sc, sz, sy,
-    m2, b2, v2, sum_m, sum_r, m3, w3, va, vb, e2, v2f, src, buf,
-):
+def total_weight(w):
+    return (w[0] + w[1]) + (w[2] + w[3]) + (w[4] + w[5])
+
+
+def height_walls():
+    sub = iota((G2, R2), 0)
+    return jnp.where(sub == 0, 0.0, 0.5), jnp.where(sub == G2 - 1, 0.0, 0.5)
+
+
+def level2_consts():
+    lane = iota((G2, R2), 1)
+    return radial_consts((G2, R2), R2, 2.0 * math.pi / AZ2, lane) + height_walls()
+
+
+def both(ref, s):
+    return (ref[s, 0], ref[s, 1])
+
+
+def close_ring(ref):
+    ref[0:2] = ref[AZ2 : AZ2 + 2]
+    ref[AZ2 + 2 : AZ2 + 4] = ref[2:4]
+
+
+HALF = AZ3 // 2
+
+
+def packed(ref):
+    row_i, col_i = iota((R2, R2), 0), iota((R2, R2), 1)
+    left = (row_i // 2 == col_i).astype(F32)
+    right = (row_i // 2 + R2 // 2 == col_i).astype(F32)
+    lower = ref[0:HALF].reshape(HALF * G2, R2)
+    upper = ref[HALF:AZ3].reshape(HALF * G2, R2)
+    return (dot(lower, left) + dot(upper, right)).reshape(HALF, G2, R2)
+
+
+def wrap(ref):
+    ref[0] = pltpu.roll(ref[HALF], R2 // 2, 1)
+    ref[HALF + 1] = pltpu.roll(ref[1], R2 // 2, 1)
+
+
+STEP = 8
+
+
+def coarse_weights(own, oth, m2, d2, w3, sum_m, m3):
     a, g = position()
     pa = a % 2
     rows = A2 * H2
-
     for k in range(N_AZ):
-        base = (k // 2) * N_GZ * 2 * rows
+        base = (k // 2) * N_GZ * rows
+        first, second = (own, oth) if k % 2 == 0 else (oth, own)
         for i in range(A2):
-            total = None
             for p in range(2):
-                at_b = pl.ds(base + i * 2 + p, G2, stride=2 * rows)
-                at_m = pl.ds(base + rows + i * 2 + p, G2, stride=2 * rows)
-                first, second = (own, oth) if k % 2 == 0 else (oth, own)
-                b2[k * A2 + i + 2, p] = pick(pa, first[at_b, :], second[at_b, :])
-                m2[k * A2 + i + 2, p] = pick(pa, first[at_m, :], second[at_m, :])
-    for ref in (m2, b2):
-        ref[0:2] = ref[AZ2 : AZ2 + 2]
-        ref[AZ2 + 2 : AZ2 + 4] = ref[2:4]
-
-    sub = iota((G2, R2), 0)
-    lane = iota((G2, R2), 1)
-    ca, ri, ro = radial_consts((G2, R2), R2, 2.0 * math.pi / AZ2, lane)
-    zlo = jnp.where(sub == 0, 0.0, 0.5)
-    zhi = jnp.where(sub == G2 - 1, 0.0, 0.5)
-    plane = functools.partial(level2_plane, ca, ri, ro, zlo, zhi)
-
-    def both(ref, s):
-        return (ref[s, 0], ref[s, 1])
-
-    def first_sweep(j, carry):
-        s = 2 * j + 2
-        planes = [both(m2, s + d) for d in (-1, 0, 1, 2)]
-        for d in range(2):
-            for p, (_, diagonal) in enumerate(plane(*planes[d : d + 3])):
-                v2[s + d, p] = OMEGA * b2[s + d, p] / diagonal
-        sum_m[j] = (planes[1][0] + planes[1][1]) + (planes[2][0] + planes[2][1])
+                at = pl.ds(base + i * 2 + p, G2, stride=rows)
+                m2[k * A2 + i + 2, p] = pick(pa, first[at, :], second[at, :])
+    close_ring(m2)
+    consts = level2_consts()
+
+    def diagonals(k, carry):
+        s = STEP * k + 2
+        mp, mc = both(m2, s - 1), both(m2, s)
+        face = level2_face(consts, mp, mc)
+        for d in range(STEP):
+            mn = both(m2, s + d + 1)
+            w, face = level2_plane(consts, face, mc, mn)
+            for p in range(2):
+                d2[s + d, p] = OMEGA / (total_weight(w[p]) + SIGMA * 16.0)
+            if d % 2:
+                sum_m[(STEP // 2) * k + d // 2] = (mp[0] + mp[1]) + (mc[0] + mc[1])
+            mp, mc = mc, mn
         return carry
 
-    lax.fori_loop(0, AZ3, first_sweep, 0)
-    v2[0:2] = v2[AZ2 : AZ2 + 2]
-    v2[AZ2 + 2 : AZ2 + 4] = v2[2:4]
-
-    def residuals(j, carry):
-        s = 2 * j + 2
-        planes = [both(m2, s + d) for d in (-1, 0, 1, 2)]
-        values = [both(v2, s + d) for d in (-1, 0, 1, 2)]
-        total = None
-        for d in range(2):
-            around = level2_around(*values[d : d + 3])
-            for p, (w, diagonal) in enumerate(plane(*planes[d : d + 3])):
-                r = b2[s + d, p] - diagonal * values[d + 1][p] + weighted(w, around[p])
-                total = r if total is None else total + r
-        sum_r[j] = total
-        return carry
-
-    lax.fori_loop(0, AZ3, residuals, 0)
-
-    half = AZ3 // 2
-    row_i, col_i = iota((R2, R2), 0), iota((R2, R2), 1)
-    left = (row_i // 2 == col_i).astype(F32)
-    right = (row_i // 2 + R2 // 2 == col_i).astype(F32)
-
-    def packed(ref):
-        lower = ref[0:half].reshape(half * G2, R2)
-        upper = ref[half:AZ3].reshape(half * G2, R2)
-        return (dot(lower, left) + dot(upper, right)).reshape(half, G2, R2)
-
-    def wrap(ref):
-        ref[0] = pltpu.roll(ref[half], R2 // 2, 1)
-        ref[half + 1] = pltpu.roll(ref[1], R2 // 2, 1)
-
-    m3[1 : half + 1] = 0.125 * packed(sum_m)
+    lax.fori_loop(0, AZ2 // STEP, diagonals, 0)
+    close_ring(d2)
+    m3[1 : HALF + 1] = 0.125 * packed(sum_m)
     wrap(m3)
-    b3 = 0.5 * packed(sum_r)
-    va[1 : half + 1] = b3
-    ca, ri, ro = radial_consts((G2, R2), R2 // 2, 2.0 * math.pi / AZ3, lane % (R2 // 2))
+    lane = iota((G2, R2), 1) % (R2 // 2)
+    ca, ri, ro = radial_consts((G2, R2), R2 // 2, 2.0 * math.pi / AZ3, lane)
+    zlo, zhi = height_walls()
     mp, mc = m3[0], m3[1]
-    for i in range(half):
+    for i in range(HALF):
         mn = m3[i + 2]
         w = (
             ca * (mc + mp),
@@ -447,19 +466,64 @@
             ri * (mc + pltpu.roll(mc, 1, 1)),
             ro * (mc + pltpu.roll(mc, R2 - 1, 1)),
         )
-        diagonal = (w[0] + w[1]) + (w[2] + w[3]) + (w[4] + w[5]) + SIGMA * 64.0
-        scale = OMEGA / diagonal
+        scale = OMEGA / (total_weight(w) + SIGMA * 64.0)
         for f in range(6):
             w3[f, i] = w[f] * scale
-        start = va[i + 1] * scale
-        w3[6, i] = start
+        w3[6, i] = scale
+        mp, mc = mc, mn
+
+
+def coarse(
+    own, oth, m2, d2, w3, b1_ref, v1_ref, m1_ref, ax, ac, az, ay, cx, cc, cz, cy,
+    v1_out, sx, sc, sz, sy,
+    b2, v2, sum_r, add, va, vb, e2, v2f, src, buf,
+):
+    a, g = position()
+    pa = a % 2
+    rows = A2 * H2
+
+    for k in range(N_AZ):
+        base = (k // 2) * N_GZ * rows
+        first, second = (own, oth) if k % 2 == 0 else (oth, own)
+        for i in range(A2):
+            for p in range(2):
+                at = pl.ds(base + i * 2 + p, G2, stride=rows)
+                b = pick(pa, first[at, :], second[at, :])
+                b2[k * A2 + i + 2, p] = b
+                v2[k * A2 + i + 2, p] = b * d2[k * A2 + i + 2, p]
+    close_ring(b2)
+    close_ring(v2)
+    consts = level2_consts()
+
+    def residuals(k, carry):
+        s = STEP * k + 2
+        mc = both(m2, s)
+        vp, vc = both(v2, s - 1), both(v2, s)
+        face = level2_face(consts, both(m2, s - 1), mc)
+        total = None
+        for d in range(STEP):
+            mn, vn = both(m2, s + d + 1), both(v2, s + d + 1)
+            w, face = level2_plane(consts, face, mc, mn)
+            n = level2_around(vp, vc, vn)
+            b = both(b2, s + d)
+            r = ((1.0 - OMEGA) * (b[0] + b[1]) + weighted(w[0], n[0])) + weighted(w[1], n[1])
+            if d % 2:
+                sum_r[(STEP // 2) * k + d // 2] = total + r
+            total, mc, vp, vc = r, mn, vc, vn
+        return carry
+
+    lax.fori_loop(0, AZ2 // STEP, residuals, 0)
+
+    b3 = 0.5 * packed(sum_r)
+    for i in range(HALF):
+        start = b3[i] * w3[6, i]
+        add[i] = start
         va[i + 1] = start
-        mp, mc = mc, mn
     wrap(va)
 
     def sweep(src_ref, dst_ref):
         vp, vc = src_ref[0], src_ref[1]
-        for i in range(half):
+        for i in range(HALF):
             vn = src_ref[i + 2]
             n = (
                 vp,
@@ -470,7 +534,7 @@
                 pltpu.roll(vc, R2 - 1, 1),
             )
             w = [w3[f, i] for f in range(6)]
-            dst_ref[i + 1] = ((1.0 - OMEGA) * vc + w3[6, i]) + weighted(w, n)
+            dst_ref[i + 1] = ((1.0 - OMEGA) * vc + add[i]) + weighted(w, n)
             vp, vc = vc, vn
         wrap(dst_ref)
 
@@ -482,23 +546,26 @@
     lax.fori_loop(0, (COARSE_SWEEPS - 2) // 2, two, 0)
     sweep(va, vb)
 
-    solved = vb[1 : half + 1].reshape(half * G2, R2)
-    e2[0:half] = dot(solved, (row_i == col_i // 2).astype(F32)).reshape(half, G2, R2)
-    e2[half:AZ3] = dot(solved, (row_i == col_i // 2 + R2 // 2).astype(F32)).reshape(half, G2, R2)
+    row_i, col_i = iota((R2, R2), 0), iota((R2, R2), 1)
+    solved = vb[1 : HALF + 1].reshape(HALF * G2, R2)
+    e2[0:HALF] = dot(solved, (row_i == col_i // 2).astype(F32)).reshape(HALF, G2, R2)
+    e2[HALF:AZ3] = dot(solved, (row_i == col_i // 2 + R2 // 2).astype(F32)).reshape(HALF, G2, R2)
 
     at = a * A2
-    ca, ri, ro = radial_consts((G2, R2), R2, 2.0 * math.pi / AZ2, lane)
-    plane = functools.partial(level2_plane, ca, ri, ro, zlo, zhi)
     values = []
     for k in range(A2 + 4):
         e = e2[(a * (A2 // 2) - 1 + k // 2 + AZ3) % AZ3]
         values.append((v2[at + k, 0] + e, v2[at + k, 1] + e))
+    mc = both(m2, at + 1)
+    face = level2_face(consts, both(m2, at), mc)
     for k in range(1, A2 + 3):
-        around = level2_around(*values[k - 1 : k + 2])
-        for p, (w, diagonal) in enumerate(plane(both(m2, at + k - 1), both(m2, at + k), both(m2, at + k + 1))):
-            v = values[k][p]
-            r = b2[at + k, p] - diagonal * v + weighted(w, around[p])
-            v2f[k - 1, p] = v + OMEGA * r / diagonal
+        mn = both(m2, at + k + 1)
+        w, face = level2_plane(consts, face, mc, mn)
+        n = level2_around(*values[k - 1 : k + 2])
+        for p in range(2):
+            gain = b2[at + k, p] + weighted(w[p], n[p])
+            v2f[k - 1, p] = (1.0 - OMEGA) * values[k][p] + d2[at + k, p] * gain
+        mc = mn
 
     low, high = jnp.maximum(g - 1, 0), jnp.minimum(g + 1, N_GZ - 1)
     for j in range(A2):
@@ -529,7 +596,7 @@
     n = level1_around(
         v1, prev + e1[96:100], nxt + e1[104:108], below + e1[64:80], above + e1[80:96], buf
     )
-    v1_out[...] = v1 + OMEGA * (b1_ref[...] - diagonal * v1 + weighted(w, n)) / diagonal
+    v1_out[...] = (1.0 - OMEGA) * v1 + OMEGA * (b1_ref[...] + weighted(w, n)) / diagonal
     store_faces1(v1_out, sx, sc, sz, sy)
 
 
@@ -558,7 +625,7 @@
         return old(i) + e_ref[i // 2]
 
     def emit(i, diagonal, around, centre):
-        out_ref[i] = centre + OMEGA * (rhs_ref[i] - diagonal * centre + around) / diagonal
+        out_ref[i] = (1.0 - OMEGA) * centre + OMEGA * (rhs_ref[i] + around) / diagonal
 
     fine_walk(
         m_of,
@@ -572,15 +639,29 @@
     store_faces(out_ref, sx, sc, sz, sy)
 
 
-def final(rhs_ref, v_ref, m_ref, ax, ac, az, ay, gx, gc, gz, gy, out_ref):
+def final(rhs_ref, v_ref, m_ref, ax, ac, az, ay, gx, gc, gz, gy, p_hbm, out_hbm, out_ref, sems):
+    part = NA // 4
+    copies = [
+        pltpu.make_async_copy(
+            src.at[pl.ds(k * part, part)], dst.at[pl.ds(k * part, part)], sems.at[4 * n + k]
+        )
+        for n, (src, dst) in enumerate(((v_ref, p_hbm), (out_ref, out_hbm)))
+        for k in range(4)
+    ]
+    for copy in copies[:4]:
+        copy.start()
     ah, gh = Halo(ax, ac, az, ay), Halo(gx, gc, gz, gy)
     m_of, mb, ma = fine_mobility(m_ref, ah)
     v_of, vb, va = fine_values(v_ref, gh)
 
     def emit(i, diagonal, around, centre):
         out_ref[i] = (rhs_ref[i] - diagonal * centre + around) / diagonal
+        if i % part == part - 1:
+            copies[4 + i // part].start()
 
     fine_walk(m_of, v_of, mb, ma, vb, va, emit)
+    for copy in copies:
+        copy.wait()
 
 
 def swap(x, axis, odd):
@@ -619,14 +700,30 @@
     pairs = vmem(A1 * NH, NR)
     buf = vmem(A1 * H1 + 16, R1)
 
-    m0, m1, m2, *send = call(
+    spread = struct(64, A2 * H2, R2)
+    m0, m1, m2, cell, *send = call(
         prepare,
-        [block, flat1, struct(A2 * H2, R2)] + faces(3 * NH, 2 * NA + A1, NR),
-        (pressure, void_fraction, volume, bubble_count),
-        [pairs],
-        smem=(3,),
+        [block, flat1, spread, jax.ShapeDtypeStruct((1, SLOTS), jnp.int32)]
+        + faces(3 * NH, 2 * NA + A1, NR),
+        (pressure, void_fraction, volume, cell, bubble_count),
+        [
+            vmem(NA, NH, NR),
+            vmem(NA, NH, NR),
+            vmem(1, SLOTS),
+            pairs,
+            pltpu.SemaphoreType.DMA((10,)),
+        ],
+        smem=(4,),
+        hbm=(0, 1, 2, 3),
     )
     ha = exchange(*send)
+    ring = (AZ2 + 4, 2, G2, R2)
+    m2, d2, w3 = call(
+        coarse_weights,
+        [struct(*ring), struct(*ring), struct(7, HALF, G2, R2)],
+        gathered(m2),
+        [vmem(AZ3, G2, R2), vmem(HALF + 2, G2, R2)],
+    )
     rhs, v0, *send = call(
         presmooth, [block, block] + faces(NH, NA, NR), (pressure, divergence, m0, cell, *ha)
     )
@@ -635,26 +732,18 @@
         restrict, [flat1, flat1] + faces(H1, A1, R1), (rhs, v0, m0, m1, *ha, *hb), [pairs, buf]
     )
     hc = exchange(*send)
-    (copies,) = call(
-        restrict1, [struct(64, 2 * A2 * H2, R2)], (b1, v1, m1, m2, *ha, *hc), [buf]
-    )
-    own, oth = gathered(copies)
-    ring = vmem(AZ2 + 4, 2, G2, R2)
-    half = AZ3 // 2
+    (copies,) = call(restrict1, [spread], (b1, v1, m1, *ha, *hc), [buf])
     v1, *send = call(
         coarse,
         [flat1] + faces(H1, A1, R1),
-        (own, oth, b1, v1, m1, *ha, *hc),
+        (*gathered(copies), m2, d2, w3, b1, v1, m1, *ha, *hc),
         [
-            ring,
-            ring,
-            ring,
+            vmem(*ring),
+            vmem(*ring),
             vmem(AZ3, G2, R2),
-            vmem(AZ3, G2, R2),
-            vmem(half + 2, G2, R2),
-            vmem(7, half, G2, R2),
-            vmem(half + 2, G2, R2),
-            vmem(half + 2, G2, R2),
+            vmem(HALF, G2, R2),
+            vmem(HALF + 2, G2, R2),
+            vmem(HALF + 2, G2, R2),
             vmem(AZ3, G2, R2),
             vmem(A2 + 2, 2, G2, R2),
             vmem(40, R2),
@@ -669,8 +758,15 @@
         [vmem(A1, NH, NR), vmem(2 * A1 + 2 * NH, NR)],
     )
     hg = exchange(*send)
-    (scaled,) = call(final, [block], (rhs, out, m0, *ha, *hg))
-    return out, scaled
+    return tuple(
+        call(
+            final,
+            [block, block],
+            (rhs, out, m0, *ha, *hg),
+            [vmem(NA, NH, NR), pltpu.SemaphoreType.DMA((8,))],
+            hbm_out=(0, 1),
+        )
+    )
 
 
 def solution(mesh):

time: 113 us -> 115 us (1.018)
  blocking collectives: 25.1 us -> 0 us
  starting transfers between devices: 31.1 us -> 49.3 us
  waiting for transfers between devices: 21.7 us -> 35.7 us
  Pallas kernels: 29.1 us -> 23.9 us
    all_to_all x1 -> x0, blocking collectives: 25.1 us -> none  [gathered(): lax.all_to_all(x, ('az', 'gz'), 0, 0, tiled=True, axis_index_groups=groups)]
    all_to_all x0 -> x2, starting transfers between devices: none -> 17.3 us  [gathered(): lax.all_to_all(x, ('az', 'gz'), 0, 0, tiled=True, axis_index_groups=groups)]
    all_to_all x0 -> x2, waiting for transfers between devices: none -> 12.5 us  [gathered(): lax.all_to_all(x, ('az', 'gz'), 0, 0, tiled=True, axis_index_groups=groups)]
    pallas_call x7 -> x8, Pallas kernels: 29.1 us -> 23.9 us  [call(): pl.pallas_call(kernel, out_shape=outs, in_specs=specs, out_specs=[pl.Bloc...]
    ppermute x21 -> x22, waiting for transfers between devices: 21.7 us -> 23.2 us  [swap(): return lax.ppermute(x, axis, pairs)]
    ppermute x21 -> x22, starting transfers between devices: 31.1 us -> 32 us  [swap(): return lax.ppermute(x, axis, pairs)]
  transfers between devices with their start and end apart: 21 -> 24, of which waited for: 6 -> 7; matrix products, arithmetic and copies ran while one was open for 0% -> 0% of each run, Pallas kernels for 0% -> 7%
where the time goes in v2:
time: 115 us
  starting transfers between devices  49.3 us (43%)
  waiting for transfers between devices  35.7 us (31%)
  Pallas kernels  23.9 us (21%)
  local copies, waits for them, and re-layouts  4.43 us (4%)
  between operations  1.56 us (1%)
    ppermute x22, starting transfers between devices, swap(): return lax.ppermute(x, axis, pairs)  32 us
    pallas_call x8, Pallas kernels, call(): pl.pallas_call(kernel, out_shape=outs, in_specs=specs, out_specs=[pl.Bloc...  23.9 us
    ppermute x22, waiting for transfers between devices, swap(): return lax.ppermute(x, axis, pairs)  23.2 us
    all_to_all x2, starting transfers between devices, gathered(): lax.all_to_all(x, ('az', 'gz'), 0, 0, tiled=True, axis_index_groups=groups)  17.3 us
    all_to_all x2, waiting for transfers between devices, gathered(): lax.all_to_all(x, ('az', 'gz'), 0, 0, tiled=True, axis_index_groups=groups)  12.5 us
    unnamed x12, local copies, waits for them, and re-layouts  4.43 us
  transfers between devices with their start and end apart: 24, of which 7 were waited for; matrix products, arithmetic and copies ran while one was open for 0% of the time, Pallas kernels for 7%

profile of v2, /device:TPU:0, one launch (start us, length us, event | category | flops | bytes accessed | tf_op | source)
XLA Modules:
  0.0 114.9 jit_solution(10341611573552396459)
XLA Ops:
  4.7 3.4 %shard_map.77 = (f32[32,8,512]{2,1,0:T(8,128)S(1)}, f32[64,256]{1,0:T(8,128)S(1)}, f32[64,16,128]{2,1,0:T(8,128)}, s32[1,128]{1,0:T(1,128)S(1)}, f32[24,512]{1,0...) custom-call(f32[32,8,512]{2,1,0:T(8,128)S(1)} %copy-done, ...), custom_call_target="tpu_custom_call" | custom-call | tf_op jit(solution)/shard_map/pallas_call | solution.py:34
  8.1 11.5 %all-to-all-start.1 = ((f32[64,16,128]{2,1,0:T(8,128)}), f32[64,16,128]{2,1,0:T(8,128)S(1)}, u32[]{:S(2)}, u32[]{:S(2)}) async-start(f32[64,16,128]{2,1,0:T(8,128)} %get-tuple-element.54), calls=%async_computation.1 | async-start | bytes 1048576 | tf_op jit(solution)/shard_map/all_to_all | solution.py:682
  19.6 1.6 %collective-permute-start.2 = (f32[80,512]{1,0:T(8,128)S(1)}, f32[80,512]{1,0:T(8,128)S(1)}, u32[]{:S(2)}, u32[]{:S(2)}) collective-permute-start(f32[80,512]{1,0:T(8,128)S(1)} %get-tuple-element.39), channel_id=1, source_target_pairs={{0,1},{1,0},{2,3},{3,2},{4,5},{5,4},{6,7},{7,6},{8,9},{9,8},{10,11... | collective-permute-start | bytes 491528 | tf_op jit(solution)/shard_map/ppermute | solution.py:673
  21.3 2.7 %collective-permute-start.3 = (f32[80,512]{1,0:T(8,128)S(1)}, f32[80,512]{1,0:T(8,128)S(1)}, u32[]{:S(2)}, u32[]{:S(2)}) collective-permute-start(f32[80,512]{1,0:T(8,128)S(1)} %get-tuple-element.40), channel_id=1, source_target_pairs={{0,7},{1,2},{2,1},{3,4},{4,3},{5,6},{6,5},{7,0},{8,15},{9,10},{10,... | collective-permute-start | bytes 491528 | tf_op jit(solution)/shard_map/ppermute | solution.py:673
  23.9 3.7 %collective-permute-start = (f32[24,512]{1,0:T(8,128)S(1)}, f32[24,512]{1,0:T(8,128)S(1)}, u32[]{:S(2)}, u32[]{:S(2)}) collective-permute-start(f32[24,512]{1,0:T(8,128)S(1)} %get-tuple-element.37), channel_id=1, source_target_pairs={{0,120},{8,16},{16,8},{24,32},{32,24},{40,48},{48,40},{56,64},{64,... | collective-permute-start | bytes 147464 | tf_op jit(solution)/shard_map/ppermute | solution.py:673
  27.6 4.6 %collective-permute-done.ax = f32[24,512]{1,0:T(8,128)S(1)} collective-permute-done((f32[24,512]{1,0:T(8,128)S(1)}, f32[24,512]{1,0:T(8,128)S(1)}, u32[]{:S(2)}, u32[]{:S(2)}) %collective-permute-start) | collective-permute-done | bytes 49184 | tf_op jit(solution)/shard_map/ppermute | solution.py:673
  32.3 2.6 %collective-permute-done.2.az = f32[80,512]{1,0:T(8,128)S(1)} collective-permute-done((f32[80,512]{1,0:T(8,128)S(1)}, f32[80,512]{1,0:T(8,128)S(1)}, u32[]{:S(2)}, u32[]{:S(2)}) %collective-permute-start.2) | collective-permute-done | bytes 163872 | tf_op jit(solution)/shard_map/ppermute | solution.py:673
  38.4 2.6 %collective-permute-start.7 = (f32[32,512]{1,0:T(8,128)S(1)}, f32[32,512]{1,0:T(8,128)S(1)}, u32[]{:S(2)}, u32[]{:S(2)}) collective-permute-start(f32[32,512]{1,0:T(8,128)S(1)} %get-tuple-element.47), channel_id=1, source_target_pairs={{0,7},{1,2},{2,1},{3,4},{4,3},{5,6},{6,5},{7,0},{8,15},{9,10},{10,... | collective-permute-start | bytes 196616 | tf_op jit(solution)/shard_map/ppermute | solution.py:673
  41.0 4.1 %collective-permute-start.4 = (f32[8,512]{1,0:T(8,128)S(1)}, f32[8,512]{1,0:T(8,128)S(1)}, u32[]{:S(2)}, u32[]{:S(2)}) collective-permute-start(f32[8,512]{1,0:T(8,128)S(1)} %get-tuple-element.44), channel_id=1, source_target_pairs={{0,120},{8,16},{16,8},{24,32},{32,24},{40,48},{48,40},{56,64},{64,... | collective-permute-start | bytes 49160 | tf_op jit(solution)/shard_map/ppermute | solution.py:673
  45.1 2.7 %collective-permute-done.4.bx = f32[8,512]{1,0:T(8,128)S(1)} collective-permute-done((f32[8,512]{1,0:T(8,128)S(1)}, f32[8,512]{1,0:T(8,128)S(1)}, u32[]{:S(2)}, u32[]{:S(2)}) %collective-permute-start.4) | collective-permute-done | bytes 16416 | tf_op jit(solution)/shard_map/ppermute | solution.py:673
  47.8 1.8 %shard_map.79 = (f32[64,256]{1,0:T(8,128)S(1)}, f32[64,256]{1,0:T(8,128)S(1)}, f32[4,256]{1,0:T(4,128)S(1)}, f32[4,256]{1,0:T(4,128)S(1)}, f32[16,256]{1,0:T(8,128)S(1)}, /*index=5*/f32[16,256]{1,0:T(8,128)S(1)}) custom-call(f32[32,8,512]{2,1,0:T(8,128)S(1)} %get-tuple-element.41.rhs_ref, f32[32,8,512]{2,1,0:T(8,128)S(1)} %get-tuple-element.42.v_ref, ...), custom_call_target="tpu_custom_call" | custom-call | tf_op jit(solution)/shard_map/pallas_call | solution.py:34
  49.6 2.5 %collective-permute-start.11 = (f32[16,256]{1,0:T(8,128)S(1)}, f32[16,256]{1,0:T(8,128)S(1)}, u32[]{:S(2)}, u32[]{:S(2)}) collective-permute-start(f32[16,256]{1,0:T(8,128)S(1)} %get-tuple-element.53), channel_id=1, source_target_pairs={{0,7},{1,2},{2,1},{3,4},{4,3},{5,6},{6,5},{7,0},{8,15},{9,10},{10,... | collective-permute-start | bytes 49160 | tf_op jit(solution)/shard_map/ppermute | solution.py:673
  52.1 3.1 %collective-permute-start.8 = (f32[4,256]{1,0:T(4,128)S(1)}, f32[4,256]{1,0:T(4,128)S(1)}, u32[]{:S(2)}, u32[]{:S(2)}) collective-permute-start(f32[4,256]{1,0:T(4,128)S(1)} %get-tuple-element.50), channel_id=1, source_target_pairs={{0,120},{8,16},{16,8},{24,32},{32,24},{40,48},{48,40},{56,64},{64,... | collective-permute-start | bytes 12296 | tf_op jit(solution)/shard_map/ppermute | solution.py:673
  55.2 3.5 %collective-permute-done.8.cx = f32[4,256]{1,0:T(4,128)S(1)} collective-permute-done((f32[4,256]{1,0:T(4,128)S(1)}, f32[4,256]{1,0:T(4,128)S(1)}, u32[]{:S(2)}, u32[]{:S(2)}) %collective-permute-start.8) | collective-permute-done | bytes 4128 | tf_op jit(solution)/shard_map/ppermute | solution.py:673
  60.3 5.7 %all-to-all-start = ((f32[64,16,128]{2,1,0:T(8,128)}), f32[64,16,128]{2,1,0:T(8,128)S(1)}, u32[]{:S(2)}, u32[]{:S(2)}) async-start(f32[64,16,128]{2,1,0:T(8,128)} %shard_map.80), calls=%async_computation | async-start | bytes 1048576 | tf_op jit(solution)/shard_map/all_to_all | solution.py:682
  66.9 12.5 %all-to-all-done = f32[64,16,128]{2,1,0:T(8,128)S(1)} async-done(((f32[64,16,128]{2,1,0:T(8,128)}), f32[64,16,128]{2,1,0:T(8,128)S(1)}, u32[]{:S(2)}, u32[]{:S(2)}) %all-to-all-start) | async-done | bytes 524320 | tf_op jit(solution)/shard_map/all_to_all | solution.py:682
  79.5 3.7 %shard_map.81 = (f32[132,2,8,128]{3,2,1,0:T(8,128)S(1)}, f32[132,2,8,128]{3,2,1,0:T(8,128)S(1)}, f32[7,32,8,128]{3,2,1,0:T(8,128)S(1)}) custom-call(f32[1024,128]{1,0:T(8,128)S(1)} %bitcast.7, f32[1024,128]{1,0:T(8,128)} %collective-permute-done.13.oth), custom_call_target="tpu_custom_call" | custom-call | tf_op jit(solution)/shard_map/pallas_call | solution.py:34
  83.2 8.2 %shard_map.82 = (f32[64,256]{1,0:T(8,128)S(1)}, f32[4,256]{1,0:T(4,128)S(1)}, f32[4,256]{1,0:T(4,128)S(1)}, f32[16,256]{1,0:T(8,128)S(1)}, f32[16,256]{1,0:T(8,128)S(1)}) custom-call(f32[1024,128]{1,0:T(8,128)S(1)} %bitcast.5, f32[1024,128]{1,0:T(8,128)S(1)} %collective-permute-done.12.oth, f32[132,2,8,128]{3,2,1,0:T(8,128)S(1)} %get-tuple-element.55.m2, ...), custom_call_target="tpu_custom_call" | custom-call | tf_op jit(solution)/shard_map/pallas_call | solution.py:34
  92.3 3.0 %collective-permute-start.17 = (f32[16,256]{1,0:T(8,128)S(1)}, f32[16,256]{1,0:T(8,128)S(1)}, u32[]{:S(2)}, u32[]{:S(2)}) collective-permute-start(f32[16,256]{1,0:T(8,128)S(1)} %get-tuple-element.62), channel_id=1, source_target_pairs={{0,7},{1,2},{2,1},{3,4},{4,3},{5,6},{6,5},{7,0},{8,15},{9,10},{10,... | collective-permute-start | bytes 49160 | tf_op jit(solution)/shard_map/ppermute | solution.py:673
  96.8 5.2 %collective-permute-done.14.fx = f32[4,256]{1,0:T(4,128)S(1)} collective-permute-done((f32[4,256]{1,0:T(4,128)S(1)}, f32[4,256]{1,0:T(4,128)S(1)}, u32[]{:S(2)}, u32[]{:S(2)}) %collective-permute-start.14) | collective-permute-done | bytes 4128 | tf_op jit(solution)/shard_map/ppermute | solution.py:673
  102.0 2.4 %shard_map.83 = (f32[32,8,512]{2,1,0:T(8,128)S(1)}, f32[8,512]{1,0:T(8,128)S(1)}, f32[8,512]{1,0:T(8,128)S(1)}, f32[32,512]{1,0:T(8,128)S(1)}, f32[32,512]{1,0:T(8,128)S(1)}) custom-call(f32[32,8,512]{2,1,0:T(8,128)S(1)} %get-tuple-element.41.rhs_ref, f32[32,8,512]{2,1,0:T(8,128)S(1)} %get-tuple-element.42.v_ref, f32[32,8,512]{2,1,0:T(8,128)S(1)} %get-tuple-element.35.m_ref, ...), custom_call_target="tpu_custom_call" | custom-call | tf_op jit(solution)/shard_map/pallas_call | solution.py:34
  104.5 1.8 %collective-permute-start.21 = (f32[32,512]{1,0:T(8,128)S(1)}, f32[32,512]{1,0:T(8,128)S(1)}, u32[]{:S(2)}, u32[]{:S(2)}) collective-permute-start(f32[32,512]{1,0:T(8,128)S(1)} %get-tuple-element.67), channel_id=1, source_target_pairs={{0,7},{1,2},{2,1},{3,4},{4,3},{5,6},{6,5},{7,0},{8,15},{9,10},{10,... | collective-permute-start | bytes 196616 | tf_op jit(solution)/shard_map/ppermute | solution.py:673
  106.3 2.2 %collective-permute-start.18 = (f32[8,512]{1,0:T(8,128)S(1)}, f32[8,512]{1,0:T(8,128)S(1)}, u32[]{:S(2)}, u32[]{:S(2)}) collective-permute-start(f32[8,512]{1,0:T(8,128)S(1)} %get-tuple-element.64), channel_id=1, source_target_pairs={{0,120},{8,16},{16,8},{24,32},{32,24},{40,48},{48,40},{56,64},{64,... | collective-permute-start | bytes 49160 | tf_op jit(solution)/shard_map/ppermute | solution.py:673
  108.5 4.6 %collective-permute-done.18.gx = f32[8,512]{1,0:T(8,128)S(1)} collective-permute-done((f32[8,512]{1,0:T(8,128)S(1)}, f32[8,512]{1,0:T(8,128)S(1)}, u32[]{:S(2)}, u32[]{:S(2)}) %collective-permute-start.18) | collective-permute-done | bytes 16416 | tf_op jit(solution)/shard_map/ppermute | solution.py:673
  (44 shorter events, 13.6 us)
Async XLA Ops:
  8.1 52.2 %all-to-all-start.1 = ((f32[64,16,128]{2,1,0:T(8,128)}), f32[64,16,128]{2,1,0:T(8,128)S(1)}, u32[]{:S(2)}, u32[]{:S(2)}) async-start(f32[64,16,128]{2,1,0:T(8,128)} %get-tuple-element.54), calls=%async_computation.1 | async-start | bytes 1048576 | tf_op jit(solution)/shard_map/all_to_all | solution.py:682
  19.6 15.2 %collective-permute-start.2 = (f32[80,512]{1,0:T(8,128)S(1)}, f32[80,512]{1,0:T(8,128)S(1)}, u32[]{:S(2)}, u32[]{:S(2)}) collective-permute-start(f32[80,512]{1,0:T(8,128)S(1)} %get-tuple-element.39), channel_id=1, source_target_pairs={{0,1},{1,0},{2,3},{3,2},{4,5},{5,4},{6,7},{7,6},{8,9},{9,8},{10,11... | collective-permute-start | bytes 491528 | tf_op jit(solution)/shard_map/ppermute | solution.py:673
  21.3 13.6 %collective-permute-start.3 = (f32[80,512]{1,0:T(8,128)S(1)}, f32[80,512]{1,0:T(8,128)S(1)}, u32[]{:S(2)}, u32[]{:S(2)}) collective-permute-start(f32[80,512]{1,0:T(8,128)S(1)} %get-tuple-element.40), channel_id=1, source_target_pairs={{0,7},{1,2},{2,1},{3,4},{4,3},{5,6},{6,5},{7,0},{8,15},{9,10},{10,... | collective-permute-start | bytes 491528 | tf_op jit(solution)/shard_map/ppermute | solution.py:673
  23.9 8.3 %collective-permute-start = (f32[24,512]{1,0:T(8,128)S(1)}, f32[24,512]{1,0:T(8,128)S(1)}, u32[]{:S(2)}, u32[]{:S(2)}) collective-permute-start(f32[24,512]{1,0:T(8,128)S(1)} %get-tuple-element.37), channel_id=1, source_target_pairs={{0,120},{8,16},{16,8},{24,32},{32,24},{40,48},{48,40},{56,64},{64,... | collective-permute-start | bytes 147464 | tf_op jit(solution)/shard_map/ppermute | solution.py:673
  27.6 4.6 %collective-permute-start.1 = (f32[24,512]{1,0:T(8,128)S(1)}, f32[24,512]{1,0:T(8,128)S(1)}, u32[]{:S(2)}, u32[]{:S(2)}) collective-permute-start(f32[24,512]{1,0:T(8,128)S(1)} %get-tuple-element.38), channel_id=1, source_target_pairs={{0,8},{8,0},{16,24},{24,16},{32,40},{40,32},{48,56},{56,48},{64,72... | collective-permute-start | bytes 147464 | tf_op jit(solution)/shard_map/ppermute | solution.py:673
  37.1 10.6 %collective-permute-start.6 = (f32[32,512]{1,0:T(8,128)S(1)}, f32[32,512]{1,0:T(8,128)S(1)}, u32[]{:S(2)}, u32[]{:S(2)}) collective-permute-start(f32[32,512]{1,0:T(8,128)S(1)} %get-tuple-element.46), channel_id=1, source_target_pairs={{0,1},{1,0},{2,3},{3,2},{4,5},{5,4},{6,7},{7,6},{8,9},{9,8},{10,11... | collective-permute-start | bytes 196616 | tf_op jit(solution)/shard_map/ppermute | solution.py:673
  38.4 9.4 %collective-permute-start.7 = (f32[32,512]{1,0:T(8,128)S(1)}, f32[32,512]{1,0:T(8,128)S(1)}, u32[]{:S(2)}, u32[]{:S(2)}) collective-permute-start(f32[32,512]{1,0:T(8,128)S(1)} %get-tuple-element.47), channel_id=1, source_target_pairs={{0,7},{1,2},{2,1},{3,4},{4,3},{5,6},{6,5},{7,0},{8,15},{9,10},{10,... | collective-permute-start | bytes 196616 | tf_op jit(solution)/shard_map/ppermute | solution.py:673
  41.0 6.8 %collective-permute-start.4 = (f32[8,512]{1,0:T(8,128)S(1)}, f32[8,512]{1,0:T(8,128)S(1)}, u32[]{:S(2)}, u32[]{:S(2)}) collective-permute-start(f32[8,512]{1,0:T(8,128)S(1)} %get-tuple-element.44), channel_id=1, source_target_pairs={{0,120},{8,16},{16,8},{24,32},{32,24},{40,48},{48,40},{56,64},{64,... | collective-permute-start | bytes 49160 | tf_op jit(solution)/shard_map/ppermute | solution.py:673
  45.1 2.7 %collective-permute-start.5 = (f32[8,512]{1,0:T(8,128)S(1)}, f32[8,512]{1,0:T(8,128)S(1)}, u32[]{:S(2)}, u32[]{:S(2)}) collective-permute-start(f32[8,512]{1,0:T(8,128)S(1)} %get-tuple-element.45), channel_id=1, source_target_pairs={{0,8},{8,0},{16,24},{24,16},{32,40},{40,32},{48,56},{56,48},{64,72... | collective-permute-start | bytes 49160 | tf_op jit(solution)/shard_map/ppermute | solution.py:673
  49.5 9.2 %collective-permute-start.10 = (f32[16,256]{1,0:T(8,128)S(1)}, f32[16,256]{1,0:T(8,128)S(1)}, u32[]{:S(2)}, u32[]{:S(2)}) collective-permute-start(f32[16,256]{1,0:T(8,128)S(1)} %get-tuple-element.52), channel_id=1, source_target_pairs={{0,1},{1,0},{2,3},{3,2},{4,5},{5,4},{6,7},{7,6},{8,9},{9,8},{10,11... | collective-permute-start | bytes 49160 | tf_op jit(solution)/shard_map/ppermute | solution.py:673
  49.6 9.1 %collective-permute-start.11 = (f32[16,256]{1,0:T(8,128)S(1)}, f32[16,256]{1,0:T(8,128)S(1)}, u32[]{:S(2)}, u32[]{:S(2)}) collective-permute-start(f32[16,256]{1,0:T(8,128)S(1)} %get-tuple-element.53), channel_id=1, source_target_pairs={{0,7},{1,2},{2,1},{3,4},{4,3},{5,6},{6,5},{7,0},{8,15},{9,10},{10,... | collective-permute-start | bytes 49160 | tf_op jit(solution)/shard_map/ppermute | solution.py:673
  52.1 6.6 %collective-permute-start.8 = (f32[4,256]{1,0:T(4,128)S(1)}, f32[4,256]{1,0:T(4,128)S(1)}, u32[]{:S(2)}, u32[]{:S(2)}) collective-permute-start(f32[4,256]{1,0:T(4,128)S(1)} %get-tuple-element.50), channel_id=1, source_target_pairs={{0,120},{8,16},{16,8},{24,32},{32,24},{40,48},{48,40},{56,64},{64,... | collective-permute-start | bytes 12296 | tf_op jit(solution)/shard_map/ppermute | solution.py:673
  55.2 3.5 %collective-permute-start.9 = (f32[4,256]{1,0:T(4,128)S(1)}, f32[4,256]{1,0:T(4,128)S(1)}, u32[]{:S(2)}, u32[]{:S(2)}) collective-permute-start(f32[4,256]{1,0:T(4,128)S(1)} %get-tuple-element.51), channel_id=1, source_target_pairs={{0,8},{8,0},{16,24},{24,16},{32,40},{40,32},{48,56},{56,48},{64,72... | collective-permute-start | bytes 12296 | tf_op jit(solution)/shard_map/ppermute | solution.py:673
  60.3 19.2 %all-to-all-start = ((f32[64,16,128]{2,1,0:T(8,128)}), f32[64,16,128]{2,1,0:T(8,128)S(1)}, u32[]{:S(2)}, u32[]{:S(2)}) async-start(f32[64,16,128]{2,1,0:T(8,128)} %shard_map.80), calls=%async_computation | async-start | bytes 1048576 | tf_op jit(solution)/shard_map/all_to_all | solution.py:682
  66.1 13.4 %collective-permute-start.13 = (f32[1024,128]{1,0:T(8,128)S(1)}, f32[1024,128]{1,0:T(8,128)}, u32[]{:S(2)}, u32[]{:S(2)}) collective-permute-start(f32[1024,128]{1,0:T(8,128)S(1)} %bitcast.6), channel_id=1, source_target_pairs={{0,8},{8,0},{16,24},{24,16},{32,40},{40,32},{48,56},{56,48},{64,72... | collective-permute-start | bytes 1572872 | tf_op jit(solution)/shard_map/ppermute | solution.py:673
  79.5 3.7 %collective-permute-start.12 = (f32[1024,128]{1,0:T(8,128)S(1)}, f32[1024,128]{1,0:T(8,128)S(1)}, u32[]{:S(2)}, u32[]{:S(2)}) collective-permute-start(f32[1024,128]{1,0:T(8,128)S(1)} %bitcast.4), channel_id=1, source_target_pairs={{0,8},{8,0},{16,24},{24,16},{32,40},{40,32},{48,56},{56,48},{64,72... | collective-permute-start | bytes 1572872 | tf_op jit(solution)/shard_map/ppermute | solution.py:673
  91.4 10.6 %collective-permute-start.16 = (f32[16,256]{1,0:T(8,128)S(1)}, f32[16,256]{1,0:T(8,128)S(1)}, u32[]{:S(2)}, u32[]{:S(2)}) collective-permute-start(f32[16,256]{1,0:T(8,128)S(1)} %get-tuple-element.61), channel_id=1, source_target_pairs={{0,1},{1,0},{2,3},{3,2},{4,5},{5,4},{6,7},{7,6},{8,9},{9,8},{10,11... | collective-permute-start | bytes 49160 | tf_op jit(solution)/shard_map/ppermute | solution.py:673
  92.3 9.7 %collective-permute-start.17 = (f32[16,256]{1,0:T(8,128)S(1)}, f32[16,256]{1,0:T(8,128)S(1)}, u32[]{:S(2)}, u32[]{:S(2)}) collective-permute-start(f32[16,256]{1,0:T(8,128)S(1)} %get-tuple-element.62), channel_id=1, source_target_pairs={{0,7},{1,2},{2,1},{3,4},{4,3},{5,6},{6,5},{7,0},{8,15},{9,10},{10,... | collective-permute-start | bytes 49160 | tf_op jit(solution)/shard_map/ppermute | solution.py:673
  95.3 6.6 %collective-permute-start.14 = (f32[4,256]{1,0:T(4,128)S(1)}, f32[4,256]{1,0:T(4,128)S(1)}, u32[]{:S(2)}, u32[]{:S(2)}) collective-permute-start(f32[4,256]{1,0:T(4,128)S(1)} %get-tuple-element.59), channel_id=1, source_target_pairs={{0,120},{8,16},{16,8},{24,32},{32,24},{40,48},{48,40},{56,64},{64,... | collective-permute-start | bytes 12296 | tf_op jit(solution)/shard_map/ppermute | solution.py:673
  96.8 5.2 %collective-permute-start.15 = (f32[4,256]{1,0:T(4,128)S(1)}, f32[4,256]{1,0:T(4,128)S(1)}, u32[]{:S(2)}, u32[]{:S(2)}) collective-permute-start(f32[4,256]{1,0:T(4,128)S(1)} %get-tuple-element.60), channel_id=1, source_target_pairs={{0,8},{8,0},{16,24},{24,16},{32,40},{40,32},{48,56},{56,48},{64,72... | collective-permute-start | bytes 12296 | tf_op jit(solution)/shard_map/ppermute | solution.py:673
  104.4 8.7 %collective-permute-start.20 = (f32[32,512]{1,0:T(8,128)S(1)}, f32[32,512]{1,0:T(8,128)S(1)}, u32[]{:S(2)}, u32[]{:S(2)}) collective-permute-start(f32[32,512]{1,0:T(8,128)S(1)} %get-tuple-element.66), channel_id=1, source_target_pairs={{0,1},{1,0},{2,3},{3,2},{4,5},{5,4},{6,7},{7,6},{8,9},{9,8},{10,11... | collective-permute-start | bytes 196616 | tf_op jit(solution)/shard_map/ppermute | solution.py:673
  104.5 8.6 %collective-permute-start.21 = (f32[32,512]{1,0:T(8,128)S(1)}, f32[32,512]{1,0:T(8,128)S(1)}, u32[]{:S(2)}, u32[]{:S(2)}) collective-permute-start(f32[32,512]{1,0:T(8,128)S(1)} %get-tuple-element.67), channel_id=1, source_target_pairs={{0,7},{1,2},{2,1},{3,4},{4,3},{5,6},{6,5},{7,0},{8,15},{9,10},{10,... | collective-permute-start | bytes 196616 | tf_op jit(solution)/shard_map/ppermute | solution.py:673
  106.3 6.8 %collective-permute-start.18 = (f32[8,512]{1,0:T(8,128)S(1)}, f32[8,512]{1,0:T(8,128)S(1)}, u32[]{:S(2)}, u32[]{:S(2)}) collective-permute-start(f32[8,512]{1,0:T(8,128)S(1)} %get-tuple-element.64), channel_id=1, source_target_pairs={{0,120},{8,16},{16,8},{24,32},{32,24},{40,48},{48,40},{56,64},{64,... | collective-permute-start | bytes 49160 | tf_op jit(solution)/shard_map/ppermute | solution.py:673
  108.4 4.6 %collective-permute-start.19 = (f32[8,512]{1,0:T(8,128)S(1)}, f32[8,512]{1,0:T(8,128)S(1)}, u32[]{:S(2)}, u32[]{:S(2)}) collective-permute-start(f32[8,512]{1,0:T(8,128)S(1)} %get-tuple-element.65), channel_id=1, source_target_pairs={{0,8},{8,0},{16,24},{24,16},{32,40},{40,32},{48,56},{56,48},{64,72... | collective-permute-start | bytes 49160 | tf_op jit(solution)/shard_map/ppermute | solution.py:673
  (6 other events, 34.6 us)

commit v3 on v2

--- a/solution.py
+++ b/solution.py
@@ -69,16 +69,15 @@
     return (iota((n, 2 * n), 0) == iota((n, 2 * n), 1) // 2).astype(F32)
 
 
-def pair_rows_h(rows):
-    return (iota((rows // 2, rows), 1) // 2 == iota((rows // 2, rows), 0)).astype(F32)
-
-
-def block_rows(az, ht):
-    out = (az // 2) * (ht // 2)
-    r = iota((out, az * ht), 1)
-    o = iota((out, az * ht), 0)
-    target = (r // (2 * ht)) * (ht // 2) + (r % ht) // 2
-    return (target == o).astype(F32)
+def row_sums(planes, out, first, per):
+    o, r = iota((planes * out, planes * per), 0), iota((planes * out, planes * per), 1)
+    h = r % per - first
+    return ((o // out == r // per) & (h >= 0) & (h // 2 == o % out)).astype(F32)
+
+
+def widened(planes):
+    o, r = iota((planes * 8, planes * 8), 0), iota((planes * 8, planes * 8), 1)
+    return ((o // 8 == r // 8) & (o % 8 == (r % 8) // 2 + 2)).astype(F32)
 
 
 def position():
@@ -136,33 +135,48 @@
         mp, mc, vp, vc, wa = mc, mn, vc, vn, wan
 
 
-def level1_weights(m, prev, nxt, below, above, buf):
+T1 = 8
+
+
+def level1_walk(m_of, v_of, first, count, emit):
     a, g = position()
-    rows = A1 * H1
-    sub = iota((rows, R1), 0)
-    lane = iota((rows, R1), 1)
-    ht = sub % H1
-    ca, ri, ro = radial_consts((rows, R1), R1, 2.0 * math.pi / (A1 * N_AZ), lane)
-    zlo = jnp.where((ht == 0) & (g == 0), 0.0, 0.5)
-    zhi = jnp.where((ht == H1 - 1) & (g == N_GZ - 1), 0.0, 0.5)
-    mp, mn, ml, mh, mi, mo = level1_around(m, prev, nxt, below, above, buf)
-    w = (ca * (m + mp), ca * (m + mn), zlo * (m + ml), zhi * (m + mh), ri * (m + mi), ro * (m + mo))
-    diagonal = (w[0] + w[1]) + (w[2] + w[3]) + (w[4] + w[5]) + SIGMA * 4.0
-    return w, diagonal
-
-
-def level1_around(x, prev, nxt, below, above, buf):
-    rows = A1 * H1
-    ht = iota((rows, R1), 0) % H1
-    spread = (iota((rows, A1), 0) // H1 == iota((rows, A1), 1)).astype(F32)
-    buf[8 : 8 + rows, :] = x
-    buf[8 - H1 : 8, :] = prev
-    buf[8 + rows : 8 + rows + H1, :] = nxt
-    xp = buf[8 - H1 : 8 - H1 + rows, :]
-    xn = buf[8 + H1 : 8 + H1 + rows, :]
-    xl = jnp.where(ht == 0, dot(spread, below), pltpu.roll(x, 1, 0))
-    xh = jnp.where(ht == H1 - 1, dot(spread, above), pltpu.roll(x, rows - 1, 0))
-    return xp, xn, xl, xh, pltpu.roll(x, 1, 1), pltpu.roll(x, R1 - 1, 1)
+    sub = iota((T1, R1), 0)
+    lane = iota((T1, R1), 1)
+    height = g * H1 + sub - 2
+    ca, ri, ro = radial_consts((T1, R1), R1, 2.0 * math.pi / (A1 * N_AZ), lane)
+    zlo = jnp.where(height <= 0, 0.0, 0.5)
+    zhi = jnp.where(height >= H1 * N_GZ - 1, 0.0, 0.5)
+    mp, mc = m_of(first - 1), m_of(first)
+    if v_of is not None:
+        vp, vc = v_of(first - 1), v_of(first)
+    wa = ca * (mp + mc)
+    for i in range(first, first + count):
+        mn = m_of(i + 1)
+        wan = ca * (mc + mn)
+        w = (
+            wa,
+            wan,
+            zlo * (mc + pltpu.roll(mc, 1, 0)),
+            zhi * (mc + pltpu.roll(mc, T1 - 1, 0)),
+            ri * (mc + pltpu.roll(mc, 1, 1)),
+            ro * (mc + pltpu.roll(mc, R1 - 1, 1)),
+        )
+        diagonal = total_weight(w) + SIGMA * 4.0
+        if v_of is None:
+            emit(i, diagonal, None, None)
+        else:
+            vn = v_of(i + 1)
+            n = (
+                vp,
+                vn,
+                pltpu.roll(vc, 1, 0),
+                pltpu.roll(vc, T1 - 1, 0),
+                pltpu.roll(vc, 1, 1),
+                pltpu.roll(vc, R1 - 1, 1),
+            )
+            emit(i, diagonal, weighted(w, n), vc)
+            vp, vc = vc, vn
+        mp, mc, wa = mc, mn, wan
 
 
 def weighted(w, n):
@@ -186,62 +200,39 @@
         y_ref[rows_at + i : rows_at + i + 1, :] = ref[i, pl.ds(y_row, 1), :]
 
 
-def store_faces1(ref, x_ref, c_ref, z_ref, y_ref, planes_at=0, rows_at=0):
+def prepare(
+    p_ref, void_ref, vol_ref, cnt_ref, m0_ref, m1_ref, m2_ref, sx, sc, sz, sy, pairs, halves
+):
     a, g = position()
     pa, pg = a % 2, g % 2
-    rows = A1 * H1
-    lo, hi = ref[0:H1, :], ref[rows - H1 : rows, :]
-    c_ref[planes_at : planes_at + H1, 0:R1] = pick(pa, hi, lo)
-    x_ref[planes_at : planes_at + H1, 0:R1] = pick(pa, lo, hi)
-    for i in range(A1):
-        low, high = ref[H1 * i : H1 * i + 1, :], ref[H1 * i + H1 - 1 : H1 * i + H1, :]
-        z_ref[rows_at + i : rows_at + i + 1, 0:R1] = pick(pg, high, low)
-        y_ref[rows_at + i : rows_at + i + 1, 0:R1] = pick(pg, low, high)
-
-
-def prepare(
-    p_hbm, void_hbm, vol_hbm, cell_hbm, cnt_ref,
-    m0_ref, m1_ref, m2_ref, cell_ref, sx, sc, sz, sy,
-    p_ref, void_ref, vol_ref, pairs, sems,
-):
-    part = NA // 4
-    copies = [
-        pltpu.make_async_copy(
-            src.at[pl.ds(k * part, part)], dst.at[pl.ds(k * part, part)], sems.at[4 * n + k]
-        )
-        for n, (src, dst) in enumerate(((void_hbm, void_ref), (p_hbm, p_ref)))
-        for k in range(4)
-    ]
-    copies.append(pltpu.make_async_copy(vol_hbm, vol_ref, sems.at[8]))
-    copies.append(pltpu.make_async_copy(cell_hbm, cell_ref, sems.at[9]))
-    for copy in copies:
-        copy.start()
-    zero = jnp.zeros((NH, NR), F32)
-    sx[2 * NH : 3 * NH, :] = zero
-    sc[2 * NH : 3 * NH, :] = zero
-    for ref in (sz, sy):
-        ref[2 * NA : 2 * NA + A1, R1:NR] = jnp.zeros((A1, NR - R1), F32)
     for i in range(0, NA, 2):
-        if i % part == 0:
-            copies[i // part].wait()
         u = 1.0 / (1.0 - void_ref[i])
         v = 1.0 / (1.0 - void_ref[i + 1])
         m0_ref[i] = u
         m0_ref[i + 1] = v
         pairs[(i // 2) * NH : (i // 2 + 1) * NH, :] = u + v
-    m1 = 0.125 * dot(pair_rows_h(A1 * NH), dot(pairs[...], pair_cols(NR)))
-    m1_ref[...] = m1
-    m2 = 0.125 * dot(block_rows(A1, H1), dot(m1, pair_cols(R1)))
-    for k in range(m2_ref.shape[0]):
-        m2_ref[k] = m2
-    for copy in copies[4:]:
-        copy.wait()
+    m1_ref[...] = 0.125 * dot(widened(A1), dot(pairs[...], pair_cols(NR))).reshape(A1, T1, R1)
+    for i in range(A2):
+        halves[i * T1 : (i + 1) * T1, :] = m1_ref[2 * i] + m1_ref[2 * i + 1]
+    m2_ref[...] = 0.125 * dot(row_sums(A2, H2, 2, T1), dot(halves[...], pair_cols(R1)))
     store_faces(p_ref, sx, sc, sz, sy, 0, 0)
     store_faces(m0_ref, sx, sc, sz, sy, NH, NA)
-    store_faces1(m1_ref, sx, sc, sz, sy, 2 * NH, 2 * NA)
+    rest = slice(2 * NH, 3 * NH)
+    sx[rest, R1:NR] = jnp.zeros((NH, NR - R1), F32)
+    sc[rest, R1:NR] = jnp.zeros((NH, NR - R1), F32)
+    c_plane = jnp.where(pa == 0, A1 - 1, 0)
+    sc[rest, 0:R1] = m1_ref[c_plane]
+    sx[rest, 0:R1] = m1_ref[A1 - 1 - c_plane]
+    for ref in (sz, sy):
+        ref[2 * NA : 2 * NA + A1, R1:NR] = jnp.zeros((A1, NR - R1), F32)
+    z_row = jnp.where(pg == 0, H1 + 1, 2)
+    for i in range(A1):
+        at = slice(2 * NA + i, 2 * NA + i + 1)
+        sz[at, 0:R1] = m1_ref[i, pl.ds(z_row, 1), :]
+        sy[at, 0:R1] = m1_ref[i, pl.ds(H1 + 3 - z_row, 1), :]
     live = jnp.where(iota((1, SLOTS), 1) < cnt_ref[0], vol_ref[...], 0.0)
-    sx[2 * NH + H1 : 2 * NH + H1 + 1, 0:SLOTS] = live
-    sc[2 * NH + H1 : 2 * NH + H1 + 1, 0:SLOTS] = live
+    for ref in (sx, sc):
+        ref[2 * NH : 2 * NH + 1, R1 : R1 + SLOTS] = live
 
 
 def fine_mobility(m_ref, ah):
@@ -276,7 +267,7 @@
 
 def presmooth(p_ref, div_ref, m_ref, cell_ref, ax, ac, az, ay, rhs_ref, v_ref, sx, sc, sz, sy):
     ah = Halo(ax, ac, az, ay)
-    arrived = ah.prev(slice(2 * NH + H1, 2 * NH + H1 + 1), slice(0, SLOTS))
+    arrived = ah.prev(slice(2 * NH, 2 * NH + 1), slice(R1, R1 + SLOTS))
     cell = cell_ref[...]
     plane_hot = (iota((NA * NH, SLOTS), 0) == lax.shift_right_logical(cell, 9)).astype(F32)
     radius_hot = jnp.where(iota((NR, SLOTS), 0) == (cell & (NR - 1)), arrived, 0.0)
@@ -298,18 +289,8 @@
     store_faces(v_ref, sx, sc, sz, sy)
 
 
-def mobility1(m1_ref, ah):
-    return (
-        m1_ref[...],
-        ah.prev(slice(2 * NH, 2 * NH + H1), slice(0, R1)),
-        ah.next(slice(2 * NH, 2 * NH + H1), slice(0, R1)),
-        ah.below(slice(2 * NA, 2 * NA + A1), slice(0, R1)),
-        ah.above(slice(2 * NA, 2 * NA + A1), slice(0, R1)),
-    )
-
-
 def restrict(
-    rhs_ref, v_ref, m_ref, m1_ref, ax, ac, az, ay, bx, bc, bz, by, b1_ref, v1_ref, sx, sc, sz, sy, pairs, buf
+    rhs_ref, v_ref, m_ref, m1_ref, ax, ac, az, ay, bx, bc, bz, by, b1_ref, v1_ref, sz, sy, pairs
 ):
     ah, bh = Halo(ax, ac, az, ay), Halo(bx, bc, bz, by)
     m_of, mb, ma = fine_mobility(m_ref, ah)
@@ -324,30 +305,87 @@
             pairs[(i // 2) * NH : (i // 2 + 1) * NH, :] = kept.pop() + r
 
     fine_walk(m_of, v_of, mb, ma, vb, va, emit)
-    b1 = 0.5 * dot(pair_rows_h(A1 * NH), dot(pairs[...], pair_cols(NR)))
-    b1_ref[...] = b1
-    _, diagonal = level1_weights(*mobility1(m1_ref, ah), buf)
-    v1_ref[...] = OMEGA * b1 / diagonal
-    store_faces1(v1_ref, sx, sc, sz, sy)
-
-
-def halo1(h):
-    return (
-        h.prev(slice(0, H1), ALL),
-        h.next(slice(0, H1), ALL),
-        h.below(slice(0, A1), ALL),
-        h.above(slice(0, A1), ALL),
-    )
-
-
-def restrict1(b1_ref, v1_ref, m1_ref, ax, ac, az, ay, cx, cc, cz, cy, out_ref, buf):
-    ah, ch = Halo(ax, ac, az, ay), Halo(cx, cc, cz, cy)
-    w, _ = level1_weights(*mobility1(m1_ref, ah), buf)
-    n = level1_around(v1_ref[...], *halo1(ch), buf)
-    r1 = (1.0 - OMEGA) * b1_ref[...] + weighted(w, n)
-    b2 = 0.5 * dot(block_rows(A1, H1), dot(r1, pair_cols(R1)))
+    b1_ref[...] = 0.5 * dot(widened(A1), dot(pairs[...], pair_cols(NR))).reshape(A1, T1, R1)
+
+    sub = iota((T1, R1), 0)
+
+    def m1_of(i):
+        if i < 0:
+            return ah.prev(slice(2 * NH, 3 * NH), slice(0, R1))
+        if i >= A1:
+            return ah.next(slice(2 * NH, 3 * NH), slice(0, R1))
+        at = slice(2 * NA + i, 2 * NA + i + 1)
+        below, above = ah.below(at, slice(0, R1)), ah.above(at, slice(0, R1))
+        return jnp.where(sub == 1, below, jnp.where(sub == H1 + 2, above, m1_ref[i]))
+
+    def emit1(i, diagonal, around, centre):
+        v1_ref[i] = OMEGA * b1_ref[i] / diagonal
+
+    level1_walk(m1_of, None, 0, A1, emit1)
+    g = lax.axis_index("gz")
+    for layer in range(2):
+        z_row = jnp.where(g % 2 == 0, H1 + 1 - layer, 2 + layer)
+        y_row = H1 + 3 - z_row
+        sources = (v1_ref, m1_ref) if layer else (v1_ref, m1_ref, b1_ref)
+        for n, ref in enumerate(sources):
+            for i in range(A1):
+                at = (2 * n + layer) * A1 + i
+                sz[at : at + 1, :] = ref[i, pl.ds(z_row, 1), :]
+                sy[at : at + 1, :] = ref[i, pl.ds(y_row, 1), :]
+
+
+def widen(b1_ref, v1_ref, m1_ref, z_ref, y_ref, vw, mw, bw, sx, sc):
+    a, g = position()
+    sub = iota((T1, R1), 0)
+    halo = Halo(None, None, z_ref, y_ref)
+    for n, (src, dst) in enumerate(((v1_ref, vw), (m1_ref, mw), (b1_ref, bw))):
+        for i in range(A1):
+            tile = src[i]
+            for layer in range(2 if n < 2 else 1):
+                at = (2 * n + layer) * A1 + i
+                at = slice(at, at + 1)
+                tile = jnp.where(sub == 1 - layer, halo.below(at, ALL), tile)
+                tile = jnp.where(sub == H1 + 2 + layer, halo.above(at, ALL), tile)
+            dst[i] = tile
+    for layer in range(2):
+        c_plane = jnp.where(a % 2 == 0, A1 - 1 - layer, layer)
+        x_plane = A1 - 1 - c_plane
+        for n, ref in enumerate((vw, mw) if layer else (vw, mw, bw)):
+            at = (2 * n + layer) * T1
+            sc[at : at + T1, :] = ref[c_plane]
+            sx[at : at + T1, :] = ref[x_plane]
+
+
+def wide_planes(ref, halo, n, i):
+    if i < 0:
+        at = (2 * n - 1 - i) * T1
+        return halo.prev(slice(at, at + T1), ALL)
+    if i >= A1:
+        at = (2 * n + i - A1) * T1
+        return halo.next(slice(at, at + T1), ALL)
+    return ref[i]
+
+
+def restrict1(bw, vw, mw, m2_ref, cx, cc, out_ref, halves):
+    halo = Halo(cx, cc, None, None)
+    kept = []
+
+    def emit(i, diagonal, around, centre):
+        r = (1.0 - OMEGA) * bw[i] + around
+        if i % 2 == 0:
+            kept.append(r)
+        else:
+            halves[(i // 2) * T1 : (i // 2 + 1) * T1, :] = kept.pop() + r
+
+    level1_walk(
+        lambda i: wide_planes(mw, halo, 1, i), lambda i: wide_planes(vw, halo, 0, i), 0, A1, emit
+    )
+    b2 = 0.5 * dot(row_sums(A2, H2, 2, T1), dot(halves[...], pair_cols(R1)))
+    m2 = m2_ref[...]
+    rows = A2 * H2
     for k in range(out_ref.shape[0]):
-        out_ref[k] = b2
+        out_ref[k, 0:rows, :] = b2
+        out_ref[k, rows : 2 * rows, :] = m2
 
 
 def level2_plane(consts, face, mc, mn):
@@ -425,11 +463,11 @@
     pa = a % 2
     rows = A2 * H2
     for k in range(N_AZ):
-        base = (k // 2) * N_GZ * rows
+        base = (k // 2) * N_GZ * 2 * rows + rows
         first, second = (own, oth) if k % 2 == 0 else (oth, own)
         for i in range(A2):
             for p in range(2):
-                at = pl.ds(base + i * 2 + p, G2, stride=rows)
+                at = pl.ds(base + i * 2 + p, G2, stride=2 * rows)
                 m2[k * A2 + i + 2, p] = pick(pa, first[at, :], second[at, :])
     close_ring(m2)
     consts = level2_consts()
@@ -474,20 +512,21 @@
 
 
 def coarse(
-    own, oth, m2, d2, w3, b1_ref, v1_ref, m1_ref, ax, ac, az, ay, cx, cc, cz, cy,
-    v1_out, sx, sc, sz, sy,
-    b2, v2, sum_r, add, va, vb, e2, v2f, src, buf,
+    own, oth, bw, vw, mw, cx, cc, rhs_ref, v_ref, m_ref, ax, ac, az, ay, bx, bc, bz, by,
+    out_ref, sx, sc, sz, sy,
+    m2, d2, w3, sum_m, m3, b2, v2, sum_r, add, va, vb, e2, v2f, src, v1f, e_ref,
 ):
+    coarse_weights(own, oth, m2, d2, w3, sum_m, m3)
     a, g = position()
     pa = a % 2
     rows = A2 * H2
 
     for k in range(N_AZ):
-        base = (k // 2) * N_GZ * rows
+        base = (k // 2) * N_GZ * 2 * rows
         first, second = (own, oth) if k % 2 == 0 else (oth, own)
         for i in range(A2):
             for p in range(2):
-                at = pl.ds(base + i * 2 + p, G2, stride=rows)
+                at = pl.ds(base + i * 2 + p, G2, stride=2 * rows)
                 b = pick(pa, first[at, :], second[at, :])
                 b2[k * A2 + i + 2, p] = b
                 v2[k * A2 + i + 2, p] = b * d2[k * A2 + i + 2, p]
@@ -568,73 +607,50 @@
         mc = mn
 
     low, high = jnp.maximum(g - 1, 0), jnp.minimum(g + 1, N_GZ - 1)
-    for j in range(A2):
-        src[2 * j : 2 * j + 1, :] = v2f[j + 1, 0, pl.ds(g, 1), :]
-        src[2 * j + 1 : 2 * j + 2, :] = v2f[j + 1, 1, pl.ds(g, 1), :]
-        src[16 + j : 17 + j, :] = v2f[j + 1, 1, pl.ds(low, 1), :]
-        src[24 + j : 25 + j, :] = v2f[j + 1, 0, pl.ds(high, 1), :]
-    for p in range(2):
-        src[32 + p : 33 + p, :] = v2f[0, p, pl.ds(g, 1), :]
-        src[34 + p : 35 + p, :] = v2f[A2 + 1, p, pl.ds(g, 1), :]
-    src[36:40, :] = jnp.zeros((4, R2), F32)
-    o, c = iota((112, 40), 0), iota((112, 40), 1)
-    target = jnp.where(
-        o < 64,
-        (o // 8) * 2 + (o % 4) // 2,
-        jnp.where(
-            o < 96,
-            16 + (o - 64) // 2,
-            jnp.where(o < 100, 32 + (o - 96) // 2, 34 + (o - 104) // 2),
-        ),
-    )
-    e1 = dot((target == c).astype(F32), dot(src[...], dup_cols(R2)))
-
-    ah, ch = Halo(ax, ac, az, ay), Halo(cx, cc, cz, cy)
-    w, diagonal = level1_weights(*mobility1(m1_ref, ah), buf)
-    prev, nxt, below, above = halo1(ch)
-    v1 = v1_ref[...] + e1[0:64]
-    n = level1_around(
-        v1, prev + e1[96:100], nxt + e1[104:108], below + e1[64:80], above + e1[80:96], buf
-    )
-    v1_out[...] = (1.0 - OMEGA) * v1 + OMEGA * (b1_ref[...] + weighted(w, n)) / diagonal
-    store_faces1(v1_out, sx, sc, sz, sy)
-
-
-def postsmooth(
-    rhs_ref, v_ref, m_ref, v1_ref, ax, ac, az, ay, bx, bc, bz, by, fx, fc, fz, fy, out_ref, sx, sc, sz, sy, e_ref, er
-):
-    ah, bh, fh = Halo(ax, ac, az, ay), Halo(bx, bc, bz, by), Halo(fx, fc, fz, fy)
-    dup = dup_cols(R1)
-    rows = A1 * NH
-    tall = (iota((rows, A1 * H1), 0) // 2 == iota((rows, A1 * H1), 1)).astype(F32)
-    e_ref[...] = dot(tall, dot(v1_ref[...], dup)).reshape(A1, NH, NR)
-    prev, nxt, below, above = halo1(fh)
-    er[0:A1, :] = dot(below, dup)
-    er[A1 : 2 * A1, :] = dot(above, dup)
-    tall = (iota((NH, H1), 0) // 2 == iota((NH, H1), 1)).astype(F32)
-    er[2 * A1 : 2 * A1 + NH, :] = dot(tall, dot(prev, dup))
-    er[2 * A1 + NH : 2 * A1 + 2 * NH, :] = dot(tall, dot(nxt, dup))
+    for j in range(A2 + 2):
+        for q, (p, row) in enumerate(((1, low), (0, g), (1, g), (0, high))):
+            src[4 * j + q : 4 * j + q + 1, :] = v2f[j, p, pl.ds(row, 1), :]
+    o, c = iota((8 * (A2 + 2), 4 * (A2 + 2)), 0), iota((8 * (A2 + 2), 4 * (A2 + 2)), 1)
+    e1 = dot((o // 2 == c).astype(F32), dot(src[...], dup_cols(R2)))
+    halo = Halo(cx, cc, None, None)
+
+    def v1_of(i):
+        j = (i + 2) // 2
+        return wide_planes(vw, halo, 0, i) + e1[T1 * j : T1 * (j + 1)]
+
+    def emit1(i, diagonal, around, centre):
+        b = wide_planes(bw, halo, 2, i)
+        at = (i + 1) * T1
+        v1f[at : at + T1, :] = (1.0 - OMEGA) * centre + OMEGA * (b + around) / diagonal
+
+    level1_walk(lambda i: wide_planes(mw, halo, 1, i), v1_of, -1, A1 + 2, emit1)
+
+    own_rows = (A1 + 2) * NH
+    shape = (own_rows + 2 * A1, (A1 + 2) * T1)
+    o, c = iota(shape, 0), iota(shape, 1)
+    j = jnp.where(o < own_rows, o // NH, (o - own_rows) % A1 + 1)
+    h = jnp.where(o < own_rows, (o % NH) // 2 + 2, jnp.where(o < own_rows + A1, 1, H1 + 2))
+    e_ref[...] = dot(dot((c == j * T1 + h).astype(F32), v1f[...]), dup_cols(R1))
+    ah, bh = Halo(ax, ac, az, ay), Halo(bx, bc, bz, by)
     m_of, mb, ma = fine_mobility(m_ref, ah)
     old, ob, oa = fine_values(v_ref, bh)
 
     def v_of(i):
-        if i < 0:
-            return old(i) + er[2 * A1 : 2 * A1 + NH, :]
-        if i >= NA:
-            return old(i) + er[2 * A1 + NH : 2 * A1 + 2 * NH, :]
-        return old(i) + e_ref[i // 2]
+        at = (i // 2 + 1) * NH
+        return old(i) + e_ref[at : at + NH, :]
+
+    def around_row(value, start):
+        def row(i):
+            at = start + i // 2
+            return value(i) + e_ref[at : at + 1, :]
+
+        return row
 
     def emit(i, diagonal, around, centre):
         out_ref[i] = (1.0 - OMEGA) * centre + OMEGA * (rhs_ref[i] + around) / diagonal
 
     fine_walk(
-        m_of,
-        v_of,
-        mb,
-        ma,
-        lambda i: ob(i) + er[i // 2 : i // 2 + 1, :],
-        lambda i: oa(i) + er[A1 + i // 2 : A1 + i // 2 + 1, :],
-        emit,
+        m_of, v_of, mb, ma, around_row(ob, own_rows), around_row(oa, own_rows + A1), emit
     )
     store_faces(out_ref, sx, sc, sz, sy)
 
@@ -694,68 +710,62 @@
 
 def body(pressure, divergence, void_fraction, bubble_volume, bubble_count, bubble_cell):
     block = struct(NA, NH, NR)
-    flat1 = struct(A1 * H1, R1)
+    wide = struct(A1, T1, R1)
     cell = bubble_cell.reshape(1, SLOTS)
     volume = bubble_volume.reshape(1, SLOTS)
     pairs = vmem(A1 * NH, NR)
-    buf = vmem(A1 * H1 + 16, R1)
-
-    spread = struct(64, A2 * H2, R2)
-    m0, m1, m2, cell, *send = call(
+    halves = vmem(A2 * T1, R1)
+
+    m0, m1, m2, *send = call(
         prepare,
-        [block, flat1, spread, jax.ShapeDtypeStruct((1, SLOTS), jnp.int32)]
-        + faces(3 * NH, 2 * NA + A1, NR),
-        (pressure, void_fraction, volume, cell, bubble_count),
-        [
-            vmem(NA, NH, NR),
-            vmem(NA, NH, NR),
-            vmem(1, SLOTS),
-            pairs,
-            pltpu.SemaphoreType.DMA((10,)),
-        ],
-        smem=(4,),
-        hbm=(0, 1, 2, 3),
+        [block, wide, struct(A2 * H2, R2)] + faces(3 * NH, 2 * NA + A1, NR),
+        (pressure, void_fraction, volume, bubble_count),
+        [pairs, halves],
+        smem=(3,),
     )
     ha = exchange(*send)
-    ring = (AZ2 + 4, 2, G2, R2)
-    m2, d2, w3 = call(
-        coarse_weights,
-        [struct(*ring), struct(*ring), struct(7, HALF, G2, R2)],
-        gathered(m2),
-        [vmem(AZ3, G2, R2), vmem(HALF + 2, G2, R2)],
-    )
     rhs, v0, *send = call(
         presmooth, [block, block] + faces(NH, NA, NR), (pressure, divergence, m0, cell, *ha)
     )
     hb = exchange(*send)
-    b1, v1, *send = call(
-        restrict, [flat1, flat1] + faces(H1, A1, R1), (rhs, v0, m0, m1, *ha, *hb), [pairs, buf]
-    )
-    hc = exchange(*send)
-    (copies,) = call(restrict1, [spread], (b1, v1, m1, *ha, *hc), [buf])
-    v1, *send = call(
+    b1, v1, sz, sy = call(
+        restrict,
+        [wide, wide] + [struct(5 * A1, R1)] * 2,
+        (rhs, v0, m0, m1, *ha, *hb),
+        [pairs],
+    )
+    v1, m1, b1, sx, sc = call(
+        widen,
+        [wide, wide, wide] + [struct(5 * T1, R1)] * 2,
+        (b1, v1, m1, swap(sz, "gz", 0), swap(sy, "gz", 1)),
+    )
+    hc = swap(sx, "az", 1), swap(sc, "az", 0)
+    (copies,) = call(restrict1, [struct(64, 2 * A2 * H2, R2)], (b1, v1, m1, m2, *hc), [halves])
+    ring = vmem(AZ2 + 4, 2, G2, R2)
+    ends = vmem(HALF + 2, G2, R2)
+    third = vmem(AZ3, G2, R2)
+    out, *send = call(
         coarse,
-        [flat1] + faces(H1, A1, R1),
-        (*gathered(copies), m2, d2, w3, b1, v1, m1, *ha, *hc),
+        [block] + faces(NH, NA, NR),
+        (*gathered(copies), b1, v1, m1, *hc, rhs, v0, m0, *ha, *hb),
         [
-            vmem(*ring),
-            vmem(*ring),
-            vmem(AZ3, G2, R2),
+            ring,
+            ring,
+            vmem(7, HALF, G2, R2),
+            third,
+            ends,
+            ring,
+            ring,
+            third,
             vmem(HALF, G2, R2),
-            vmem(HALF + 2, G2, R2),
-            vmem(HALF + 2, G2, R2),
-            vmem(AZ3, G2, R2),
+            ends,
+            ends,
+            third,
             vmem(A2 + 2, 2, G2, R2),
-            vmem(40, R2),
-            buf,
+            vmem(4 * (A2 + 2), R2),
+            vmem((A1 + 2) * T1, R1),
+            vmem((A1 + 2) * NH + 2 * A1, NR),
         ],
-    )
-    hf = exchange(*send)
-    out, *send = call(
-        postsmooth,
-        [block] + faces(NH, NA, NR),
-        (rhs, v0, m0, v1, *ha, *hb, *hf),
-        [vmem(A1, NH, NR), vmem(2 * A1 + 2 * NH, NR)],
     )
     hg = exchange(*send)
     return tuple(

time: 115 us -> 98.6 us (0.86)
  blocking collectives: 0 us -> 23.7 us
  starting transfers between devices: 49.3 us -> 26.9 us
  waiting for transfers between devices: 35.7 us -> 22.7 us
  Pallas kernels: 23.9 us -> 20.2 us
    all_to_all x0 -> x1, blocking collectives: none -> 23.7 us  [gathered(): lax.all_to_all(x, ('az', 'gz'), 0, 0, tiled=True, axis_index_groups=groups)]
    all_to_all x2 -> x0, starting transfers between devices: 17.3 us -> none  [gathered(): lax.all_to_all(x, ('az', 'gz'), 0, 0, tiled=True, axis_index_groups=groups)]
    all_to_all x2 -> x0, waiting for transfers between devices: 12.5 us -> none  [gathered(): lax.all_to_all(x, ('az', 'gz'), 0, 0, tiled=True, axis_index_groups=groups)]
    ppermute x22 -> x17, starting transfers between devices: 32 us -> 26.9 us  [swap(): return lax.ppermute(x, axis, pairs)]
    pallas_call x8 -> x7, Pallas kernels: 23.9 us -> 20.2 us  [call(): pl.pallas_call(kernel, out_shape=outs, in_specs=specs, out_specs=[pl.Bloc...]
    unnamed x12 -> x10, local copies, waits for them, and re-layouts: 4.43 us -> 3.37 us
    ppermute x22 -> x17, waiting for transfers between devices: 23.2 us -> 22.7 us  [swap(): return lax.ppermute(x, axis, pairs)]
  transfers between devices with their start and end apart: 24 -> 17, of which waited for: 7 -> 7; matrix products, arithmetic and copies ran while one was open for 0% -> 0% of each run, Pallas kernels for 7% -> 0%
where the time goes in v3:
time: 98.6 us; the launch traced here: 98.3 us
  starting transfers between devices  26.9 us (27%)
  blocking collectives  23.7 us (24%)
  waiting for transfers between devices  22.7 us (23%)
  Pallas kernels  20.2 us (20%)
  local copies, waits for them, and re-layouts  3.37 us (3%)
  between operations  1.51 us (2%)
    ppermute x17, starting transfers between devices, swap(): return lax.ppermute(x, axis, pairs)  26.9 us
    all_to_all x1, blocking collectives, gathered(): lax.all_to_all(x, ('az', 'gz'), 0, 0, tiled=True, axis_index_groups=groups)  23.7 us
    ppermute x17, waiting for transfers between devices, swap(): return lax.ppermute(x, axis, pairs)  22.7 us
    pallas_call x7, Pallas kernels, call(): pl.pallas_call(kernel, out_shape=outs, in_specs=specs, out_specs=[pl.Bloc...  20.2 us
    unnamed x10, local copies, waits for them, and re-layouts  3.37 us
  transfers between devices with their start and end apart: 17, of which 7 were waited for; matrix products, arithmetic and copies ran while one was open for 0% of the time, Pallas kernels for 0%

profile of v3, /device:TPU:0, one launch (start us, length us, event | category | flops | bytes accessed | tf_op | source)
XLA Modules:
  0.0 98.3 jit_solution(17949619701042360764)
XLA Ops:
  1.9 1.0 %copy-done = f32[32,8,512]{2,1,0:T(8,128)S(1)} copy-done((f32[32,8,512]{2,1,0:T(8,128)S(1)}, f32[32,8,512]{2,1,0:T(8,128)}, u32[]{:S(2)}) %copy-start) | copy-done | bytes 524312
  3.0 1.0 %copy-done.2 = f32[32,8,512]{2,1,0:T(8,128)S(1)} copy-done((f32[32,8,512]{2,1,0:T(8,128)S(1)}, f32[32,8,512]{2,1,0:T(8,128)}, u32[]{:S(2)}) %copy-start.2) | copy-done | bytes 524312
  4.0 1.3 %shard_map.77 = (f32[32,8,512]{2,1,0:T(8,128)S(1)}, f32[16,8,256]{2,1,0:T(8,128)S(1)}, f32[16,128]{1,0:T(8,128)S(1)}, f32[24,512]{1,0:T(8,128)S(1)}, f32[24,512]...) custom-call(f32[32,8,512]{2,1,0:T(8,128)S(1)} %copy-done, f32[32,8,512]{2,1,0:T(8,128)S(1)} %copy-done.2, ...), custom_call_target="tpu_custom_call" | custom-call | tf_op jit(solution)/shard_map/pallas_call | solution.py:34
  5.3 2.0 %collective-permute-start.2 = (f32[80,512]{1,0:T(8,128)S(1)}, f32[80,512]{1,0:T(8,128)S(1)}, u32[]{:S(2)}, u32[]{:S(2)}) collective-permute-start(f32[80,512]{1,0:T(8,128)S(1)} %get-tuple-element.32), channel_id=1, source_target_pairs={{0,1},{1,0},{2,3},{3,2},{4,5},{5,4},{6,7},{7,6},{8,9},{9,8},{10,11... | collective-permute-start | bytes 491528 | tf_op jit(solution)/shard_map/ppermute | solution.py:689
  7.3 2.6 %collective-permute-start.3 = (f32[80,512]{1,0:T(8,128)S(1)}, f32[80,512]{1,0:T(8,128)S(1)}, u32[]{:S(2)}, u32[]{:S(2)}) collective-permute-start(f32[80,512]{1,0:T(8,128)S(1)} %get-tuple-element.33), channel_id=1, source_target_pairs={{0,7},{1,2},{2,1},{3,4},{4,3},{5,6},{6,5},{7,0},{8,15},{9,10},{10,... | collective-permute-start | bytes 491528 | tf_op jit(solution)/shard_map/ppermute | solution.py:689
  9.9 5.0 %collective-permute-start = (f32[24,512]{1,0:T(8,128)S(1)}, f32[24,512]{1,0:T(8,128)S(1)}, u32[]{:S(2)}, u32[]{:S(2)}) collective-permute-start(f32[24,512]{1,0:T(8,128)S(1)} %get-tuple-element.30), channel_id=1, source_target_pairs={{0,120},{8,16},{16,8},{24,32},{32,24},{40,48},{48,40},{56,64},{64,... | collective-permute-start | bytes 147464 | tf_op jit(solution)/shard_map/ppermute | solution.py:689
  14.8 2.3 %collective-permute-done.ax = f32[24,512]{1,0:T(8,128)S(1)} collective-permute-done((f32[24,512]{1,0:T(8,128)S(1)}, f32[24,512]{1,0:T(8,128)S(1)}, u32[]{:S(2)}, u32[]{:S(2)}) %collective-permute-start) | collective-permute-done | bytes 49184 | tf_op jit(solution)/shard_map/ppermute | solution.py:689
  17.8 1.3 %shard_map.78 = (f32[32,8,512]{2,1,0:T(8,128)S(1)}, f32[32,8,512]{2,1,0:T(8,128)S(1)}, f32[8,512]{1,0:T(8,128)S(1)}, f32[8,512]{1,0:T(8,128)S(1)}, f32[32,512]{1,0:T(8,128)S(1)}, /*index=5*/f32[32,512]{1,0:T(8,128)S(1)}) custom-call(f32[32,8,512]{2,1,0:T(8,128)S(1)} %copy-done, f32[32,8,512]{2,1,0:T(8,128)S(1)} %copy-done.1, ...), custom_call_target="tpu_custom_call" | custom-call | tf_op jit(solution)/shard_map/pallas_call | solution.py:34
  20.1 1.8 %collective-permute-start.7 = (f32[32,512]{1,0:T(8,128)S(1)}, f32[32,512]{1,0:T(8,128)S(1)}, u32[]{:S(2)}, u32[]{:S(2)}) collective-permute-start(f32[32,512]{1,0:T(8,128)S(1)} %get-tuple-element.40), channel_id=1, source_target_pairs={{0,7},{1,2},{2,1},{3,4},{4,3},{5,6},{6,5},{7,0},{8,15},{9,10},{10,... | collective-permute-start | bytes 196616 | tf_op jit(solution)/shard_map/ppermute | solution.py:689
  21.9 4.1 %collective-permute-start.4 = (f32[8,512]{1,0:T(8,128)S(1)}, f32[8,512]{1,0:T(8,128)S(1)}, u32[]{:S(2)}, u32[]{:S(2)}) collective-permute-start(f32[8,512]{1,0:T(8,128)S(1)} %get-tuple-element.37), channel_id=1, source_target_pairs={{0,120},{8,16},{16,8},{24,32},{32,24},{40,48},{48,40},{56,64},{64,... | collective-permute-start | bytes 49160 | tf_op jit(solution)/shard_map/ppermute | solution.py:689
  26.0 2.7 %collective-permute-done.4.bx = f32[8,512]{1,0:T(8,128)S(1)} collective-permute-done((f32[8,512]{1,0:T(8,128)S(1)}, f32[8,512]{1,0:T(8,128)S(1)}, u32[]{:S(2)}, u32[]{:S(2)}) %collective-permute-start.4) | collective-permute-done | bytes 16416 | tf_op jit(solution)/shard_map/ppermute | solution.py:689
  28.7 1.7 %shard_map.79 = (f32[16,8,256]{2,1,0:T(8,128)S(1)}, f32[16,8,256]{2,1,0:T(8,128)S(1)}, f32[80,256]{1,0:T(8,128)S(1)}, f32[80,256]{1,0:T(8,128)S(1)}) custom-call(f32[32,8,512]{2,1,0:T(8,128)S(1)} %get-tuple-element.34.rhs_ref, f32[32,8,512]{2,1,0:T(8,128)S(1)} %get-tuple-element.35.v_ref, f32[32,8,512]{2,1,0:T(8,128)S(1)} %get-tuple-element.29.m_ref, ...), custom_call_target="tpu_custom_call" | custom-call | tf_op jit(solution)/shard_map/pallas_call | solution.py:34
  31.2 1.7 %collective-permute-start.9 = (f32[80,256]{1,0:T(8,128)S(1)}, f32[80,256]{1,0:T(8,128)S(1)}, u32[]{:S(2)}, u32[]{:S(2)}) collective-permute-start(f32[80,256]{1,0:T(8,128)S(1)} %get-tuple-element.44), channel_id=1, source_target_pairs={{0,7},{1,2},{2,1},{3,4},{4,3},{5,6},{6,5},{7,0},{8,15},{9,10},{10,... | collective-permute-start | bytes 245768 | tf_op jit(solution)/shard_map/ppermute | solution.py:689
  32.9 2.7 %collective-permute-done.8.z_ref = f32[80,256]{1,0:T(8,128)S(1)} collective-permute-done((f32[80,256]{1,0:T(8,128)S(1)}, f32[80,256]{1,0:T(8,128)S(1)}, u32[]{:S(2)}, u32[]{:S(2)}) %collective-permute-start.8) | collective-permute-done | bytes 81952 | tf_op jit(solution)/shard_map/ppermute | solution.py:689
  35.7 2.1 %collective-permute-done.9.y_ref = f32[80,256]{1,0:T(8,128)S(1)} collective-permute-done((f32[80,256]{1,0:T(8,128)S(1)}, f32[80,256]{1,0:T(8,128)S(1)}, u32[]{:S(2)}, u32[]{:S(2)}) %collective-permute-start.9) | collective-permute-done | bytes 81952 | tf_op jit(solution)/shard_map/ppermute | solution.py:689
  37.9 2.7 %collective-permute-start.10 = (f32[40,256]{1,0:T(8,128)S(1)}, f32[40,256]{1,0:T(8,128)S(1)}, u32[]{:S(2)}, u32[]{:S(2)}) collective-permute-start(f32[40,256]{1,0:T(8,128)S(1)} %get-tuple-element.49), channel_id=1, source_target_pairs={{0,120},{8,16},{16,8},{24,32},{32,24},{40,48},{48,40},{56,64},{64,... | collective-permute-start | bytes 122888 | tf_op jit(solution)/shard_map/ppermute | solution.py:689
  40.6 4.4 %collective-permute-done.10.cx = f32[40,256]{1,0:T(8,128)S(1)} collective-permute-done((f32[40,256]{1,0:T(8,128)S(1)}, f32[40,256]{1,0:T(8,128)S(1)}, u32[]{:S(2)}, u32[]{:S(2)}) %collective-permute-start.10) | collective-permute-done | bytes 40992 | tf_op jit(solution)/shard_map/ppermute | solution.py:689
  45.7 23.7 %all_to_all.5 = f32[64,32,128]{2,1,0:T(8,128)S(1)} all-to-all(f32[64,32,128]{2,1,0:T(8,128)S(1)} %shard_map.81), channel_id=1, replica_groups={{0,1,2,3,4,5,6,7,16,17,18,19,20,21,22,23,32,33,34,35,36,37,38,39,48,49,..., dimensions={0} | all-to-all | bytes 2097152 | tf_op jit(solution)/shard_map/all_to_all | solution.py:698
  69.3 2.7 %collective-permute-done.12.oth = f32[2048,128]{1,0:T(8,128)S(1)} collective-permute-done((f32[2048,128]{1,0:T(8,128)S(1)}, f32[2048,128]{1,0:T(8,128)S(1)}, u32[]{:S(2)}, u32[]{:S(2)}) %collective-permute-start.12) | collective-permute-done | bytes 1048608 | tf_op jit(solution)/shard_map/ppermute | solution.py:689
  72.0 13.6 %shard_map.82 = (f32[32,8,512]{2,1,0:T(8,128)S(1)}, f32[8,512]{1,0:T(8,128)S(1)}, f32[8,512]{1,0:T(8,128)S(1)}, f32[32,512]{1,0:T(8,128)S(1)}, f32[32,512]{1,0:T(8,128)S(1)}) custom-call(f32[2048,128]{1,0:T(8,128)S(1)} %bitcast.4, f32[2048,128]{1,0:T(8,128)S(1)} %collective-permute-done.12.oth, f32[16,8,256]{2,1,0:T(8,128)S(1)} %get-tuple-element.45.bw, ...), custom_call_target="tpu_custom_call" | custom-call | tf_op jit(solution)/shard_map/pallas_call | solution.py:34
  85.6 1.1 %collective-permute-start.15 = (f32[32,512]{1,0:T(8,128)S(1)}, f32[32,512]{1,0:T(8,128)S(1)}, u32[]{:S(2)}, u32[]{:S(2)}) collective-permute-start(f32[32,512]{1,0:T(8,128)S(1)} %get-tuple-element.54), channel_id=1, source_target_pairs={{0,1},{1,0},{2,3},{3,2},{4,5},{5,4},{6,7},{7,6},{8,9},{9,8},{10,11... | collective-permute-start | bytes 196616 | tf_op jit(solution)/shard_map/ppermute | solution.py:689
  86.7 3.1 %collective-permute-start.16 = (f32[32,512]{1,0:T(8,128)S(1)}, f32[32,512]{1,0:T(8,128)S(1)}, u32[]{:S(2)}, u32[]{:S(2)}) collective-permute-start(f32[32,512]{1,0:T(8,128)S(1)} %get-tuple-element.55), channel_id=1, source_target_pairs={{0,7},{1,2},{2,1},{3,4},{4,3},{5,6},{6,5},{7,0},{8,15},{9,10},{10,... | collective-permute-start | bytes 196616 | tf_op jit(solution)/shard_map/ppermute | solution.py:689
  90.8 5.8 %collective-permute-done.13.gx = f32[8,512]{1,0:T(8,128)S(1)} collective-permute-done((f32[8,512]{1,0:T(8,128)S(1)}, f32[8,512]{1,0:T(8,128)S(1)}, u32[]{:S(2)}, u32[]{:S(2)}) %collective-permute-start.13) | collective-permute-done | bytes 16416 | tf_op jit(solution)/shard_map/ppermute | solution.py:689
  96.6 1.6 %shard_map.83 = (f32[32,8,512]{2,1,0:T(8,128)}, f32[32,8,512]{2,1,0:T(8,128)}) custom-call(f32[32,8,512]{2,1,0:T(8,128)S(1)} %get-tuple-element.34.rhs_ref, f32[32,8,512]{2,1,0:T(8,128)S(1)} %get-tuple-element.51.v_ref, f32[32,8,512]{2,1,0:T(8,128)S(1)} %get-tuple-element.29.m_ref, f32[24,512]{1,0:T(8,128)S(1)} %collective-permute-done.ax, ...), custom_call_target="tpu_custom_call" | custom-call | tf_op jit(solution)/shard_map/pallas_call | solution.py:34
  (28 shorter events, 5.0 us)
Async XLA Ops:
  1.3 0.7 copy-start.3
  1.9 1.0 %copy-start = (f32[32,8,512]{2,1,0:T(8,128)S(1)}, f32[32,8,512]{2,1,0:T(8,128)}, u32[]{:S(2)}) copy-start(f32[32,8,512]{2,1,0:T(8,128)} %p_ref.3) | copy-start | bytes 1572868
  3.0 1.0 %copy-start.2 = (f32[32,8,512]{2,1,0:T(8,128)S(1)}, f32[32,8,512]{2,1,0:T(8,128)}, u32[]{:S(2)}) copy-start(f32[32,8,512]{2,1,0:T(8,128)} %void_ref.1) | copy-start | bytes 1572868
  4.0 13.1 %copy-start.1 = (f32[32,8,512]{2,1,0:T(8,128)S(1)}, f32[32,8,512]{2,1,0:T(8,128)}, u32[]{:S(2)}) copy-start(f32[32,8,512]{2,1,0:T(8,128)} %div_ref.1) | copy-start | bytes 1572868
  5.3 11.8 %collective-permute-start.2 = (f32[80,512]{1,0:T(8,128)S(1)}, f32[80,512]{1,0:T(8,128)S(1)}, u32[]{:S(2)}, u32[]{:S(2)}) collective-permute-start(f32[80,512]{1,0:T(8,128)S(1)} %get-tuple-element.32), channel_id=1, source_target_pairs={{0,1},{1,0},{2,3},{3,2},{4,5},{5,4},{6,7},{7,6},{8,9},{9,8},{10,11... | collective-permute-start | bytes 491528 | tf_op jit(solution)/shard_map/ppermute | solution.py:689
  7.3 9.8 %collective-permute-start.3 = (f32[80,512]{1,0:T(8,128)S(1)}, f32[80,512]{1,0:T(8,128)S(1)}, u32[]{:S(2)}, u32[]{:S(2)}) collective-permute-start(f32[80,512]{1,0:T(8,128)S(1)} %get-tuple-element.33), channel_id=1, source_target_pairs={{0,7},{1,2},{2,1},{3,4},{4,3},{5,6},{6,5},{7,0},{8,15},{9,10},{10,... | collective-permute-start | bytes 491528 | tf_op jit(solution)/shard_map/ppermute | solution.py:689
  9.9 7.2 %collective-permute-start = (f32[24,512]{1,0:T(8,128)S(1)}, f32[24,512]{1,0:T(8,128)S(1)}, u32[]{:S(2)}, u32[]{:S(2)}) collective-permute-start(f32[24,512]{1,0:T(8,128)S(1)} %get-tuple-element.30), channel_id=1, source_target_pairs={{0,120},{8,16},{16,8},{24,32},{32,24},{40,48},{48,40},{56,64},{64,... | collective-permute-start | bytes 147464 | tf_op jit(solution)/shard_map/ppermute | solution.py:689
  14.8 2.3 %collective-permute-start.1 = (f32[24,512]{1,0:T(8,128)S(1)}, f32[24,512]{1,0:T(8,128)S(1)}, u32[]{:S(2)}, u32[]{:S(2)}) collective-permute-start(f32[24,512]{1,0:T(8,128)S(1)} %get-tuple-element.31), channel_id=1, source_target_pairs={{0,8},{8,0},{16,24},{24,16},{32,40},{40,32},{48,56},{56,48},{64,72... | collective-permute-start | bytes 147464 | tf_op jit(solution)/shard_map/ppermute | solution.py:689
  17.1 0.7 copy-start.4
  19.1 9.6 %collective-permute-start.6 = (f32[32,512]{1,0:T(8,128)S(1)}, f32[32,512]{1,0:T(8,128)S(1)}, u32[]{:S(2)}, u32[]{:S(2)}) collective-permute-start(f32[32,512]{1,0:T(8,128)S(1)} %get-tuple-element.39), channel_id=1, source_target_pairs={{0,1},{1,0},{2,3},{3,2},{4,5},{5,4},{6,7},{7,6},{8,9},{9,8},{10,11... | collective-permute-start | bytes 196616 | tf_op jit(solution)/shard_map/ppermute | solution.py:689
  20.1 8.6 %collective-permute-start.7 = (f32[32,512]{1,0:T(8,128)S(1)}, f32[32,512]{1,0:T(8,128)S(1)}, u32[]{:S(2)}, u32[]{:S(2)}) collective-permute-start(f32[32,512]{1,0:T(8,128)S(1)} %get-tuple-element.40), channel_id=1, source_target_pairs={{0,7},{1,2},{2,1},{3,4},{4,3},{5,6},{6,5},{7,0},{8,15},{9,10},{10,... | collective-permute-start | bytes 196616 | tf_op jit(solution)/shard_map/ppermute | solution.py:689
  21.9 6.8 %collective-permute-start.4 = (f32[8,512]{1,0:T(8,128)S(1)}, f32[8,512]{1,0:T(8,128)S(1)}, u32[]{:S(2)}, u32[]{:S(2)}) collective-permute-start(f32[8,512]{1,0:T(8,128)S(1)} %get-tuple-element.37), channel_id=1, source_target_pairs={{0,120},{8,16},{16,8},{24,32},{32,24},{40,48},{48,40},{56,64},{64,... | collective-permute-start | bytes 49160 | tf_op jit(solution)/shard_map/ppermute | solution.py:689
  25.9 2.7 %collective-permute-start.5 = (f32[8,512]{1,0:T(8,128)S(1)}, f32[8,512]{1,0:T(8,128)S(1)}, u32[]{:S(2)}, u32[]{:S(2)}) collective-permute-start(f32[8,512]{1,0:T(8,128)S(1)} %get-tuple-element.38), channel_id=1, source_target_pairs={{0,8},{8,0},{16,24},{24,16},{32,40},{40,32},{48,56},{56,48},{64,72... | collective-permute-start | bytes 49160 | tf_op jit(solution)/shard_map/ppermute | solution.py:689
  30.4 5.3 %collective-permute-start.8 = (f32[80,256]{1,0:T(8,128)S(1)}, f32[80,256]{1,0:T(8,128)S(1)}, u32[]{:S(2)}, u32[]{:S(2)}) collective-permute-start(f32[80,256]{1,0:T(8,128)S(1)} %get-tuple-element.43), channel_id=1, source_target_pairs={{0,1},{1,0},{2,3},{3,2},{4,5},{5,4},{6,7},{7,6},{8,9},{9,8},{10,11... | collective-permute-start | bytes 245768 | tf_op jit(solution)/shard_map/ppermute | solution.py:689
  31.2 6.6 %collective-permute-start.9 = (f32[80,256]{1,0:T(8,128)S(1)}, f32[80,256]{1,0:T(8,128)S(1)}, u32[]{:S(2)}, u32[]{:S(2)}) collective-permute-start(f32[80,256]{1,0:T(8,128)S(1)} %get-tuple-element.44), channel_id=1, source_target_pairs={{0,7},{1,2},{2,1},{3,4},{4,3},{5,6},{6,5},{7,0},{8,15},{9,10},{10,... | collective-permute-start | bytes 245768 | tf_op jit(solution)/shard_map/ppermute | solution.py:689
  37.9 7.1 %collective-permute-start.10 = (f32[40,256]{1,0:T(8,128)S(1)}, f32[40,256]{1,0:T(8,128)S(1)}, u32[]{:S(2)}, u32[]{:S(2)}) collective-permute-start(f32[40,256]{1,0:T(8,128)S(1)} %get-tuple-element.49), channel_id=1, source_target_pairs={{0,120},{8,16},{16,8},{24,32},{32,24},{40,48},{48,40},{56,64},{64,... | collective-permute-start | bytes 122888 | tf_op jit(solution)/shard_map/ppermute | solution.py:689
  40.6 4.4 %collective-permute-start.11 = (f32[40,256]{1,0:T(8,128)S(1)}, f32[40,256]{1,0:T(8,128)S(1)}, u32[]{:S(2)}, u32[]{:S(2)}) collective-permute-start(f32[40,256]{1,0:T(8,128)S(1)} %get-tuple-element.50), channel_id=1, source_target_pairs={{0,8},{8,0},{16,24},{24,16},{32,40},{40,32},{48,56},{56,48},{64,72... | collective-permute-start | bytes 122888 | tf_op jit(solution)/shard_map/ppermute | solution.py:689
  69.3 2.7 %collective-permute-start.12 = (f32[2048,128]{1,0:T(8,128)S(1)}, f32[2048,128]{1,0:T(8,128)S(1)}, u32[]{:S(2)}, u32[]{:S(2)}) collective-permute-start(f32[2048,128]{1,0:T(8,128)S(1)} %bitcast.3), channel_id=1, source_target_pairs={{0,8},{8,0},{16,24},{24,16},{32,40},{40,32},{48,56},{56,48},{64,72... | collective-permute-start | bytes 3145736 | tf_op jit(solution)/shard_map/ppermute | solution.py:689
  85.6 11.0 %collective-permute-start.15 = (f32[32,512]{1,0:T(8,128)S(1)}, f32[32,512]{1,0:T(8,128)S(1)}, u32[]{:S(2)}, u32[]{:S(2)}) collective-permute-start(f32[32,512]{1,0:T(8,128)S(1)} %get-tuple-element.54), channel_id=1, source_target_pairs={{0,1},{1,0},{2,3},{3,2},{4,5},{5,4},{6,7},{7,6},{8,9},{9,8},{10,11... | collective-permute-start | bytes 196616 | tf_op jit(solution)/shard_map/ppermute | solution.py:689
  86.7 9.8 %collective-permute-start.16 = (f32[32,512]{1,0:T(8,128)S(1)}, f32[32,512]{1,0:T(8,128)S(1)}, u32[]{:S(2)}, u32[]{:S(2)}) collective-permute-start(f32[32,512]{1,0:T(8,128)S(1)} %get-tuple-element.55), channel_id=1, source_target_pairs={{0,7},{1,2},{2,1},{3,4},{4,3},{5,6},{6,5},{7,0},{8,15},{9,10},{10,... | collective-permute-start | bytes 196616 | tf_op jit(solution)/shard_map/ppermute | solution.py:689
  89.8 6.8 %collective-permute-start.13 = (f32[8,512]{1,0:T(8,128)S(1)}, f32[8,512]{1,0:T(8,128)S(1)}, u32[]{:S(2)}, u32[]{:S(2)}) collective-permute-start(f32[8,512]{1,0:T(8,128)S(1)} %get-tuple-element.52), channel_id=1, source_target_pairs={{0,120},{8,16},{16,8},{24,32},{32,24},{40,48},{48,40},{56,64},{64,... | collective-permute-start | bytes 49160 | tf_op jit(solution)/shard_map/ppermute | solution.py:689
  90.8 5.8 %collective-permute-start.14 = (f32[8,512]{1,0:T(8,128)S(1)}, f32[8,512]{1,0:T(8,128)S(1)}, u32[]{:S(2)}, u32[]{:S(2)}) collective-permute-start(f32[8,512]{1,0:T(8,128)S(1)} %get-tuple-element.53), channel_id=1, source_target_pairs={{0,8},{8,0},{16,24},{24,16},{32,40},{40,32},{48,56},{56,48},{64,72... | collective-permute-start | bytes 49160 | tf_op jit(solution)/shard_map/ppermute | solution.py:689

commit v4 on v3

--- a/solution.py
+++ b/solution.py
@@ -12,6 +12,7 @@
 OMEGA = 0.8
 COARSE_SWEEPS = 32
 F32 = jnp.float32
+BF16 = jnp.bfloat16
 
 NA, NH, NR = 32, 8, 512
 A1, H1, R1 = 16, 4, 256
@@ -48,8 +49,19 @@
     return lax.broadcasted_iota(jnp.int32, shape, dim)
 
 
+def parts(x):
+    high = x.astype(BF16)
+    rest = x - high.astype(F32)
+    mid = rest.astype(BF16)
+    return high, mid, (rest - mid.astype(F32)).astype(BF16)
+
+
 def dot(a, b):
-    return jnp.dot(a, b, precision=lax.Precision.HIGHEST, preferred_element_type=F32)
+    if b.dtype == BF16:
+        p = [jnp.dot(x, b, preferred_element_type=F32) for x in parts(a)]
+    else:
+        p = [jnp.dot(a, x, preferred_element_type=F32) for x in parts(b)]
+    return (p[2] + p[1]) + p[0]
 
 
 def radial_consts(shape, size, step, rad):
@@ -61,23 +73,27 @@
     return ca, ri, ro
 
 
+def hot(mask):
+    return mask.astype(F32).astype(BF16)
+
+
 def pair_cols(n):
-    return (iota((n, n // 2), 0) // 2 == iota((n, n // 2), 1)).astype(F32)
+    return hot(iota((n, n // 2), 0) // 2 == iota((n, n // 2), 1))
 
 
 def dup_cols(n):
-    return (iota((n, 2 * n), 0) == iota((n, 2 * n), 1) // 2).astype(F32)
+    return hot(iota((n, 2 * n), 0) == iota((n, 2 * n), 1) // 2)
 
 
 def row_sums(planes, out, first, per):
     o, r = iota((planes * out, planes * per), 0), iota((planes * out, planes * per), 1)
     h = r % per - first
-    return ((o // out == r // per) & (h >= 0) & (h // 2 == o % out)).astype(F32)
+    return hot((o // out == r // per) & (h >= 0) & (h // 2 == o % out))
 
 
 def widened(planes):
     o, r = iota((planes * 8, planes * 8), 0), iota((planes * 8, planes * 8), 1)
-    return ((o // 8 == r // 8) & (o % 8 == (r % 8) // 2 + 2)).astype(F32)
+    return hot((o // 8 == r // 8) & (o % 8 == (r % 8) // 2 + 2))
 
 
 def position():
@@ -200,11 +216,7 @@
         y_ref[rows_at + i : rows_at + i + 1, :] = ref[i, pl.ds(y_row, 1), :]
 
 
-def prepare(
-    p_ref, void_ref, vol_ref, cnt_ref, m0_ref, m1_ref, m2_ref, sx, sc, sz, sy, pairs, halves
-):
-    a, g = position()
-    pa, pg = a % 2, g % 2
+def mobilities(void_ref, m0_ref, m1_ref, m2_ref, pairs, halves):
     for i in range(0, NA, 2):
         u = 1.0 / (1.0 - void_ref[i])
         v = 1.0 / (1.0 - void_ref[i + 1])
@@ -215,6 +227,11 @@
     for i in range(A2):
         halves[i * T1 : (i + 1) * T1, :] = m1_ref[2 * i] + m1_ref[2 * i + 1]
     m2_ref[...] = 0.125 * dot(row_sums(A2, H2, 2, T1), dot(halves[...], pair_cols(R1)))
+
+
+def first_faces(p_ref, m0_ref, m1_ref, vol_ref, cnt_ref, sx, sc, sz, sy):
+    a, g = position()
+    pa, pg = a % 2, g % 2
     store_faces(p_ref, sx, sc, sz, sy, 0, 0)
     store_faces(m0_ref, sx, sc, sz, sy, NH, NA)
     rest = slice(2 * NH, 3 * NH)
@@ -269,15 +286,13 @@
     ah = Halo(ax, ac, az, ay)
     arrived = ah.prev(slice(2 * NH, 2 * NH + 1), slice(R1, R1 + SLOTS))
     cell = cell_ref[...]
-    plane_hot = (iota((NA * NH, SLOTS), 0) == lax.shift_right_logical(cell, 9)).astype(F32)
+    plane_hot = hot(iota((NA * NH, SLOTS), 0) == lax.shift_right_logical(cell, 9))
     radius_hot = jnp.where(iota((NR, SLOTS), 0) == (cell & (NR - 1)), arrived, 0.0)
-    deposit = lax.dot_general(
-        plane_hot,
-        radius_hot,
-        (((1,), (1,)), ((), ())),
-        precision=lax.Precision.HIGHEST,
-        preferred_element_type=F32,
-    )
+    deposit = [
+        lax.dot_general(plane_hot, x, (((1,), (1,)), ((), ())), preferred_element_type=F32)
+        for x in parts(radius_hot)
+    ]
+    deposit = (deposit[2] + deposit[1]) + deposit[0]
     rhs_ref[...] = div_ref[...] + deposit.reshape(NA, NH, NR)
     m_of, mb, ma = fine_mobility(m_ref, ah)
     v_of, vb, va = fine_values(p_ref, ah)
@@ -443,8 +458,8 @@
 
 def packed(ref):
     row_i, col_i = iota((R2, R2), 0), iota((R2, R2), 1)
-    left = (row_i // 2 == col_i).astype(F32)
-    right = (row_i // 2 + R2 // 2 == col_i).astype(F32)
+    left = hot(row_i // 2 == col_i)
+    right = hot(row_i // 2 + R2 // 2 == col_i)
     lower = ref[0:HALF].reshape(HALF * G2, R2)
     upper = ref[HALF:AZ3].reshape(HALF * G2, R2)
     return (dot(lower, left) + dot(upper, right)).reshape(HALF, G2, R2)
@@ -462,13 +477,17 @@
     a, g = position()
     pa = a % 2
     rows = A2 * H2
-    for k in range(N_AZ):
-        base = (k // 2) * N_GZ * 2 * rows + rows
-        first, second = (own, oth) if k % 2 == 0 else (oth, own)
-        for i in range(A2):
-            for p in range(2):
-                at = pl.ds(base + i * 2 + p, G2, stride=2 * rows)
-                m2[k * A2 + i + 2, p] = pick(pa, first[at, :], second[at, :])
+    def lay(own, oth):
+        for k in range(N_AZ):
+            base = (k // 2) * N_GZ * 2 * rows + rows
+            ref = oth if k % 2 else own
+            for i in range(A2):
+                for p in range(2):
+                    at = pl.ds(base + i * 2 + p, G2, stride=2 * rows)
+                    m2[k * A2 + i + 2, p] = ref[at, :]
+
+    pl.when(pa == 0)(lambda: lay(own, oth))
+    pl.when(pa == 1)(lambda: lay(oth, own))
     close_ring(m2)
     consts = level2_consts()
 
@@ -521,15 +540,19 @@
     pa = a % 2
     rows = A2 * H2
 
-    for k in range(N_AZ):
-        base = (k // 2) * N_GZ * 2 * rows
-        first, second = (own, oth) if k % 2 == 0 else (oth, own)
-        for i in range(A2):
-            for p in range(2):
-                at = pl.ds(base + i * 2 + p, G2, stride=2 * rows)
-                b = pick(pa, first[at, :], second[at, :])
-                b2[k * A2 + i + 2, p] = b
-                v2[k * A2 + i + 2, p] = b * d2[k * A2 + i + 2, p]
+    def lay(own, oth):
+        for k in range(N_AZ):
+            base = (k // 2) * N_GZ * 2 * rows
+            ref = oth if k % 2 else own
+            for i in range(A2):
+                s = k * A2 + i + 2
+                for p in range(2):
+                    b = ref[pl.ds(base + i * 2 + p, G2, stride=2 * rows), :]
+                    b2[s, p] = b
+                    v2[s, p] = b * d2[s, p]
+
+    pl.when(pa == 0)(lambda: lay(own, oth))
+    pl.when(pa == 1)(lambda: lay(oth, own))
     close_ring(b2)
     close_ring(v2)
     consts = level2_consts()
@@ -587,8 +610,8 @@
 
     row_i, col_i = iota((R2, R2), 0), iota((R2, R2), 1)
     solved = vb[1 : HALF + 1].reshape(HALF * G2, R2)
-    e2[0:HALF] = dot(solved, (row_i == col_i // 2).astype(F32)).reshape(HALF, G2, R2)
-    e2[HALF:AZ3] = dot(solved, (row_i == col_i // 2 + R2 // 2).astype(F32)).reshape(HALF, G2, R2)
+    e2[0:HALF] = dot(solved, hot(row_i == col_i // 2)).reshape(HALF, G2, R2)
+    e2[HALF:AZ3] = dot(solved, hot(row_i == col_i // 2 + R2 // 2)).reshape(HALF, G2, R2)
 
     at = a * A2
     values = []
@@ -611,7 +634,7 @@
         for q, (p, row) in enumerate(((1, low), (0, g), (1, g), (0, high))):
             src[4 * j + q : 4 * j + q + 1, :] = v2f[j, p, pl.ds(row, 1), :]
     o, c = iota((8 * (A2 + 2), 4 * (A2 + 2)), 0), iota((8 * (A2 + 2), 4 * (A2 + 2)), 1)
-    e1 = dot((o // 2 == c).astype(F32), dot(src[...], dup_cols(R2)))
+    e1 = dot(hot(o // 2 == c), dot(src[...], dup_cols(R2)))
     halo = Halo(cx, cc, None, None)
 
     def v1_of(i):
@@ -630,7 +653,7 @@
     o, c = iota(shape, 0), iota(shape, 1)
     j = jnp.where(o < own_rows, o // NH, (o - own_rows) % A1 + 1)
     h = jnp.where(o < own_rows, (o % NH) // 2 + 2, jnp.where(o < own_rows + A1, 1, H1 + 2))
-    e_ref[...] = dot(dot((c == j * T1 + h).astype(F32), v1f[...]), dup_cols(R1))
+    e_ref[...] = dot(dot(hot(c == j * T1 + h), v1f[...]), dup_cols(R1))
     ah, bh = Halo(ax, ac, az, ay), Halo(bx, bc, bz, by)
     m_of, mb, ma = fine_mobility(m_ref, ah)
     old, ob, oa = fine_values(v_ref, bh)
@@ -716,12 +739,14 @@
     pairs = vmem(A1 * NH, NR)
     halves = vmem(A2 * T1, R1)
 
-    m0, m1, m2, *send = call(
-        prepare,
-        [block, wide, struct(A2 * H2, R2)] + faces(3 * NH, 2 * NA + A1, NR),
-        (pressure, void_fraction, volume, bubble_count),
-        [pairs, halves],
-        smem=(3,),
+    m0, m1, m2 = call(
+        mobilities, [block, wide, struct(A2 * H2, R2)], (void_fraction,), [pairs, halves]
+    )
+    send = call(
+        first_faces,
+        faces(3 * NH, 2 * NA + A1, NR),
+        (pressure, m0, m1, volume, bubble_count),
+        smem=(4,),
     )
     ha = exchange(*send)
     rhs, v0, *send = call(

time: 98.6 us -> 94.8 us (0.961)
  Pallas kernels: 20.2 us -> 18.1 us
  local copies, waits for them, and re-layouts: 3.37 us -> 1.71 us
    pallas_call x7 -> x8, Pallas kernels: 20.2 us -> 18.1 us  [call(): pl.pallas_call(kernel, out_shape=outs, in_specs=specs, out_specs=[pl.Bloc...]
    unnamed x10, local copies, waits for them, and re-layouts: 3.37 us -> 1.71 us
where the time goes in v4:
time: 94.8 us; the launch traced here: 94.7 us
  starting transfers between devices  26.9 us (28%)
  blocking collectives  23.7 us (25%)
  waiting for transfers between devices  22.7 us (24%)
  Pallas kernels  18.1 us (19%)
  local copies, waits for them, and re-layouts  1.71 us (2%)
  between operations  1.58 us (2%)
    ppermute x17, starting transfers between devices, swap(): return lax.ppermute(x, axis, pairs)  26.9 us
    all_to_all x1, blocking collectives, gathered(): lax.all_to_all(x, ('az', 'gz'), 0, 0, tiled=True, axis_index_groups=groups)  23.7 us
    ppermute x17, waiting for transfers between devices, swap(): return lax.ppermute(x, axis, pairs)  22.7 us
    pallas_call x8, Pallas kernels, call(): pl.pallas_call(kernel, out_shape=outs, in_specs=specs, out_specs=[pl.Bloc...  18.1 us
  transfers between devices with their start and end apart: 17, of which 7 were waited for; matrix products, arithmetic and copies ran while one was open for 0% of the time, Pallas kernels for 0%

profile of v4, /device:TPU:0, one launch (start us, length us, event | category | flops | bytes accessed | tf_op | source)
XLA Modules:
  0.0 94.7 jit_solution(13505047778031290285)
XLA Ops:
  1.4 1.0 %copy-done.2 = f32[32,8,512]{2,1,0:T(8,128)S(1)} copy-done((f32[32,8,512]{2,1,0:T(8,128)S(1)}, f32[32,8,512]{2,1,0:T(8,128)}, u32[]{:S(2)}) %copy-start.2) | copy-done | bytes 524312
  4.0 2.1 %collective-permute-start.2 = (f32[80,512]{1,0:T(8,128)S(1)}, f32[80,512]{1,0:T(8,128)S(1)}, u32[]{:S(2)}, u32[]{:S(2)}) collective-permute-start(f32[80,512]{1,0:T(8,128)S(1)} %get-tuple-element.33), channel_id=1, source_target_pairs={{0,1},{1,0},{2,3},{3,2},{4,5},{5,4},{6,7},{7,6},{8,9},{9,8},{10,11... | collective-permute-start | bytes 491528 | tf_op jit(solution)/shard_map/ppermute | solution.py:712
  6.1 2.6 %collective-permute-start.3 = (f32[80,512]{1,0:T(8,128)S(1)}, f32[80,512]{1,0:T(8,128)S(1)}, u32[]{:S(2)}, u32[]{:S(2)}) collective-permute-start(f32[80,512]{1,0:T(8,128)S(1)} %get-tuple-element.34), channel_id=1, source_target_pairs={{0,7},{1,2},{2,1},{3,4},{4,3},{5,6},{6,5},{7,0},{8,15},{9,10},{10,... | collective-permute-start | bytes 491528 | tf_op jit(solution)/shard_map/ppermute | solution.py:712
  8.7 5.0 %collective-permute-start = (f32[24,512]{1,0:T(8,128)S(1)}, f32[24,512]{1,0:T(8,128)S(1)}, u32[]{:S(2)}, u32[]{:S(2)}) collective-permute-start(f32[24,512]{1,0:T(8,128)S(1)} %get-tuple-element.31), channel_id=1, source_target_pairs={{0,120},{8,16},{16,8},{24,32},{32,24},{40,48},{48,40},{56,64},{64,... | collective-permute-start | bytes 147464 | tf_op jit(solution)/shard_map/ppermute | solution.py:712
  13.6 2.3 %collective-permute-done.ax = f32[24,512]{1,0:T(8,128)S(1)} collective-permute-done((f32[24,512]{1,0:T(8,128)S(1)}, f32[24,512]{1,0:T(8,128)S(1)}, u32[]{:S(2)}, u32[]{:S(2)}) %collective-permute-start) | collective-permute-done | bytes 49184 | tf_op jit(solution)/shard_map/ppermute | solution.py:712
  15.9 1.2 %shard_map.79 = (f32[32,8,512]{2,1,0:T(8,128)S(1)}, f32[32,8,512]{2,1,0:T(8,128)S(1)}, f32[8,512]{1,0:T(8,128)S(1)}, f32[8,512]{1,0:T(8,128)S(1)}, f32[32,512]{1,0:T(8,128)S(1)}, /*index=5*/f32[32,512]{1,0:T(8,128)S(1)}) custom-call(f32[32,8,512]{2,1,0:T(8,128)S(1)} %copy-done, f32[32,8,512]{2,1,0:T(8,128)S(1)} %copy-done.1, ...), custom_call_target="tpu_custom_call" | custom-call | tf_op jit(solution)/shard_map/pallas_call | solution.py:35
  17.1 1.0 %collective-permute-start.6 = (f32[32,512]{1,0:T(8,128)S(1)}, f32[32,512]{1,0:T(8,128)S(1)}, u32[]{:S(2)}, u32[]{:S(2)}) collective-permute-start(f32[32,512]{1,0:T(8,128)S(1)} %get-tuple-element.39), channel_id=1, source_target_pairs={{0,1},{1,0},{2,3},{3,2},{4,5},{5,4},{6,7},{7,6},{8,9},{9,8},{10,11... | collective-permute-start | bytes 196616 | tf_op jit(solution)/shard_map/ppermute | solution.py:712
  18.2 1.8 %collective-permute-start.7 = (f32[32,512]{1,0:T(8,128)S(1)}, f32[32,512]{1,0:T(8,128)S(1)}, u32[]{:S(2)}, u32[]{:S(2)}) collective-permute-start(f32[32,512]{1,0:T(8,128)S(1)} %get-tuple-element.40), channel_id=1, source_target_pairs={{0,7},{1,2},{2,1},{3,4},{4,3},{5,6},{6,5},{7,0},{8,15},{9,10},{10,... | collective-permute-start | bytes 196616 | tf_op jit(solution)/shard_map/ppermute | solution.py:712
  19.9 4.1 %collective-permute-start.4 = (f32[8,512]{1,0:T(8,128)S(1)}, f32[8,512]{1,0:T(8,128)S(1)}, u32[]{:S(2)}, u32[]{:S(2)}) collective-permute-start(f32[8,512]{1,0:T(8,128)S(1)} %get-tuple-element.37), channel_id=1, source_target_pairs={{0,120},{8,16},{16,8},{24,32},{32,24},{40,48},{48,40},{56,64},{64,... | collective-permute-start | bytes 49160 | tf_op jit(solution)/shard_map/ppermute | solution.py:712
  24.0 2.7 %collective-permute-done.4.bx = f32[8,512]{1,0:T(8,128)S(1)} collective-permute-done((f32[8,512]{1,0:T(8,128)S(1)}, f32[8,512]{1,0:T(8,128)S(1)}, u32[]{:S(2)}, u32[]{:S(2)}) %collective-permute-start.4) | collective-permute-done | bytes 16416 | tf_op jit(solution)/shard_map/ppermute | solution.py:712
  26.7 1.5 %shard_map.80 = (f32[16,8,256]{2,1,0:T(8,128)S(1)}, f32[16,8,256]{2,1,0:T(8,128)S(1)}, f32[80,256]{1,0:T(8,128)S(1)}, f32[80,256]{1,0:T(8,128)S(1)}) custom-call(f32[32,8,512]{2,1,0:T(8,128)S(1)} %get-tuple-element.35.rhs_ref, f32[32,8,512]{2,1,0:T(8,128)S(1)} %get-tuple-element.36.v_ref, f32[32,8,512]{2,1,0:T(8,128)S(1)} %get-tuple-element.29.m0_ref.m_ref, ...), custom_call_target="tpu_custom_call" | custom-call | tf_op jit(solution)/shard_map/pallas_call | solution.py:35
  29.0 1.7 %collective-permute-start.9 = (f32[80,256]{1,0:T(8,128)S(1)}, f32[80,256]{1,0:T(8,128)S(1)}, u32[]{:S(2)}, u32[]{:S(2)}) collective-permute-start(f32[80,256]{1,0:T(8,128)S(1)} %get-tuple-element.44), channel_id=1, source_target_pairs={{0,7},{1,2},{2,1},{3,4},{4,3},{5,6},{6,5},{7,0},{8,15},{9,10},{10,... | collective-permute-start | bytes 245768 | tf_op jit(solution)/shard_map/ppermute | solution.py:712
  30.7 2.7 %collective-permute-done.8.z_ref = f32[80,256]{1,0:T(8,128)S(1)} collective-permute-done((f32[80,256]{1,0:T(8,128)S(1)}, f32[80,256]{1,0:T(8,128)S(1)}, u32[]{:S(2)}, u32[]{:S(2)}) %collective-permute-start.8) | collective-permute-done | bytes 81952 | tf_op jit(solution)/shard_map/ppermute | solution.py:712
  33.5 2.1 %collective-permute-done.9.y_ref = f32[80,256]{1,0:T(8,128)S(1)} collective-permute-done((f32[80,256]{1,0:T(8,128)S(1)}, f32[80,256]{1,0:T(8,128)S(1)}, u32[]{:S(2)}, u32[]{:S(2)}) %collective-permute-start.9) | collective-permute-done | bytes 81952 | tf_op jit(solution)/shard_map/ppermute | solution.py:712
  35.7 2.7 %collective-permute-start.10 = (f32[40,256]{1,0:T(8,128)S(1)}, f32[40,256]{1,0:T(8,128)S(1)}, u32[]{:S(2)}, u32[]{:S(2)}) collective-permute-start(f32[40,256]{1,0:T(8,128)S(1)} %get-tuple-element.49), channel_id=1, source_target_pairs={{0,120},{8,16},{16,8},{24,32},{32,24},{40,48},{48,40},{56,64},{64,... | collective-permute-start | bytes 122888 | tf_op jit(solution)/shard_map/ppermute | solution.py:712
  38.4 4.4 %collective-permute-done.10.cx = f32[40,256]{1,0:T(8,128)S(1)} collective-permute-done((f32[40,256]{1,0:T(8,128)S(1)}, f32[40,256]{1,0:T(8,128)S(1)}, u32[]{:S(2)}, u32[]{:S(2)}) %collective-permute-start.10) | collective-permute-done | bytes 40992 | tf_op jit(solution)/shard_map/ppermute | solution.py:712
  43.4 23.7 %all_to_all.5 = f32[64,32,128]{2,1,0:T(8,128)S(1)} all-to-all(f32[64,32,128]{2,1,0:T(8,128)S(1)} %shard_map.82), channel_id=1, replica_groups={{0,1,2,3,4,5,6,7,16,17,18,19,20,21,22,23,32,33,34,35,36,37,38,39,48,49,..., dimensions={0} | all-to-all | bytes 2097152 | tf_op jit(solution)/shard_map/all_to_all | solution.py:721
  67.1 2.7 %collective-permute-done.12.oth = f32[2048,128]{1,0:T(8,128)S(1)} collective-permute-done((f32[2048,128]{1,0:T(8,128)S(1)}, f32[2048,128]{1,0:T(8,128)S(1)}, u32[]{:S(2)}, u32[]{:S(2)}) %collective-permute-start.12) | collective-permute-done | bytes 1048608 | tf_op jit(solution)/shard_map/ppermute | solution.py:712
  69.7 12.2 %shard_map.83 = (f32[32,8,512]{2,1,0:T(8,128)S(1)}, f32[8,512]{1,0:T(8,128)S(1)}, f32[8,512]{1,0:T(8,128)S(1)}, f32[32,512]{1,0:T(8,128)S(1)}, f32[32,512]{1,0:T(8,128)S(1)}) custom-call(f32[2048,128]{1,0:T(8,128)S(1)} %bitcast.4, f32[2048,128]{1,0:T(8,128)S(1)} %collective-permute-done.12.oth, f32[16,8,256]{2,1,0:T(8,128)S(1)} %get-tuple-element.45.bw, ...), custom_call_target="tpu_custom_call" | custom-call | tf_op jit(solution)/shard_map/pallas_call | solution.py:35
  81.9 1.1 %collective-permute-start.15 = (f32[32,512]{1,0:T(8,128)S(1)}, f32[32,512]{1,0:T(8,128)S(1)}, u32[]{:S(2)}, u32[]{:S(2)}) collective-permute-start(f32[32,512]{1,0:T(8,128)S(1)} %get-tuple-element.54), channel_id=1, source_target_pairs={{0,1},{1,0},{2,3},{3,2},{4,5},{5,4},{6,7},{7,6},{8,9},{9,8},{10,11... | collective-permute-start | bytes 196616 | tf_op jit(solution)/shard_map/ppermute | solution.py:712
  83.0 3.1 %collective-permute-start.16 = (f32[32,512]{1,0:T(8,128)S(1)}, f32[32,512]{1,0:T(8,128)S(1)}, u32[]{:S(2)}, u32[]{:S(2)}) collective-permute-start(f32[32,512]{1,0:T(8,128)S(1)} %get-tuple-element.55), channel_id=1, source_target_pairs={{0,7},{1,2},{2,1},{3,4},{4,3},{5,6},{6,5},{7,0},{8,15},{9,10},{10,... | collective-permute-start | bytes 196616 | tf_op jit(solution)/shard_map/ppermute | solution.py:712
  86.1 1.0 %collective-permute-start.13 = (f32[8,512]{1,0:T(8,128)S(1)}, f32[8,512]{1,0:T(8,128)S(1)}, u32[]{:S(2)}, u32[]{:S(2)}) collective-permute-start(f32[8,512]{1,0:T(8,128)S(1)} %get-tuple-element.52), channel_id=1, source_target_pairs={{0,120},{8,16},{16,8},{24,32},{32,24},{40,48},{48,40},{56,64},{64,... | collective-permute-start | bytes 49160 | tf_op jit(solution)/shard_map/ppermute | solution.py:712
  87.1 5.8 %collective-permute-done.13.gx = f32[8,512]{1,0:T(8,128)S(1)} collective-permute-done((f32[8,512]{1,0:T(8,128)S(1)}, f32[8,512]{1,0:T(8,128)S(1)}, u32[]{:S(2)}, u32[]{:S(2)}) %collective-permute-start.13) | collective-permute-done | bytes 16416 | tf_op jit(solution)/shard_map/ppermute | solution.py:712
  92.9 1.6 %shard_map.84 = (f32[32,8,512]{2,1,0:T(8,128)}, f32[32,8,512]{2,1,0:T(8,128)}) custom-call(f32[32,8,512]{2,1,0:T(8,128)S(1)} %get-tuple-element.35.rhs_ref, f32[32,8,512]{2,1,0:T(8,128)S(1)} %get-tuple-element.51.v_ref, f32[32,8,512]{2,1,0:T(8,128)S(1)} %get-tuple-element.29.m0_ref.m_ref, f32[24,512]{1,0:T(8,128)S(1)} %collective-permute-done.ax, ...), custom_call_target="tpu_custom_call" | custom-call | tf_op jit(solution)/shard_map/pallas_call | solution.py:35
  (29 shorter events, 3.2 us)
Async XLA Ops:
  0.6 2.6 %copy-start = (f32[32,8,512]{2,1,0:T(8,128)S(1)}, f32[32,8,512]{2,1,0:T(8,128)}, u32[]{:S(2)}) copy-start(f32[32,8,512]{2,1,0:T(8,128)} %p_ref.3) | copy-start | bytes 1572868
  1.3 1.0 %copy-start.2 = (f32[32,8,512]{2,1,0:T(8,128)S(1)}, f32[32,8,512]{2,1,0:T(8,128)}, u32[]{:S(2)}) copy-start(f32[32,8,512]{2,1,0:T(8,128)} %void_ref.1) | copy-start | bytes 1572868
  3.2 0.7 copy-start.3
  3.9 12.0 %copy-start.1 = (f32[32,8,512]{2,1,0:T(8,128)S(1)}, f32[32,8,512]{2,1,0:T(8,128)}, u32[]{:S(2)}) copy-start(f32[32,8,512]{2,1,0:T(8,128)} %div_ref.1) | copy-start | bytes 1572868
  4.0 11.9 %collective-permute-start.2 = (f32[80,512]{1,0:T(8,128)S(1)}, f32[80,512]{1,0:T(8,128)S(1)}, u32[]{:S(2)}, u32[]{:S(2)}) collective-permute-start(f32[80,512]{1,0:T(8,128)S(1)} %get-tuple-element.33), channel_id=1, source_target_pairs={{0,1},{1,0},{2,3},{3,2},{4,5},{5,4},{6,7},{7,6},{8,9},{9,8},{10,11... | collective-permute-start | bytes 491528 | tf_op jit(solution)/shard_map/ppermute | solution.py:712
  6.1 9.8 %collective-permute-start.3 = (f32[80,512]{1,0:T(8,128)S(1)}, f32[80,512]{1,0:T(8,128)S(1)}, u32[]{:S(2)}, u32[]{:S(2)}) collective-permute-start(f32[80,512]{1,0:T(8,128)S(1)} %get-tuple-element.34), channel_id=1, source_target_pairs={{0,7},{1,2},{2,1},{3,4},{4,3},{5,6},{6,5},{7,0},{8,15},{9,10},{10,... | collective-permute-start | bytes 491528 | tf_op jit(solution)/shard_map/ppermute | solution.py:712
  8.7 7.2 %collective-permute-start = (f32[24,512]{1,0:T(8,128)S(1)}, f32[24,512]{1,0:T(8,128)S(1)}, u32[]{:S(2)}, u32[]{:S(2)}) collective-permute-start(f32[24,512]{1,0:T(8,128)S(1)} %get-tuple-element.31), channel_id=1, source_target_pairs={{0,120},{8,16},{16,8},{24,32},{32,24},{40,48},{48,40},{56,64},{64,... | collective-permute-start | bytes 147464 | tf_op jit(solution)/shard_map/ppermute | solution.py:712
  13.6 2.3 %copy-start.4 = (s32[128]{0:T(128)S(1)}, s32[128]{0:T(128)}, u32[]{:S(2)}) copy-start(s32[128]{0:T(128)} %param.11) | copy-start | bytes 1540
  13.6 2.3 %collective-permute-start.1 = (f32[24,512]{1,0:T(8,128)S(1)}, f32[24,512]{1,0:T(8,128)S(1)}, u32[]{:S(2)}, u32[]{:S(2)}) collective-permute-start(f32[24,512]{1,0:T(8,128)S(1)} %get-tuple-element.32), channel_id=1, source_target_pairs={{0,8},{8,0},{16,24},{24,16},{32,40},{40,32},{48,56},{56,48},{64,72... | collective-permute-start | bytes 147464 | tf_op jit(solution)/shard_map/ppermute | solution.py:712
  17.1 9.6 %collective-permute-start.6 = (f32[32,512]{1,0:T(8,128)S(1)}, f32[32,512]{1,0:T(8,128)S(1)}, u32[]{:S(2)}, u32[]{:S(2)}) collective-permute-start(f32[32,512]{1,0:T(8,128)S(1)} %get-tuple-element.39), channel_id=1, source_target_pairs={{0,1},{1,0},{2,3},{3,2},{4,5},{5,4},{6,7},{7,6},{8,9},{9,8},{10,11... | collective-permute-start | bytes 196616 | tf_op jit(solution)/shard_map/ppermute | solution.py:712
  18.2 8.6 %collective-permute-start.7 = (f32[32,512]{1,0:T(8,128)S(1)}, f32[32,512]{1,0:T(8,128)S(1)}, u32[]{:S(2)}, u32[]{:S(2)}) collective-permute-start(f32[32,512]{1,0:T(8,128)S(1)} %get-tuple-element.40), channel_id=1, source_target_pairs={{0,7},{1,2},{2,1},{3,4},{4,3},{5,6},{6,5},{7,0},{8,15},{9,10},{10,... | collective-permute-start | bytes 196616 | tf_op jit(solution)/shard_map/ppermute | solution.py:712
  19.9 6.8 %collective-permute-start.4 = (f32[8,512]{1,0:T(8,128)S(1)}, f32[8,512]{1,0:T(8,128)S(1)}, u32[]{:S(2)}, u32[]{:S(2)}) collective-permute-start(f32[8,512]{1,0:T(8,128)S(1)} %get-tuple-element.37), channel_id=1, source_target_pairs={{0,120},{8,16},{16,8},{24,32},{32,24},{40,48},{48,40},{56,64},{64,... | collective-permute-start | bytes 49160 | tf_op jit(solution)/shard_map/ppermute | solution.py:712
  24.0 2.7 %collective-permute-start.5 = (f32[8,512]{1,0:T(8,128)S(1)}, f32[8,512]{1,0:T(8,128)S(1)}, u32[]{:S(2)}, u32[]{:S(2)}) collective-permute-start(f32[8,512]{1,0:T(8,128)S(1)} %get-tuple-element.38), channel_id=1, source_target_pairs={{0,8},{8,0},{16,24},{24,16},{32,40},{40,32},{48,56},{56,48},{64,72... | collective-permute-start | bytes 49160 | tf_op jit(solution)/shard_map/ppermute | solution.py:712
  28.2 5.3 %collective-permute-start.8 = (f32[80,256]{1,0:T(8,128)S(1)}, f32[80,256]{1,0:T(8,128)S(1)}, u32[]{:S(2)}, u32[]{:S(2)}) collective-permute-start(f32[80,256]{1,0:T(8,128)S(1)} %get-tuple-element.43), channel_id=1, source_target_pairs={{0,1},{1,0},{2,3},{3,2},{4,5},{5,4},{6,7},{7,6},{8,9},{9,8},{10,11... | collective-permute-start | bytes 245768 | tf_op jit(solution)/shard_map/ppermute | solution.py:712
  29.0 6.6 %collective-permute-start.9 = (f32[80,256]{1,0:T(8,128)S(1)}, f32[80,256]{1,0:T(8,128)S(1)}, u32[]{:S(2)}, u32[]{:S(2)}) collective-permute-start(f32[80,256]{1,0:T(8,128)S(1)} %get-tuple-element.44), channel_id=1, source_target_pairs={{0,7},{1,2},{2,1},{3,4},{4,3},{5,6},{6,5},{7,0},{8,15},{9,10},{10,... | collective-permute-start | bytes 245768 | tf_op jit(solution)/shard_map/ppermute | solution.py:712
  35.7 7.1 %collective-permute-start.10 = (f32[40,256]{1,0:T(8,128)S(1)}, f32[40,256]{1,0:T(8,128)S(1)}, u32[]{:S(2)}, u32[]{:S(2)}) collective-permute-start(f32[40,256]{1,0:T(8,128)S(1)} %get-tuple-element.49), channel_id=1, source_target_pairs={{0,120},{8,16},{16,8},{24,32},{32,24},{40,48},{48,40},{56,64},{64,... | collective-permute-start | bytes 122888 | tf_op jit(solution)/shard_map/ppermute | solution.py:712
  38.4 4.4 %collective-permute-start.11 = (f32[40,256]{1,0:T(8,128)S(1)}, f32[40,256]{1,0:T(8,128)S(1)}, u32[]{:S(2)}, u32[]{:S(2)}) collective-permute-start(f32[40,256]{1,0:T(8,128)S(1)} %get-tuple-element.50), channel_id=1, source_target_pairs={{0,8},{8,0},{16,24},{24,16},{32,40},{40,32},{48,56},{56,48},{64,72... | collective-permute-start | bytes 122888 | tf_op jit(solution)/shard_map/ppermute | solution.py:712
  67.1 2.7 %collective-permute-start.12 = (f32[2048,128]{1,0:T(8,128)S(1)}, f32[2048,128]{1,0:T(8,128)S(1)}, u32[]{:S(2)}, u32[]{:S(2)}) collective-permute-start(f32[2048,128]{1,0:T(8,128)S(1)} %bitcast.3), channel_id=1, source_target_pairs={{0,8},{8,0},{16,24},{24,16},{32,40},{40,32},{48,56},{56,48},{64,72... | collective-permute-start | bytes 3145736 | tf_op jit(solution)/shard_map/ppermute | solution.py:712
  81.9 11.0 %collective-permute-start.15 = (f32[32,512]{1,0:T(8,128)S(1)}, f32[32,512]{1,0:T(8,128)S(1)}, u32[]{:S(2)}, u32[]{:S(2)}) collective-permute-start(f32[32,512]{1,0:T(8,128)S(1)} %get-tuple-element.54), channel_id=1, source_target_pairs={{0,1},{1,0},{2,3},{3,2},{4,5},{5,4},{6,7},{7,6},{8,9},{9,8},{10,11... | collective-permute-start | bytes 196616 | tf_op jit(solution)/shard_map/ppermute | solution.py:712
  83.0 9.8 %collective-permute-start.16 = (f32[32,512]{1,0:T(8,128)S(1)}, f32[32,512]{1,0:T(8,128)S(1)}, u32[]{:S(2)}, u32[]{:S(2)}) collective-permute-start(f32[32,512]{1,0:T(8,128)S(1)} %get-tuple-element.55), channel_id=1, source_target_pairs={{0,7},{1,2},{2,1},{3,4},{4,3},{5,6},{6,5},{7,0},{8,15},{9,10},{10,... | collective-permute-start | bytes 196616 | tf_op jit(solution)/shard_map/ppermute | solution.py:712
  86.1 6.8 %collective-permute-start.13 = (f32[8,512]{1,0:T(8,128)S(1)}, f32[8,512]{1,0:T(8,128)S(1)}, u32[]{:S(2)}, u32[]{:S(2)}) collective-permute-start(f32[8,512]{1,0:T(8,128)S(1)} %get-tuple-element.52), channel_id=1, source_target_pairs={{0,120},{8,16},{16,8},{24,32},{32,24},{40,48},{48,40},{56,64},{64,... | collective-permute-start | bytes 49160 | tf_op jit(solution)/shard_map/ppermute | solution.py:712
  87.1 5.8 %collective-permute-start.14 = (f32[8,512]{1,0:T(8,128)S(1)}, f32[8,512]{1,0:T(8,128)S(1)}, u32[]{:S(2)}, u32[]{:S(2)}) collective-permute-start(f32[8,512]{1,0:T(8,128)S(1)} %get-tuple-element.53), channel_id=1, source_target_pairs={{0,8},{8,0},{16,24},{24,16},{32,40},{40,32},{48,56},{56,48},{64,72... | collective-permute-start | bytes 49160 | tf_op jit(solution)/shard_map/ppermute | solution.py:712

commit v5 on v4

--- a/solution.py
+++ b/solution.py
@@ -305,7 +305,7 @@
 
 
 def restrict(
-    rhs_ref, v_ref, m_ref, m1_ref, ax, ac, az, ay, bx, bc, bz, by, b1_ref, v1_ref, sz, sy, pairs
+    rhs_ref, v_ref, m_ref, m1_ref, ax, ac, az, ay, bx, bc, bz, by, b1_ref, v1_ref, sx, sc, sz, sy, pairs
 ):
     ah, bh = Halo(ax, ac, az, ay), Halo(bx, bc, bz, by)
     m_of, mb, ma = fine_mobility(m_ref, ah)
@@ -337,8 +337,9 @@
         v1_ref[i] = OMEGA * b1_ref[i] / diagonal
 
     level1_walk(m1_of, None, 0, A1, emit1)
-    g = lax.axis_index("gz")
+    a, g = position()
     for layer in range(2):
+        c_plane = jnp.where(a % 2 == 0, A1 - 1 - layer, layer)
         z_row = jnp.where(g % 2 == 0, H1 + 1 - layer, 2 + layer)
         y_row = H1 + 3 - z_row
         sources = (v1_ref, m1_ref) if layer else (v1_ref, m1_ref, b1_ref)
@@ -347,13 +348,14 @@
                 at = (2 * n + layer) * A1 + i
                 sz[at : at + 1, :] = ref[i, pl.ds(z_row, 1), :]
                 sy[at : at + 1, :] = ref[i, pl.ds(y_row, 1), :]
-
-
-def widen(b1_ref, v1_ref, m1_ref, z_ref, y_ref, vw, mw, bw, sx, sc):
-    a, g = position()
+            at = (2 * n + layer) * T1
+            sc[at : at + T1, :] = ref[c_plane]
+            sx[at : at + T1, :] = ref[A1 - 1 - c_plane]
+
+
+def widen(pairs, halo):
     sub = iota((T1, R1), 0)
-    halo = Halo(None, None, z_ref, y_ref)
-    for n, (src, dst) in enumerate(((v1_ref, vw), (m1_ref, mw), (b1_ref, bw))):
+    for n, (src, dst) in enumerate(pairs):
         for i in range(A1):
             tile = src[i]
             for layer in range(2 if n < 2 else 1):
@@ -362,16 +364,13 @@
                 tile = jnp.where(sub == 1 - layer, halo.below(at, ALL), tile)
                 tile = jnp.where(sub == H1 + 2 + layer, halo.above(at, ALL), tile)
             dst[i] = tile
-    for layer in range(2):
-        c_plane = jnp.where(a % 2 == 0, A1 - 1 - layer, layer)
-        x_plane = A1 - 1 - c_plane
-        for n, ref in enumerate((vw, mw) if layer else (vw, mw, bw)):
-            at = (2 * n + layer) * T1
-            sc[at : at + T1, :] = ref[c_plane]
-            sx[at : at + T1, :] = ref[x_plane]
-
-
-def wide_planes(ref, halo, n, i):
+
+
+def wide_planes(ref, halo, n, i, corners=None):
+    if corners is not None and i == -1:
+        return corners.prev(slice(n * T1, (n + 1) * T1), ALL)
+    if corners is not None and i == A1:
+        return corners.next(slice(n * T1, (n + 1) * T1), ALL)
     if i < 0:
         at = (2 * n - 1 - i) * T1
         return halo.prev(slice(at, at + T1), ALL)
@@ -381,8 +380,15 @@
     return ref[i]
 
 
-def restrict1(bw, vw, mw, m2_ref, cx, cc, out_ref, halves):
-    halo = Halo(cx, cc, None, None)
+def restrict1(
+    b1_ref, v1_ref, m1_ref, m2_ref, cx, cc, cz, cy, out_ref, bw, vw, mw, sx, sc, halves
+):
+    halo = Halo(cx, cc, cz, cy)
+    widen(((v1_ref, vw), (m1_ref, mw), (b1_ref, bw)), halo)
+    c_plane = jnp.where(lax.axis_index("az") % 2 == 0, A1 - 1, 0)
+    for n, ref in enumerate((vw, mw)):
+        sc[n * T1 : (n + 1) * T1, :] = ref[c_plane]
+        sx[n * T1 : (n + 1) * T1, :] = ref[A1 - 1 - c_plane]
     kept = []
 
     def emit(i, diagonal, around, centre):
@@ -531,7 +537,7 @@
 
 
 def coarse(
-    own, oth, bw, vw, mw, cx, cc, rhs_ref, v_ref, m_ref, ax, ac, az, ay, bx, bc, bz, by,
+    own, oth, bw, vw, mw, cx, cc, kx, kc, rhs_ref, v_ref, m_ref, ax, ac, az, ay, bx, bc, bz, by,
     out_ref, sx, sc, sz, sy,
     m2, d2, w3, sum_m, m3, b2, v2, sum_r, add, va, vb, e2, v2f, src, v1f, e_ref,
 ):
@@ -635,18 +641,18 @@
             src[4 * j + q : 4 * j + q + 1, :] = v2f[j, p, pl.ds(row, 1), :]
     o, c = iota((8 * (A2 + 2), 4 * (A2 + 2)), 0), iota((8 * (A2 + 2), 4 * (A2 + 2)), 1)
     e1 = dot(hot(o // 2 == c), dot(src[...], dup_cols(R2)))
-    halo = Halo(cx, cc, None, None)
+    halo, corners = Halo(cx, cc, None, None), Halo(kx, kc, None, None)
 
     def v1_of(i):
         j = (i + 2) // 2
-        return wide_planes(vw, halo, 0, i) + e1[T1 * j : T1 * (j + 1)]
+        return wide_planes(vw, halo, 0, i, corners) + e1[T1 * j : T1 * (j + 1)]
 
     def emit1(i, diagonal, around, centre):
         b = wide_planes(bw, halo, 2, i)
         at = (i + 1) * T1
         v1f[at : at + T1, :] = (1.0 - OMEGA) * centre + OMEGA * (b + around) / diagonal
 
-    level1_walk(lambda i: wide_planes(mw, halo, 1, i), v1_of, -1, A1 + 2, emit1)
+    level1_walk(lambda i: wide_planes(mw, halo, 1, i, corners), v1_of, -1, A1 + 2, emit1)
 
     own_rows = (A1 + 2) * NH
     shape = (own_rows + 2 * A1, (A1 + 2) * T1)
@@ -716,11 +722,12 @@
     return swap(sx, "az", 1), swap(sc, "az", 0), swap(sz, "gz", 0), swap(sy, "gz", 1)
 
 
-def gathered(x):
+def gathered(x, sides):
     groups = [[a * N_GZ + g for a in range(c, N_AZ, 2) for g in range(N_GZ)] for c in range(2)]
     own = lax.all_to_all(x, ("az", "gz"), 0, 0, tiled=True, axis_index_groups=groups)
     own = own.reshape(own.shape[0] * own.shape[1], own.shape[2])
-    return own, swap(own, "az", 0)
+    own, *sides = lax.optimization_barrier((own, *sides))
+    return own, swap(own, "az", 0), sides
 
 
 def faces(planes, rows, width):
@@ -753,26 +760,28 @@
         presmooth, [block, block] + faces(NH, NA, NR), (pressure, divergence, m0, cell, *ha)
     )
     hb = exchange(*send)
-    b1, v1, sz, sy = call(
+    b1, v1, *send = call(
         restrict,
-        [wide, wide] + [struct(5 * A1, R1)] * 2,
+        [wide, wide] + faces(5 * T1, 5 * A1, R1),
         (rhs, v0, m0, m1, *ha, *hb),
         [pairs],
     )
-    v1, m1, b1, sx, sc = call(
-        widen,
-        [wide, wide, wide] + [struct(5 * T1, R1)] * 2,
-        (b1, v1, m1, swap(sz, "gz", 0), swap(sy, "gz", 1)),
-    )
-    hc = swap(sx, "az", 1), swap(sc, "az", 0)
-    (copies,) = call(restrict1, [struct(64, 2 * A2 * H2, R2)], (b1, v1, m1, m2, *hc), [halves])
+    hc = exchange(*send)
+    copies, b1, v1, m1, kx, kc = call(
+        restrict1,
+        [struct(64, 2 * A2 * H2, R2), wide, wide, wide] + [struct(2 * T1, R1)] * 2,
+        (b1, v1, m1, m2, *hc),
+        [halves],
+    )
+    corners = swap(kx, "az", 1), swap(kc, "az", 0)
+    own, oth, corners = gathered(copies, corners)
     ring = vmem(AZ2 + 4, 2, G2, R2)
     ends = vmem(HALF + 2, G2, R2)
     third = vmem(AZ3, G2, R2)
     out, *send = call(
         coarse,
         [block] + faces(NH, NA, NR),
-        (*gathered(copies), b1, v1, m1, *hc, rhs, v0, m0, *ha, *hb),
+        (own, oth, b1, v1, m1, *hc[:2], *corners, rhs, v0, m0, *ha, *hb),
         [
             ring,
             ring,

time: 94.8 us -> 98 us (1.034)
  blocking collectives: 23.7 us -> 0 us
  starting transfers between devices: 26.9 us -> 40 us
  local copies, waits for them, and re-layouts: 1.71 us -> 8.74 us
  waiting for transfers between devices: 22.7 us -> 29.1 us
    all_to_all x1 -> x0, blocking collectives: 23.7 us -> none  [gathered(): lax.all_to_all(x, ('az', 'gz'), 0, 0, tiled=True, axis_index_groups=groups)]
    all_to_all x0 -> x1, starting transfers between devices: none -> 7.3 us  [gathered(): lax.all_to_all(x, ('az', 'gz'), 0, 0, tiled=True, axis_index_groups=groups)]
    unnamed x10 -> x32, local copies, waits for them, and re-layouts: 1.71 us -> 8.74 us
    ppermute x17 -> x19, waiting for transfers between devices: 22.7 us -> 29.1 us  [swap(): return lax.ppermute(x, axis, pairs)]
    ppermute x17 -> x19, starting transfers between devices: 26.9 us -> 32.7 us  [swap(): return lax.ppermute(x, axis, pairs)]
    pallas_call x8 -> x7, Pallas kernels: 18.1 us -> 18 us  [call(): pl.pallas_call(kernel, out_shape=outs, in_specs=specs, out_specs=[pl.Bloc...]
  transfers between devices with their start and end apart: 17 -> 20, of which waited for: 7 -> 7; matrix products, arithmetic and copies ran while one was open for 0% -> 0% of each run, Pallas kernels for 0% -> 0%
where the time goes in v5:
time: 98 us; the launch traced here: 97.5 us
  starting transfers between devices  40 us (41%)
  waiting for transfers between devices  29.1 us (30%)
  Pallas kernels  18 us (18%)
  local copies, waits for them, and re-layouts  8.74 us (9%)
  between operations  1.61 us (2%)
    ppermute x19, starting transfers between devices, swap(): return lax.ppermute(x, axis, pairs)  32.7 us
    ppermute x19, waiting for transfers between devices, swap(): return lax.ppermute(x, axis, pairs)  29.1 us
    pallas_call x7, Pallas kernels, call(): pl.pallas_call(kernel, out_shape=outs, in_specs=specs, out_specs=[pl.Bloc...  18 us
    unnamed x32, local copies, waits for them, and re-layouts  8.74 us
    all_to_all x1, starting transfers between devices, gathered(): lax.all_to_all(x, ('az', 'gz'), 0, 0, tiled=True, axis_index_groups=groups)  7.3 us
  transfers between devices with their start and end apart: 20, of which 7 were waited for; matrix products, arithmetic and copies ran while one was open for 0% of the time, Pallas kernels for 0%

profile of v5, /device:TPU:0, one launch (start us, length us, event | category | flops | bytes accessed | tf_op | source)
XLA Modules:
  0.0 97.5 jit_solution(8501818093182535586)
XLA Ops:
  1.4 1.0 %copy-done.3 = f32[32,8,512]{2,1,0:T(8,128)S(1)} copy-done((f32[32,8,512]{2,1,0:T(8,128)S(1)}, f32[32,8,512]{2,1,0:T(8,128)}, u32[]{:S(2)}) %copy-start.3) | copy-done | bytes 524312
  4.0 2.1 %collective-permute-start.2 = (f32[80,512]{1,0:T(8,128)S(1)}, f32[80,512]{1,0:T(8,128)S(1)}, u32[]{:S(2)}, u32[]{:S(2)}) collective-permute-start(f32[80,512]{1,0:T(8,128)S(1)} %get-tuple-element.39), channel_id=1, source_target_pairs={{0,1},{1,0},{2,3},{3,2},{4,5},{5,4},{6,7},{7,6},{8,9},{9,8},{10,11... | collective-permute-start | bytes 491528 | tf_op jit(solution)/shard_map/ppermute | solution.py:718
  6.1 2.6 %collective-permute-start.3 = (f32[80,512]{1,0:T(8,128)S(1)}, f32[80,512]{1,0:T(8,128)S(1)}, u32[]{:S(2)}, u32[]{:S(2)}) collective-permute-start(f32[80,512]{1,0:T(8,128)S(1)} %get-tuple-element.40), channel_id=1, source_target_pairs={{0,7},{1,2},{2,1},{3,4},{4,3},{5,6},{6,5},{7,0},{8,15},{9,10},{10,... | collective-permute-start | bytes 491528 | tf_op jit(solution)/shard_map/ppermute | solution.py:718
  8.7 5.0 %collective-permute-start = (f32[24,512]{1,0:T(8,128)S(1)}, f32[24,512]{1,0:T(8,128)S(1)}, u32[]{:S(2)}, u32[]{:S(2)}) collective-permute-start(f32[24,512]{1,0:T(8,128)S(1)} %get-tuple-element.37), channel_id=1, source_target_pairs={{0,120},{8,16},{16,8},{24,32},{32,24},{40,48},{48,40},{56,64},{64,... | collective-permute-start | bytes 147464 | tf_op jit(solution)/shard_map/ppermute | solution.py:718
  13.6 2.3 %collective-permute-done.ax = f32[24,512]{1,0:T(8,128)S(1)} collective-permute-done((f32[24,512]{1,0:T(8,128)S(1)}, f32[24,512]{1,0:T(8,128)S(1)}, u32[]{:S(2)}, u32[]{:S(2)}) %collective-permute-start) | collective-permute-done | bytes 49184 | tf_op jit(solution)/shard_map/ppermute | solution.py:718
  15.9 1.2 %shard_map.79 = (f32[32,8,512]{2,1,0:T(8,128)S(1)}, f32[32,8,512]{2,1,0:T(8,128)S(1)}, f32[8,512]{1,0:T(8,128)S(1)}, f32[8,512]{1,0:T(8,128)S(1)}, f32[32,512]{1,0:T(8,128)S(1)}, /*index=5*/f32[32,512]{1,0:T(8,128)S(1)}) custom-call(f32[32,8,512]{2,1,0:T(8,128)S(1)} %copy-done, f32[32,8,512]{2,1,0:T(8,128)S(1)} %copy-done.2, ...), custom_call_target="tpu_custom_call" | custom-call | tf_op jit(solution)/shard_map/pallas_call | solution.py:35
  17.1 1.0 %collective-permute-start.6 = (f32[32,512]{1,0:T(8,128)S(1)}, f32[32,512]{1,0:T(8,128)S(1)}, u32[]{:S(2)}, u32[]{:S(2)}) collective-permute-start(f32[32,512]{1,0:T(8,128)S(1)} %get-tuple-element.45), channel_id=1, source_target_pairs={{0,1},{1,0},{2,3},{3,2},{4,5},{5,4},{6,7},{7,6},{8,9},{9,8},{10,11... | collective-permute-start | bytes 196616 | tf_op jit(solution)/shard_map/ppermute | solution.py:718
  18.1 1.8 %collective-permute-start.7 = (f32[32,512]{1,0:T(8,128)S(1)}, f32[32,512]{1,0:T(8,128)S(1)}, u32[]{:S(2)}, u32[]{:S(2)}) collective-permute-start(f32[32,512]{1,0:T(8,128)S(1)} %get-tuple-element.46), channel_id=1, source_target_pairs={{0,7},{1,2},{2,1},{3,4},{4,3},{5,6},{6,5},{7,0},{8,15},{9,10},{10,... | collective-permute-start | bytes 196616 | tf_op jit(solution)/shard_map/ppermute | solution.py:718
  19.9 4.1 %collective-permute-start.4 = (f32[8,512]{1,0:T(8,128)S(1)}, f32[8,512]{1,0:T(8,128)S(1)}, u32[]{:S(2)}, u32[]{:S(2)}) collective-permute-start(f32[8,512]{1,0:T(8,128)S(1)} %get-tuple-element.43), channel_id=1, source_target_pairs={{0,120},{8,16},{16,8},{24,32},{32,24},{40,48},{48,40},{56,64},{64,... | collective-permute-start | bytes 49160 | tf_op jit(solution)/shard_map/ppermute | solution.py:718
  24.0 2.7 %collective-permute-done.4.bx = f32[8,512]{1,0:T(8,128)S(1)} collective-permute-done((f32[8,512]{1,0:T(8,128)S(1)}, f32[8,512]{1,0:T(8,128)S(1)}, u32[]{:S(2)}, u32[]{:S(2)}) %collective-permute-start.4) | collective-permute-done | bytes 16416 | tf_op jit(solution)/shard_map/ppermute | solution.py:718
  26.7 1.5 %shard_map.80 = (f32[16,8,256]{2,1,0:T(8,128)S(1)}, f32[16,8,256]{2,1,0:T(8,128)S(1)}, f32[40,256]{1,0:T(8,128)S(1)}, f32[40,256]{1,0:T(8,128)S(1)}, f32[80,256]{1,0:T(8,128)S(1)}, /*index=5*/f32[80,256]{1,0:T(8,128)S(1)}) custom-call(f32[32,8,512]{2,1,0:T(8,128)S(1)} %get-tuple-element.41.rhs_ref, f32[32,8,512]{2,1,0:T(8,128)S(1)} %get-tuple-element.42.v_ref, ...), custom_call_target="tpu_custom_call" | custom-call | tf_op jit(solution)/shard_map/pallas_call | solution.py:35
  29.0 1.7 %collective-permute-start.11 = (f32[80,256]{1,0:T(8,128)S(1)}, f32[80,256]{1,0:T(8,128)S(1)}, u32[]{:S(2)}, u32[]{:S(2)}) collective-permute-start(f32[80,256]{1,0:T(8,128)S(1)} %get-tuple-element.53), channel_id=1, source_target_pairs={{0,7},{1,2},{2,1},{3,4},{4,3},{5,6},{6,5},{7,0},{8,15},{9,10},{10,... | collective-permute-start | bytes 245768 | tf_op jit(solution)/shard_map/ppermute | solution.py:718
  30.7 3.5 %collective-permute-start.8 = (f32[40,256]{1,0:T(8,128)S(1)}, f32[40,256]{1,0:T(8,128)S(1)}, u32[]{:S(2)}, u32[]{:S(2)}) collective-permute-start(f32[40,256]{1,0:T(8,128)S(1)} %get-tuple-element.50), channel_id=1, source_target_pairs={{0,120},{8,16},{16,8},{24,32},{32,24},{40,48},{48,40},{56,64},{64,... | collective-permute-start | bytes 122888 | tf_op jit(solution)/shard_map/ppermute | solution.py:718
  34.2 3.7 %collective-permute-done.8.cx = f32[40,256]{1,0:T(8,128)S(1)} collective-permute-done((f32[40,256]{1,0:T(8,128)S(1)}, f32[40,256]{1,0:T(8,128)S(1)}, u32[]{:S(2)}, u32[]{:S(2)}) %collective-permute-start.8) | collective-permute-done | bytes 40992 | tf_op jit(solution)/shard_map/ppermute | solution.py:718
  38.6 1.0 %copy-done.1 = f32[64,32,128]{2,1,0:T(8,128)} copy-done((f32[64,32,128]{2,1,0:T(8,128)}, f32[64,32,128]{2,1,0:T(8,128)S(1)}, u32[]{:S(2)}) %copy-start.1) | copy-done | bytes 1048600
  42.1 7.3 %all-to-all-start = ((f32[64,32,128]{2,1,0:T(8,128)}), f32[64,32,128]{2,1,0:T(8,128)S(1)}, u32[]{:S(2)}, u32[]{:S(2)}) async-start(f32[64,32,128]{2,1,0:T(8,128)} %copy-done.1), calls=%async_computation | async-start | bytes 2097152 | tf_op jit(solution)/shard_map/all_to_all | solution.py:727
  49.4 4.9 %collective-permute-start.12 = (f32[16,256]{1,0:T(8,128)}, f32[16,256]{1,0:T(8,128)S(1)}, u32[]{:S(2)}, u32[]{:S(2)}) collective-permute-start(f32[16,256]{1,0:T(8,128)} %copy-done.15), channel_id=1, source_target_pairs={{0,120},{8,16},{16,8},{24,32},{32,24},{40,48},{48,40},{56,64},{64,... | collective-permute-start | bytes 49160 | tf_op jit(solution)/shard_map/ppermute | solution.py:718
  54.3 11.7 %collective-permute-done.12.kx = f32[16,256]{1,0:T(8,128)S(1)} collective-permute-done((f32[16,256]{1,0:T(8,128)}, f32[16,256]{1,0:T(8,128)S(1)}, u32[]{:S(2)}, u32[]{:S(2)}) %collective-permute-start.12) | collective-permute-done | bytes 16416 | tf_op jit(solution)/shard_map/ppermute | solution.py:718
  67.3 2.7 %collective-permute-done.14.oth = f32[2048,128]{1,0:T(8,128)S(1)} collective-permute-done((f32[2048,128]{1,0:T(8,128)S(1)}, f32[2048,128]{1,0:T(8,128)S(1)}, u32[]{:S(2)}, u32[]{:S(2)}) %collective-permute-start.14) | collective-permute-done | bytes 1048608 | tf_op jit(solution)/shard_map/ppermute | solution.py:718
  72.3 12.2 %shard_map.82 = (f32[32,8,512]{2,1,0:T(8,128)S(1)}, f32[8,512]{1,0:T(8,128)S(1)}, f32[8,512]{1,0:T(8,128)S(1)}, f32[32,512]{1,0:T(8,128)S(1)}, f32[32,512]{1,0:T(8,128)S(1)}) custom-call(f32[2048,128]{1,0:T(8,128)S(1)} %bitcast.4, f32[2048,128]{1,0:T(8,128)S(1)} %collective-permute-done.14.oth, f32[16,8,256]{2,1,0:T(8,128)S(1)} %get-tuple-element.58.bw, ...), custom_call_target="tpu_custom_call" | custom-call | tf_op jit(solution)/shard_map/pallas_call | solution.py:35
  84.5 1.1 %collective-permute-start.17 = (f32[32,512]{1,0:T(8,128)S(1)}, f32[32,512]{1,0:T(8,128)S(1)}, u32[]{:S(2)}, u32[]{:S(2)}) collective-permute-start(f32[32,512]{1,0:T(8,128)S(1)} %get-tuple-element.66), channel_id=1, source_target_pairs={{0,1},{1,0},{2,3},{3,2},{4,5},{5,4},{6,7},{7,6},{8,9},{9,8},{10,11... | collective-permute-start | bytes 196616 | tf_op jit(solution)/shard_map/ppermute | solution.py:718
  85.6 3.4 %collective-permute-start.18 = (f32[32,512]{1,0:T(8,128)S(1)}, f32[32,512]{1,0:T(8,128)S(1)}, u32[]{:S(2)}, u32[]{:S(2)}) collective-permute-start(f32[32,512]{1,0:T(8,128)S(1)} %get-tuple-element.67), channel_id=1, source_target_pairs={{0,7},{1,2},{2,1},{3,4},{4,3},{5,6},{6,5},{7,0},{8,15},{9,10},{10,... | collective-permute-start | bytes 196616 | tf_op jit(solution)/shard_map/ppermute | solution.py:718
  89.8 5.9 %collective-permute-done.15.gx = f32[8,512]{1,0:T(8,128)S(1)} collective-permute-done((f32[8,512]{1,0:T(8,128)S(1)}, f32[8,512]{1,0:T(8,128)S(1)}, u32[]{:S(2)}, u32[]{:S(2)}) %collective-permute-start.15) | collective-permute-done | bytes 16416 | tf_op jit(solution)/shard_map/ppermute | solution.py:718
  95.8 1.6 %shard_map.83 = (f32[32,8,512]{2,1,0:T(8,128)}, f32[32,8,512]{2,1,0:T(8,128)}) custom-call(f32[32,8,512]{2,1,0:T(8,128)S(1)} %get-tuple-element.41.rhs_ref, f32[32,8,512]{2,1,0:T(8,128)S(1)} %get-tuple-element.63.v_ref, f32[32,8,512]{2,1,0:T(8,128)S(1)} %get-tuple-element.35.m0_ref.m_ref, f32[24,512]{1,0:T(8,128)S(1)} %collective-permute-done.ax, ...), custom_call_target="tpu_custom_call" | custom-call | tf_op jit(solution)/shard_map/pallas_call | solution.py:35
  (55 shorter events, 10.1 us)
Async XLA Ops:
  0.6 2.6 %copy-start = (f32[32,8,512]{2,1,0:T(8,128)S(1)}, f32[32,8,512]{2,1,0:T(8,128)}, u32[]{:S(2)}) copy-start(f32[32,8,512]{2,1,0:T(8,128)} %p_ref.3) | copy-start | bytes 1572868
  3.9 12.0 %copy-start.2 = (f32[32,8,512]{2,1,0:T(8,128)S(1)}, f32[32,8,512]{2,1,0:T(8,128)}, u32[]{:S(2)}) copy-start(f32[32,8,512]{2,1,0:T(8,128)} %div_ref.1) | copy-start | bytes 1572868
  4.0 11.9 %collective-permute-start.2 = (f32[80,512]{1,0:T(8,128)S(1)}, f32[80,512]{1,0:T(8,128)S(1)}, u32[]{:S(2)}, u32[]{:S(2)}) collective-permute-start(f32[80,512]{1,0:T(8,128)S(1)} %get-tuple-element.39), channel_id=1, source_target_pairs={{0,1},{1,0},{2,3},{3,2},{4,5},{5,4},{6,7},{7,6},{8,9},{9,8},{10,11... | collective-permute-start | bytes 491528 | tf_op jit(solution)/shard_map/ppermute | solution.py:718
  6.1 9.8 %collective-permute-start.3 = (f32[80,512]{1,0:T(8,128)S(1)}, f32[80,512]{1,0:T(8,128)S(1)}, u32[]{:S(2)}, u32[]{:S(2)}) collective-permute-start(f32[80,512]{1,0:T(8,128)S(1)} %get-tuple-element.40), channel_id=1, source_target_pairs={{0,7},{1,2},{2,1},{3,4},{4,3},{5,6},{6,5},{7,0},{8,15},{9,10},{10,... | collective-permute-start | bytes 491528 | tf_op jit(solution)/shard_map/ppermute | solution.py:718
  8.7 7.2 %collective-permute-start = (f32[24,512]{1,0:T(8,128)S(1)}, f32[24,512]{1,0:T(8,128)S(1)}, u32[]{:S(2)}, u32[]{:S(2)}) collective-permute-start(f32[24,512]{1,0:T(8,128)S(1)} %get-tuple-element.37), channel_id=1, source_target_pairs={{0,120},{8,16},{16,8},{24,32},{32,24},{40,48},{48,40},{56,64},{64,... | collective-permute-start | bytes 147464 | tf_op jit(solution)/shard_map/ppermute | solution.py:718
  13.6 2.3 %copy-start.13 = (s32[128]{0:T(128)S(1)}, s32[128]{0:T(128)}, u32[]{:S(2)}) copy-start(s32[128]{0:T(128)} %param.11) | copy-start | bytes 1540
  13.6 2.3 %collective-permute-start.1 = (f32[24,512]{1,0:T(8,128)S(1)}, f32[24,512]{1,0:T(8,128)S(1)}, u32[]{:S(2)}, u32[]{:S(2)}) collective-permute-start(f32[24,512]{1,0:T(8,128)S(1)} %get-tuple-element.38), channel_id=1, source_target_pairs={{0,8},{8,0},{16,24},{24,16},{32,40},{40,32},{48,56},{56,48},{64,72... | collective-permute-start | bytes 147464 | tf_op jit(solution)/shard_map/ppermute | solution.py:718
  17.1 9.6 %collective-permute-start.6 = (f32[32,512]{1,0:T(8,128)S(1)}, f32[32,512]{1,0:T(8,128)S(1)}, u32[]{:S(2)}, u32[]{:S(2)}) collective-permute-start(f32[32,512]{1,0:T(8,128)S(1)} %get-tuple-element.45), channel_id=1, source_target_pairs={{0,1},{1,0},{2,3},{3,2},{4,5},{5,4},{6,7},{7,6},{8,9},{9,8},{10,11... | collective-permute-start | bytes 196616 | tf_op jit(solution)/shard_map/ppermute | solution.py:718
  18.1 8.6 %collective-permute-start.7 = (f32[32,512]{1,0:T(8,128)S(1)}, f32[32,512]{1,0:T(8,128)S(1)}, u32[]{:S(2)}, u32[]{:S(2)}) collective-permute-start(f32[32,512]{1,0:T(8,128)S(1)} %get-tuple-element.46), channel_id=1, source_target_pairs={{0,7},{1,2},{2,1},{3,4},{4,3},{5,6},{6,5},{7,0},{8,15},{9,10},{10,... | collective-permute-start | bytes 196616 | tf_op jit(solution)/shard_map/ppermute | solution.py:718
  19.9 6.8 %collective-permute-start.4 = (f32[8,512]{1,0:T(8,128)S(1)}, f32[8,512]{1,0:T(8,128)S(1)}, u32[]{:S(2)}, u32[]{:S(2)}) collective-permute-start(f32[8,512]{1,0:T(8,128)S(1)} %get-tuple-element.43), channel_id=1, source_target_pairs={{0,120},{8,16},{16,8},{24,32},{32,24},{40,48},{48,40},{56,64},{64,... | collective-permute-start | bytes 49160 | tf_op jit(solution)/shard_map/ppermute | solution.py:718
  24.0 2.7 %collective-permute-start.5 = (f32[8,512]{1,0:T(8,128)S(1)}, f32[8,512]{1,0:T(8,128)S(1)}, u32[]{:S(2)}, u32[]{:S(2)}) collective-permute-start(f32[8,512]{1,0:T(8,128)S(1)} %get-tuple-element.44), channel_id=1, source_target_pairs={{0,8},{8,0},{16,24},{24,16},{32,40},{40,32},{48,56},{56,48},{64,72... | collective-permute-start | bytes 49160 | tf_op jit(solution)/shard_map/ppermute | solution.py:718
  28.2 9.7 %collective-permute-start.10 = (f32[80,256]{1,0:T(8,128)S(1)}, f32[80,256]{1,0:T(8,128)S(1)}, u32[]{:S(2)}, u32[]{:S(2)}) collective-permute-start(f32[80,256]{1,0:T(8,128)S(1)} %get-tuple-element.52), channel_id=1, source_target_pairs={{0,1},{1,0},{2,3},{3,2},{4,5},{5,4},{6,7},{7,6},{8,9},{9,8},{10,11... | collective-permute-start | bytes 245768 | tf_op jit(solution)/shard_map/ppermute | solution.py:718
  29.0 8.9 %collective-permute-start.11 = (f32[80,256]{1,0:T(8,128)S(1)}, f32[80,256]{1,0:T(8,128)S(1)}, u32[]{:S(2)}, u32[]{:S(2)}) collective-permute-start(f32[80,256]{1,0:T(8,128)S(1)} %get-tuple-element.53), channel_id=1, source_target_pairs={{0,7},{1,2},{2,1},{3,4},{4,3},{5,6},{6,5},{7,0},{8,15},{9,10},{10,... | collective-permute-start | bytes 245768 | tf_op jit(solution)/shard_map/ppermute | solution.py:718
  30.7 7.2 %collective-permute-start.8 = (f32[40,256]{1,0:T(8,128)S(1)}, f32[40,256]{1,0:T(8,128)S(1)}, u32[]{:S(2)}, u32[]{:S(2)}) collective-permute-start(f32[40,256]{1,0:T(8,128)S(1)} %get-tuple-element.50), channel_id=1, source_target_pairs={{0,120},{8,16},{16,8},{24,32},{32,24},{40,48},{48,40},{56,64},{64,... | collective-permute-start | bytes 122888 | tf_op jit(solution)/shard_map/ppermute | solution.py:718
  34.2 3.7 %collective-permute-start.9 = (f32[40,256]{1,0:T(8,128)S(1)}, f32[40,256]{1,0:T(8,128)S(1)}, u32[]{:S(2)}, u32[]{:S(2)}) collective-permute-start(f32[40,256]{1,0:T(8,128)S(1)} %get-tuple-element.51), channel_id=1, source_target_pairs={{0,8},{8,0},{16,24},{24,16},{32,40},{40,32},{48,56},{56,48},{64,72... | collective-permute-start | bytes 122888 | tf_op jit(solution)/shard_map/ppermute | solution.py:718
  42.1 27.9 %copy-start.5 = (f32[16,8,256]{2,1,0:T(8,128)S(1)}, f32[16,8,256]{2,1,0:T(8,128)}, u32[]{:S(2)}) copy-start(f32[16,8,256]{2,1,0:T(8,128)} %copy-done.4) | copy-start | bytes 393220
  42.1 25.3 %all-to-all-start = ((f32[64,32,128]{2,1,0:T(8,128)}), f32[64,32,128]{2,1,0:T(8,128)S(1)}, u32[]{:S(2)}, u32[]{:S(2)}) async-start(f32[64,32,128]{2,1,0:T(8,128)} %copy-done.1), calls=%async_computation | async-start | bytes 2097152 | tf_op jit(solution)/shard_map/all_to_all | solution.py:727
  49.4 16.7 %collective-permute-start.12 = (f32[16,256]{1,0:T(8,128)}, f32[16,256]{1,0:T(8,128)S(1)}, u32[]{:S(2)}, u32[]{:S(2)}) collective-permute-start(f32[16,256]{1,0:T(8,128)} %copy-done.15), channel_id=1, source_target_pairs={{0,120},{8,16},{16,8},{24,32},{32,24},{40,48},{48,40},{56,64},{64,... | collective-permute-start | bytes 49160 | tf_op jit(solution)/shard_map/ppermute | solution.py:718
  54.3 12.3 %collective-permute-start.13 = (f32[16,256]{1,0:T(8,128)}, f32[16,256]{1,0:T(8,128)S(1)}, u32[]{:S(2)}, u32[]{:S(2)}) collective-permute-start(f32[16,256]{1,0:T(8,128)} %copy-done.14), channel_id=1, source_target_pairs={{0,8},{8,0},{16,24},{24,16},{32,40},{40,32},{48,56},{56,48},{64,72... | collective-permute-start | bytes 49160 | tf_op jit(solution)/shard_map/ppermute | solution.py:718
  67.3 2.7 %collective-permute-start.14 = (f32[2048,128]{1,0:T(8,128)S(1)}, f32[2048,128]{1,0:T(8,128)S(1)}, u32[]{:S(2)}, u32[]{:S(2)}) collective-permute-start(f32[2048,128]{1,0:T(8,128)S(1)} %bitcast.3), channel_id=1, source_target_pairs={{0,8},{8,0},{16,24},{24,16},{32,40},{40,32},{48,56},{56,48},{64,72... | collective-permute-start | bytes 3145736 | tf_op jit(solution)/shard_map/ppermute | solution.py:718
  84.5 11.3 %collective-permute-start.17 = (f32[32,512]{1,0:T(8,128)S(1)}, f32[32,512]{1,0:T(8,128)S(1)}, u32[]{:S(2)}, u32[]{:S(2)}) collective-permute-start(f32[32,512]{1,0:T(8,128)S(1)} %get-tuple-element.66), channel_id=1, source_target_pairs={{0,1},{1,0},{2,3},{3,2},{4,5},{5,4},{6,7},{7,6},{8,9},{9,8},{10,11... | collective-permute-start | bytes 196616 | tf_op jit(solution)/shard_map/ppermute | solution.py:718
  85.6 10.1 %collective-permute-start.18 = (f32[32,512]{1,0:T(8,128)S(1)}, f32[32,512]{1,0:T(8,128)S(1)}, u32[]{:S(2)}, u32[]{:S(2)}) collective-permute-start(f32[32,512]{1,0:T(8,128)S(1)} %get-tuple-element.67), channel_id=1, source_target_pairs={{0,7},{1,2},{2,1},{3,4},{4,3},{5,6},{6,5},{7,0},{8,15},{9,10},{10,... | collective-permute-start | bytes 196616 | tf_op jit(solution)/shard_map/ppermute | solution.py:718
  89.0 6.8 %collective-permute-start.15 = (f32[8,512]{1,0:T(8,128)S(1)}, f32[8,512]{1,0:T(8,128)S(1)}, u32[]{:S(2)}, u32[]{:S(2)}) collective-permute-start(f32[8,512]{1,0:T(8,128)S(1)} %get-tuple-element.64), channel_id=1, source_target_pairs={{0,120},{8,16},{16,8},{24,32},{32,24},{40,48},{48,40},{56,64},{64,... | collective-permute-start | bytes 49160 | tf_op jit(solution)/shard_map/ppermute | solution.py:718
  89.8 5.9 %collective-permute-start.16 = (f32[8,512]{1,0:T(8,128)S(1)}, f32[8,512]{1,0:T(8,128)S(1)}, u32[]{:S(2)}, u32[]{:S(2)}) collective-permute-start(f32[8,512]{1,0:T(8,128)S(1)} %get-tuple-element.65), channel_id=1, source_target_pairs={{0,8},{8,0},{16,24},{24,16},{32,40},{40,32},{48,56},{56,48},{64,72... | collective-permute-start | bytes 49160 | tf_op jit(solution)/shard_map/ppermute | solution.py:718
  (12 other events, 8.7 us)

commit v6 on v5

--- a/solution.py
+++ b/solution.py
@@ -27,7 +27,7 @@
     return jax.ShapeDtypeStruct(shape, F32)
 
 
-def call(kernel, outs, ins, scratch=(), smem=(), hbm=(), hbm_out=(), limit=48):
+def call(kernel, outs, ins, scratch=(), smem=(), hbm=(), hbm_out=(), limit=16):
     def space(i, far):
         return pltpu.HBM if i in far else pltpu.SMEM if i in smem else pltpu.VMEM
 
@@ -381,7 +381,9 @@
 
 
 def restrict1(
-    b1_ref, v1_ref, m1_ref, m2_ref, cx, cc, cz, cy, out_ref, bw, vw, mw, sx, sc, halves
+    b1_ref, v1_ref, m1_ref, m2_ref, cx, cc, cz, cy,
+    out_hbm, sx, sc,
+    bw, vw, mw, halves, several, sems,
 ):
     halo = Halo(cx, cc, cz, cy)
     widen(((v1_ref, vw), (m1_ref, mw), (b1_ref, bw)), halo)
@@ -404,9 +406,22 @@
     b2 = 0.5 * dot(row_sums(A2, H2, 2, T1), dot(halves[...], pair_cols(R1)))
     m2 = m2_ref[...]
     rows = A2 * H2
-    for k in range(out_ref.shape[0]):
-        out_ref[k, 0:rows, :] = b2
-        out_ref[k, rows : 2 * rows, :] = m2
+    count = several.shape[0]
+    for k in range(count):
+        several[k, 0:rows, :] = b2
+        several[k, rows : 2 * rows, :] = m2
+    writes = [
+        pltpu.make_async_copy(several, out_hbm.at[pl.ds(k * count, count)], sems.at[k])
+        for k in range(out_hbm.shape[0] // count)
+    ]
+    for write in writes:
+        write.start()
+    for write in writes:
+        write.wait()
+
+
+def hand_on(own, kx, kc, out):
+    pass
 
 
 def level2_plane(consts, face, mc, mn):
@@ -537,9 +552,9 @@
 
 
 def coarse(
-    own, oth, bw, vw, mw, cx, cc, kx, kc, rhs_ref, v_ref, m_ref, ax, ac, az, ay, bx, bc, bz, by,
+    own, oth, b1_ref, v1_ref, m1_ref, cx, cc, cz, cy, kx, kc, rhs_ref, v_ref, m_ref, ax, ac, az, ay, bx, bc, bz, by,
     out_ref, sx, sc, sz, sy,
-    m2, d2, w3, sum_m, m3, b2, v2, sum_r, add, va, vb, e2, v2f, src, v1f, e_ref,
+    m2, d2, w3, sum_m, m3, b2, v2, sum_r, add, va, vb, e2, v2f, src, v1f, e_ref, bw, vw, mw,
 ):
     coarse_weights(own, oth, m2, d2, w3, sum_m, m3)
     a, g = position()
@@ -641,7 +656,8 @@
             src[4 * j + q : 4 * j + q + 1, :] = v2f[j, p, pl.ds(row, 1), :]
     o, c = iota((8 * (A2 + 2), 4 * (A2 + 2)), 0), iota((8 * (A2 + 2), 4 * (A2 + 2)), 1)
     e1 = dot(hot(o // 2 == c), dot(src[...], dup_cols(R2)))
-    halo, corners = Halo(cx, cc, None, None), Halo(kx, kc, None, None)
+    halo, corners = Halo(cx, cc, cz, cy), Halo(kx, kc, None, None)
+    widen(((v1_ref, vw), (m1_ref, mw), (b1_ref, bw)), halo)
 
     def v1_of(i):
         j = (i + 2) // 2
@@ -726,8 +742,15 @@
     groups = [[a * N_GZ + g for a in range(c, N_AZ, 2) for g in range(N_GZ)] for c in range(2)]
     own = lax.all_to_all(x, ("az", "gz"), 0, 0, tiled=True, axis_index_groups=groups)
     own = own.reshape(own.shape[0] * own.shape[1], own.shape[2])
-    own, *sides = lax.optimization_barrier((own, *sides))
-    return own, swap(own, "az", 0), sides
+    anywhere, near = pl.BlockSpec(memory_space=pl.ANY), pl.BlockSpec(memory_space=pltpu.VMEM)
+    own = pl.pallas_call(
+        hand_on,
+        out_shape=struct(*own.shape),
+        in_specs=[anywhere, near, near],
+        out_specs=anywhere,
+        input_output_aliases={0: 0},
+    )(own, *sides)
+    return own, swap(own, "az", 0)
 
 
 def faces(planes, rows, width):
@@ -767,21 +790,30 @@
         [pairs],
     )
     hc = exchange(*send)
-    copies, b1, v1, m1, kx, kc = call(
+    planes = vmem(A1, T1, R1)
+    copies, kx, kc = call(
         restrict1,
-        [struct(64, 2 * A2 * H2, R2), wide, wide, wide] + [struct(2 * T1, R1)] * 2,
+        [struct(64, 2 * A2 * H2, R2)] + [struct(2 * T1, R1)] * 2,
         (b1, v1, m1, m2, *hc),
-        [halves],
+        [
+            planes,
+            planes,
+            planes,
+            halves,
+            vmem(8, 2 * A2 * H2, R2),
+            pltpu.SemaphoreType.DMA((8,)),
+        ],
+        hbm_out=(0,),
     )
     corners = swap(kx, "az", 1), swap(kc, "az", 0)
-    own, oth, corners = gathered(copies, corners)
+    own, oth = gathered(copies, corners)
     ring = vmem(AZ2 + 4, 2, G2, R2)
     ends = vmem(HALF + 2, G2, R2)
     third = vmem(AZ3, G2, R2)
     out, *send = call(
         coarse,
         [block] + faces(NH, NA, NR),
-        (own, oth, b1, v1, m1, *hc[:2], *corners, rhs, v0, m0, *ha, *hb),
+        (own, oth, b1, v1, m1, *hc, *corners, rhs, v0, m0, *ha, *hb),
         [
             ring,
             ring,
@@ -799,7 +831,11 @@
             vmem(4 * (A2 + 2), R2),
             vmem((A1 + 2) * T1, R1),
             vmem((A1 + 2) * NH + 2 * A1, NR),
+            planes,
+            planes,
+            planes,
         ],
+        limit=24,
     )
     hg = exchange(*send)
     return tuple(

time: 98 us -> 105 us (1.071)
  Pallas kernels: 18 us -> 21 us
  local copies, waits for them, and re-layouts: 8.74 us -> 11.6 us
    unnamed x32 -> x44, local copies, waits for them, and re-layouts: 8.74 us -> 11.6 us
    pallas_call x7, Pallas kernels: 18 us -> 20.3 us  [call(): pl.pallas_call(kernel, out_shape=outs, in_specs=specs, out_specs=[pl.Bloc...]
where the time goes in v6:
time: 105 us; the launch traced here: 104 us
  starting transfers between devices  39.9 us (38%)
  waiting for transfers between devices  29.9 us (28%)
  Pallas kernels  21 us (20%)
  local copies, waits for them, and re-layouts  11.6 us (11%)
  between operations  1.68 us (2%)
    ppermute x19, starting transfers between devices, swap(): return lax.ppermute(x, axis, pairs)  32.8 us
    ppermute x19, waiting for transfers between devices, swap(): return lax.ppermute(x, axis, pairs)  29.3 us
    pallas_call x7, Pallas kernels, call(): pl.pallas_call(kernel, out_shape=outs, in_specs=specs, out_specs=[pl.Bloc...  20.3 us
    unnamed x44, local copies, waits for them, and re-layouts  11.6 us
    all_to_all x1, starting transfers between devices, gathered(): lax.all_to_all(x, ('az', 'gz'), 0, 0, tiled=True, axis_index_groups=groups)  7.18 us
  transfers between devices with their start and end apart: 20, of which 7 were waited for; matrix products, arithmetic and copies ran while one was open for 0% of the time, Pallas kernels for 0%

profile of v6, /device:TPU:0, one launch (start us, length us, event | category | flops | bytes accessed | tf_op | source)
XLA Modules:
  0.0 104.1 jit_solution(5115584966812621681)
XLA Ops:
  1.4 1.0 copy-done.5
  4.0 2.1 %collective-permute-start.2 = (f32[80,512]{1,0:T(8,128)S(1)}, f32[80,512]{1,0:T(8,128)S(1)}, u32[]{:S(2)}, u32[]{:S(2)}) collective-permute-start(f32[80,512]{1,0:T(8,128)S(1)} %get-tuple-element.33), channel_id=1, source_target_pairs={{0,1},{1,0},{2,3},{3,2},{4,5},{5,4},{6,7},{7,6},{8,9},{9,8},{10,11... | collective-permute-start | bytes 491528 | tf_op jit(solution)/shard_map/ppermute | solution.py:734
  6.1 2.6 %collective-permute-start.3 = (f32[80,512]{1,0:T(8,128)S(1)}, f32[80,512]{1,0:T(8,128)S(1)}, u32[]{:S(2)}, u32[]{:S(2)}) collective-permute-start(f32[80,512]{1,0:T(8,128)S(1)} %get-tuple-element.34), channel_id=1, source_target_pairs={{0,7},{1,2},{2,1},{3,4},{4,3},{5,6},{6,5},{7,0},{8,15},{9,10},{10,... | collective-permute-start | bytes 491528 | tf_op jit(solution)/shard_map/ppermute | solution.py:734
  8.7 5.0 %collective-permute-start = (f32[24,512]{1,0:T(8,128)S(1)}, f32[24,512]{1,0:T(8,128)S(1)}, u32[]{:S(2)}, u32[]{:S(2)}) collective-permute-start(f32[24,512]{1,0:T(8,128)S(1)} %get-tuple-element.31), channel_id=1, source_target_pairs={{0,120},{8,16},{16,8},{24,32},{32,24},{40,48},{48,40},{56,64},{64,... | collective-permute-start | bytes 147464 | tf_op jit(solution)/shard_map/ppermute | solution.py:734
  13.6 2.3 %collective-permute-done.ax = f32[24,512]{1,0:T(8,128)S(1)} collective-permute-done((f32[24,512]{1,0:T(8,128)S(1)}, f32[24,512]{1,0:T(8,128)S(1)}, u32[]{:S(2)}, u32[]{:S(2)}) %collective-permute-start) | collective-permute-done | bytes 49184 | tf_op jit(solution)/shard_map/ppermute | solution.py:734
  15.9 1.2 %shard_map.79 = (f32[32,8,512]{2,1,0:T(8,128)S(1)}, f32[32,8,512]{2,1,0:T(8,128)S(1)}, f32[8,512]{1,0:T(8,128)S(1)}, f32[8,512]{1,0:T(8,128)S(1)}, f32[32,512]{1,0:T(8,128)S(1)}, /*index=5*/f32[32,512]{1,0:T(8,128)S(1)}) custom-call(f32[32,8,512]{2,1,0:T(8,128)S(1)} %copy-done.2, f32[32,8,512]{2,1,0:T(8,128)S(1)} %copy-done.4, ...), custom_call_target="tpu_custom_call" | custom-call | tf_op jit(solution)/shard_map/pallas_call | solution.py:35
  18.2 1.8 %collective-permute-start.7 = (f32[32,512]{1,0:T(8,128)S(1)}, f32[32,512]{1,0:T(8,128)S(1)}, u32[]{:S(2)}, u32[]{:S(2)}) collective-permute-start(f32[32,512]{1,0:T(8,128)S(1)} %get-tuple-element.40), channel_id=1, source_target_pairs={{0,7},{1,2},{2,1},{3,4},{4,3},{5,6},{6,5},{7,0},{8,15},{9,10},{10,... | collective-permute-start | bytes 196616 | tf_op jit(solution)/shard_map/ppermute | solution.py:734
  20.0 4.1 %collective-permute-start.4 = (f32[8,512]{1,0:T(8,128)S(1)}, f32[8,512]{1,0:T(8,128)S(1)}, u32[]{:S(2)}, u32[]{:S(2)}) collective-permute-start(f32[8,512]{1,0:T(8,128)S(1)} %get-tuple-element.37), channel_id=1, source_target_pairs={{0,120},{8,16},{16,8},{24,32},{32,24},{40,48},{48,40},{56,64},{64,... | collective-permute-start | bytes 49160 | tf_op jit(solution)/shard_map/ppermute | solution.py:734
  24.0 2.7 %collective-permute-done.4.bx = f32[8,512]{1,0:T(8,128)S(1)} collective-permute-done((f32[8,512]{1,0:T(8,128)S(1)}, f32[8,512]{1,0:T(8,128)S(1)}, u32[]{:S(2)}, u32[]{:S(2)}) %collective-permute-start.4) | collective-permute-done | bytes 16416 | tf_op jit(solution)/shard_map/ppermute | solution.py:734
  26.8 1.5 %shard_map.80 = (f32[16,8,256]{2,1,0:T(8,128)S(1)}, f32[16,8,256]{2,1,0:T(8,128)S(1)}, f32[40,256]{1,0:T(8,128)S(1)}, f32[40,256]{1,0:T(8,128)S(1)}, f32[80,256]{1,0:T(8,128)S(1)}, /*index=5*/f32[80,256]{1,0:T(8,128)S(1)}) custom-call(f32[32,8,512]{2,1,0:T(8,128)S(1)} %get-tuple-element.35.rhs_ref, f32[32,8,512]{2,1,0:T(8,128)S(1)} %get-tuple-element.36.v_ref, ...), custom_call_target="tpu_custom_call" | custom-call | tf_op jit(solution)/shard_map/pallas_call | solution.py:35
  29.1 1.7 %collective-permute-start.11 = (f32[80,256]{1,0:T(8,128)S(1)}, f32[80,256]{1,0:T(8,128)S(1)}, u32[]{:S(2)}, u32[]{:S(2)}) collective-permute-start(f32[80,256]{1,0:T(8,128)S(1)} %get-tuple-element.47), channel_id=1, source_target_pairs={{0,7},{1,2},{2,1},{3,4},{4,3},{5,6},{6,5},{7,0},{8,15},{9,10},{10,... | collective-permute-start | bytes 245768 | tf_op jit(solution)/shard_map/ppermute | solution.py:734
  30.8 3.5 %collective-permute-start.8 = (f32[40,256]{1,0:T(8,128)S(1)}, f32[40,256]{1,0:T(8,128)S(1)}, u32[]{:S(2)}, u32[]{:S(2)}) collective-permute-start(f32[40,256]{1,0:T(8,128)S(1)} %get-tuple-element.44), channel_id=1, source_target_pairs={{0,120},{8,16},{16,8},{24,32},{32,24},{40,48},{48,40},{56,64},{64,... | collective-permute-start | bytes 122888 | tf_op jit(solution)/shard_map/ppermute | solution.py:734
  34.3 3.7 %collective-permute-done.8.cx = f32[40,256]{1,0:T(8,128)S(1)} collective-permute-done((f32[40,256]{1,0:T(8,128)S(1)}, f32[40,256]{1,0:T(8,128)S(1)}, u32[]{:S(2)}, u32[]{:S(2)}) %collective-permute-start.8) | collective-permute-done | bytes 40992 | tf_op jit(solution)/shard_map/ppermute | solution.py:734
  38.0 2.0 %shard_map.81 = (f32[64,32,128]{2,1,0:T(8,128)S(1)}, f32[16,256]{1,0:T(8,128)S(1)}, f32[16,256]{1,0:T(8,128)S(1)}) custom-call(f32[16,8,256]{2,1,0:T(8,128)S(1)} %get-tuple-element.41.b1_ref, f32[16,8,256]{2,1,0:T(8,128)S(1)} %get-tuple-element.42.v1_ref, f32[16,8,256]{2,1,0:T(8,128)S(1)} %get-tuple-element.30.m1_ref, ...), custom_call_target="tpu_custom_call" | custom-call | tf_op jit(solution)/shard_map/pallas_call | solution.py:35
  42.3 7.2 %all-to-all-start = ((f32[64,32,128]{2,1,0:T(8,128)}), f32[64,32,128]{2,1,0:T(8,128)S(1)}, u32[]{:S(2)}, u32[]{:S(2)}) async-start(f32[64,32,128]{2,1,0:T(8,128)} %copy-done.3), calls=%async_computation | async-start | bytes 2097152 | tf_op jit(solution)/shard_map/all_to_all | solution.py:743
  49.5 4.9 %collective-permute-start.12 = (f32[16,256]{1,0:T(8,128)}, f32[16,256]{1,0:T(8,128)S(1)}, u32[]{:S(2)}, u32[]{:S(2)}) collective-permute-start(f32[16,256]{1,0:T(8,128)} %copy-done.21), channel_id=1, source_target_pairs={{0,120},{8,16},{16,8},{24,32},{32,24},{40,48},{48,40},{56,64},{64,... | collective-permute-start | bytes 49160 | tf_op jit(solution)/shard_map/ppermute | solution.py:734
  54.4 11.7 %collective-permute-done.12.kx = f32[16,256]{1,0:T(8,128)S(1)} collective-permute-done((f32[16,256]{1,0:T(8,128)}, f32[16,256]{1,0:T(8,128)S(1)}, u32[]{:S(2)}, u32[]{:S(2)}) %collective-permute-start.12) | collective-permute-done | bytes 16416 | tf_op jit(solution)/shard_map/ppermute | solution.py:734
  69.2 2.9 %collective-permute-done.14.oth = f32[2048,128]{1,0:T(8,128)S(1)} collective-permute-done((f32[2048,128]{1,0:T(8,128)}, f32[2048,128]{1,0:T(8,128)S(1)}, u32[]{:S(2)}, u32[]{:S(2)}) %collective-permute-start.14) | collective-permute-done | bytes 1048608 | tf_op jit(solution)/shard_map/ppermute | solution.py:734
  72.0 1.2 %copy-done.1 = f32[2048,128]{1,0:T(8,128)S(1)} copy-done((f32[2048,128]{1,0:T(8,128)S(1)}, f32[2048,128]{1,0:T(8,128)}, u32[]{:S(2)}) %copy-start.1) | copy-done | bytes 1048600
  78.1 13.0 %shard_map.83 = (f32[32,8,512]{2,1,0:T(8,128)S(1)}, f32[8,512]{1,0:T(8,128)S(1)}, f32[8,512]{1,0:T(8,128)S(1)}, f32[32,512]{1,0:T(8,128)S(1)}, f32[32,512]{1,0:T(8,128)S(1)}) custom-call(f32[2048,128]{1,0:T(8,128)S(1)} %copy-done.1, f32[2048,128]{1,0:T(8,128)S(1)} %collective-permute-done.14.oth, f32[16,8,256]{2,1,0:T(8,128)S(1)} %get-tuple-element.41.b1_ref, ...), custom_call_target="tpu_custom_call" | custom-call | tf_op jit(solution)/shard_map/pallas_call | solution.py:35
  91.1 1.1 %collective-permute-start.17 = (f32[32,512]{1,0:T(8,128)S(1)}, f32[32,512]{1,0:T(8,128)S(1)}, u32[]{:S(2)}, u32[]{:S(2)}) collective-permute-start(f32[32,512]{1,0:T(8,128)S(1)} %get-tuple-element.54), channel_id=1, source_target_pairs={{0,1},{1,0},{2,3},{3,2},{4,5},{5,4},{6,7},{7,6},{8,9},{9,8},{10,11... | collective-permute-start | bytes 196616 | tf_op jit(solution)/shard_map/ppermute | solution.py:734
  92.2 3.4 %collective-permute-start.18 = (f32[32,512]{1,0:T(8,128)S(1)}, f32[32,512]{1,0:T(8,128)S(1)}, u32[]{:S(2)}, u32[]{:S(2)}) collective-permute-start(f32[32,512]{1,0:T(8,128)S(1)} %get-tuple-element.55), channel_id=1, source_target_pairs={{0,7},{1,2},{2,1},{3,4},{4,3},{5,6},{6,5},{7,0},{8,15},{9,10},{10,... | collective-permute-start | bytes 196616 | tf_op jit(solution)/shard_map/ppermute | solution.py:734
  96.4 5.9 %collective-permute-done.15.gx = f32[8,512]{1,0:T(8,128)S(1)} collective-permute-done((f32[8,512]{1,0:T(8,128)S(1)}, f32[8,512]{1,0:T(8,128)S(1)}, u32[]{:S(2)}, u32[]{:S(2)}) %collective-permute-start.15) | collective-permute-done | bytes 16416 | tf_op jit(solution)/shard_map/ppermute | solution.py:734
  102.4 1.6 %shard_map.84 = (f32[32,8,512]{2,1,0:T(8,128)}, f32[32,8,512]{2,1,0:T(8,128)}) custom-call(f32[32,8,512]{2,1,0:T(8,128)S(1)} %get-tuple-element.35.rhs_ref, f32[32,8,512]{2,1,0:T(8,128)S(1)} %get-tuple-element.51.v_ref, f32[32,8,512]{2,1,0:T(8,128)S(1)} %get-tuple-element.29.m0_ref.m_ref, f32[24,512]{1,0:T(8,128)S(1)} %collective-permute-done.ax, ...), custom_call_target="tpu_custom_call" | custom-call | tf_op jit(solution)/shard_map/pallas_call | solution.py:35
  (68 shorter events, 14.4 us)
Async XLA Ops:
  0.6 2.6 %copy-start.2 = (f32[32,8,512]{2,1,0:T(8,128)S(1)}, f32[32,8,512]{2,1,0:T(8,128)}, u32[]{:S(2)}) copy-start(f32[32,8,512]{2,1,0:T(8,128)} %p_ref.3) | copy-start | bytes 1572868
  3.9 12.0 %copy-start.4 = (f32[32,8,512]{2,1,0:T(8,128)S(1)}, f32[32,8,512]{2,1,0:T(8,128)}, u32[]{:S(2)}) copy-start(f32[32,8,512]{2,1,0:T(8,128)} %div_ref.1) | copy-start | bytes 1572868
  4.0 11.9 %collective-permute-start.2 = (f32[80,512]{1,0:T(8,128)S(1)}, f32[80,512]{1,0:T(8,128)S(1)}, u32[]{:S(2)}, u32[]{:S(2)}) collective-permute-start(f32[80,512]{1,0:T(8,128)S(1)} %get-tuple-element.33), channel_id=1, source_target_pairs={{0,1},{1,0},{2,3},{3,2},{4,5},{5,4},{6,7},{7,6},{8,9},{9,8},{10,11... | collective-permute-start | bytes 491528 | tf_op jit(solution)/shard_map/ppermute | solution.py:734
  6.1 9.8 %collective-permute-start.3 = (f32[80,512]{1,0:T(8,128)S(1)}, f32[80,512]{1,0:T(8,128)S(1)}, u32[]{:S(2)}, u32[]{:S(2)}) collective-permute-start(f32[80,512]{1,0:T(8,128)S(1)} %get-tuple-element.34), channel_id=1, source_target_pairs={{0,7},{1,2},{2,1},{3,4},{4,3},{5,6},{6,5},{7,0},{8,15},{9,10},{10,... | collective-permute-start | bytes 491528 | tf_op jit(solution)/shard_map/ppermute | solution.py:734
  8.7 7.2 %collective-permute-start = (f32[24,512]{1,0:T(8,128)S(1)}, f32[24,512]{1,0:T(8,128)S(1)}, u32[]{:S(2)}, u32[]{:S(2)}) collective-permute-start(f32[24,512]{1,0:T(8,128)S(1)} %get-tuple-element.31), channel_id=1, source_target_pairs={{0,120},{8,16},{16,8},{24,32},{32,24},{40,48},{48,40},{56,64},{64,... | collective-permute-start | bytes 147464 | tf_op jit(solution)/shard_map/ppermute | solution.py:734
  13.6 2.3 %copy-start.19 = (s32[128]{0:T(128)S(1)}, s32[128]{0:T(128)}, u32[]{:S(2)}) copy-start(s32[128]{0:T(128)} %param.11) | copy-start | bytes 1540
  13.6 2.3 %collective-permute-start.1 = (f32[24,512]{1,0:T(8,128)S(1)}, f32[24,512]{1,0:T(8,128)S(1)}, u32[]{:S(2)}, u32[]{:S(2)}) collective-permute-start(f32[24,512]{1,0:T(8,128)S(1)} %get-tuple-element.32), channel_id=1, source_target_pairs={{0,8},{8,0},{16,24},{24,16},{32,40},{40,32},{48,56},{56,48},{64,72... | collective-permute-start | bytes 147464 | tf_op jit(solution)/shard_map/ppermute | solution.py:734
  17.2 9.6 %collective-permute-start.6 = (f32[32,512]{1,0:T(8,128)S(1)}, f32[32,512]{1,0:T(8,128)S(1)}, u32[]{:S(2)}, u32[]{:S(2)}) collective-permute-start(f32[32,512]{1,0:T(8,128)S(1)} %get-tuple-element.39), channel_id=1, source_target_pairs={{0,1},{1,0},{2,3},{3,2},{4,5},{5,4},{6,7},{7,6},{8,9},{9,8},{10,11... | collective-permute-start | bytes 196616 | tf_op jit(solution)/shard_map/ppermute | solution.py:734
  18.2 8.6 %collective-permute-start.7 = (f32[32,512]{1,0:T(8,128)S(1)}, f32[32,512]{1,0:T(8,128)S(1)}, u32[]{:S(2)}, u32[]{:S(2)}) collective-permute-start(f32[32,512]{1,0:T(8,128)S(1)} %get-tuple-element.40), channel_id=1, source_target_pairs={{0,7},{1,2},{2,1},{3,4},{4,3},{5,6},{6,5},{7,0},{8,15},{9,10},{10,... | collective-permute-start | bytes 196616 | tf_op jit(solution)/shard_map/ppermute | solution.py:734
  20.0 6.8 %collective-permute-start.4 = (f32[8,512]{1,0:T(8,128)S(1)}, f32[8,512]{1,0:T(8,128)S(1)}, u32[]{:S(2)}, u32[]{:S(2)}) collective-permute-start(f32[8,512]{1,0:T(8,128)S(1)} %get-tuple-element.37), channel_id=1, source_target_pairs={{0,120},{8,16},{16,8},{24,32},{32,24},{40,48},{48,40},{56,64},{64,... | collective-permute-start | bytes 49160 | tf_op jit(solution)/shard_map/ppermute | solution.py:734
  24.0 2.7 %collective-permute-start.5 = (f32[8,512]{1,0:T(8,128)S(1)}, f32[8,512]{1,0:T(8,128)S(1)}, u32[]{:S(2)}, u32[]{:S(2)}) collective-permute-start(f32[8,512]{1,0:T(8,128)S(1)} %get-tuple-element.38), channel_id=1, source_target_pairs={{0,8},{8,0},{16,24},{24,16},{32,40},{40,32},{48,56},{56,48},{64,72... | collective-permute-start | bytes 49160 | tf_op jit(solution)/shard_map/ppermute | solution.py:734
  28.3 9.7 %collective-permute-start.10 = (f32[80,256]{1,0:T(8,128)S(1)}, f32[80,256]{1,0:T(8,128)S(1)}, u32[]{:S(2)}, u32[]{:S(2)}) collective-permute-start(f32[80,256]{1,0:T(8,128)S(1)} %get-tuple-element.46), channel_id=1, source_target_pairs={{0,1},{1,0},{2,3},{3,2},{4,5},{5,4},{6,7},{7,6},{8,9},{9,8},{10,11... | collective-permute-start | bytes 245768 | tf_op jit(solution)/shard_map/ppermute | solution.py:734
  29.1 8.9 %collective-permute-start.11 = (f32[80,256]{1,0:T(8,128)S(1)}, f32[80,256]{1,0:T(8,128)S(1)}, u32[]{:S(2)}, u32[]{:S(2)}) collective-permute-start(f32[80,256]{1,0:T(8,128)S(1)} %get-tuple-element.47), channel_id=1, source_target_pairs={{0,7},{1,2},{2,1},{3,4},{4,3},{5,6},{6,5},{7,0},{8,15},{9,10},{10,... | collective-permute-start | bytes 245768 | tf_op jit(solution)/shard_map/ppermute | solution.py:734
  30.8 7.2 %collective-permute-start.8 = (f32[40,256]{1,0:T(8,128)S(1)}, f32[40,256]{1,0:T(8,128)S(1)}, u32[]{:S(2)}, u32[]{:S(2)}) collective-permute-start(f32[40,256]{1,0:T(8,128)S(1)} %get-tuple-element.44), channel_id=1, source_target_pairs={{0,120},{8,16},{16,8},{24,32},{32,24},{40,48},{48,40},{56,64},{64,... | collective-permute-start | bytes 122888 | tf_op jit(solution)/shard_map/ppermute | solution.py:734
  34.3 3.7 %collective-permute-start.9 = (f32[40,256]{1,0:T(8,128)S(1)}, f32[40,256]{1,0:T(8,128)S(1)}, u32[]{:S(2)}, u32[]{:S(2)}) collective-permute-start(f32[40,256]{1,0:T(8,128)S(1)} %get-tuple-element.45), channel_id=1, source_target_pairs={{0,8},{8,0},{16,24},{24,16},{32,40},{40,32},{48,56},{56,48},{64,72... | collective-permute-start | bytes 122888 | tf_op jit(solution)/shard_map/ppermute | solution.py:734
  38.0 2.1 %copy-start.14 = (f32[40,256]{1,0:T(8,128)}, f32[40,256]{1,0:T(8,128)S(1)}, u32[]{:S(2)}) copy-start(f32[40,256]{1,0:T(8,128)S(1)} %collective-permute-done.9.cc) | copy-start | bytes 122884
  42.3 25.1 %all-to-all-start = ((f32[64,32,128]{2,1,0:T(8,128)}), f32[64,32,128]{2,1,0:T(8,128)S(1)}, u32[]{:S(2)}, u32[]{:S(2)}) async-start(f32[64,32,128]{2,1,0:T(8,128)} %copy-done.3), calls=%async_computation | async-start | bytes 2097152 | tf_op jit(solution)/shard_map/all_to_all | solution.py:743
  49.5 16.7 %collective-permute-start.12 = (f32[16,256]{1,0:T(8,128)}, f32[16,256]{1,0:T(8,128)S(1)}, u32[]{:S(2)}, u32[]{:S(2)}) collective-permute-start(f32[16,256]{1,0:T(8,128)} %copy-done.21), channel_id=1, source_target_pairs={{0,120},{8,16},{16,8},{24,32},{32,24},{40,48},{48,40},{56,64},{64,... | collective-permute-start | bytes 49160 | tf_op jit(solution)/shard_map/ppermute | solution.py:734
  54.4 12.3 %collective-permute-start.13 = (f32[16,256]{1,0:T(8,128)}, f32[16,256]{1,0:T(8,128)}, u32[]{:S(2)}, u32[]{:S(2)}) collective-permute-start(f32[16,256]{1,0:T(8,128)} %copy-done.20), channel_id=1, source_target_pairs={{0,8},{8,0},{16,24},{24,16},{32,40},{40,32},{48,56},{56,48},{64,72... | collective-permute-start | bytes 49160 | tf_op jit(solution)/shard_map/ppermute | solution.py:734
  69.2 2.9 %collective-permute-start.14 = (f32[2048,128]{1,0:T(8,128)}, f32[2048,128]{1,0:T(8,128)S(1)}, u32[]{:S(2)}, u32[]{:S(2)}) collective-permute-start(f32[2048,128]{1,0:T(8,128)} %shard_map.82.own), channel_id=1, source_target_pairs={{0,8},{8,0},{16,24},{24,16},{32,40},{40,32},{48,56},{56,48},{64,72... | collective-permute-start | bytes 3145736 | tf_op jit(solution)/shard_map/ppermute | solution.py:734
  91.1 11.3 %collective-permute-start.17 = (f32[32,512]{1,0:T(8,128)S(1)}, f32[32,512]{1,0:T(8,128)S(1)}, u32[]{:S(2)}, u32[]{:S(2)}) collective-permute-start(f32[32,512]{1,0:T(8,128)S(1)} %get-tuple-element.54), channel_id=1, source_target_pairs={{0,1},{1,0},{2,3},{3,2},{4,5},{5,4},{6,7},{7,6},{8,9},{9,8},{10,11... | collective-permute-start | bytes 196616 | tf_op jit(solution)/shard_map/ppermute | solution.py:734
  92.2 10.1 %collective-permute-start.18 = (f32[32,512]{1,0:T(8,128)S(1)}, f32[32,512]{1,0:T(8,128)S(1)}, u32[]{:S(2)}, u32[]{:S(2)}) collective-permute-start(f32[32,512]{1,0:T(8,128)S(1)} %get-tuple-element.55), channel_id=1, source_target_pairs={{0,7},{1,2},{2,1},{3,4},{4,3},{5,6},{6,5},{7,0},{8,15},{9,10},{10,... | collective-permute-start | bytes 196616 | tf_op jit(solution)/shard_map/ppermute | solution.py:734
  95.6 6.8 %collective-permute-start.15 = (f32[8,512]{1,0:T(8,128)S(1)}, f32[8,512]{1,0:T(8,128)S(1)}, u32[]{:S(2)}, u32[]{:S(2)}) collective-permute-start(f32[8,512]{1,0:T(8,128)S(1)} %get-tuple-element.52), channel_id=1, source_target_pairs={{0,120},{8,16},{16,8},{24,32},{32,24},{40,48},{48,40},{56,64},{64,... | collective-permute-start | bytes 49160 | tf_op jit(solution)/shard_map/ppermute | solution.py:734
  96.4 5.9 %collective-permute-start.16 = (f32[8,512]{1,0:T(8,128)S(1)}, f32[8,512]{1,0:T(8,128)S(1)}, u32[]{:S(2)}, u32[]{:S(2)}) collective-permute-start(f32[8,512]{1,0:T(8,128)S(1)} %get-tuple-element.53), channel_id=1, source_target_pairs={{0,8},{8,0},{16,24},{24,16},{32,40},{40,32},{48,56},{56,48},{64,72... | collective-permute-start | bytes 49160 | tf_op jit(solution)/shard_map/ppermute | solution.py:734
  (18 other events, 18.7 us)

commit v7 on v4

--- a/solution.py
+++ b/solution.py
@@ -216,8 +216,24 @@
         y_ref[rows_at + i : rows_at + i + 1, :] = ref[i, pl.ds(y_row, 1), :]
 
 
-def mobilities(void_ref, m0_ref, m1_ref, m2_ref, pairs, halves):
+def mobilities(
+    void_hbm, vol_hbm, cnt_ref,
+    m0_ref, m1_ref, m2_ref, live_ref,
+    pairs, halves, void_ref, vol_ref, sems,
+):
+    part = NA // 4
+    reads = [
+        pltpu.make_async_copy(
+            void_hbm.at[pl.ds(k * part, part)], void_ref.at[pl.ds(k * part, part)], sems.at[k]
+        )
+        for k in range(4)
+    ]
+    reads.append(pltpu.make_async_copy(vol_hbm, vol_ref, sems.at[4]))
+    for read in reads:
+        read.start()
     for i in range(0, NA, 2):
+        if i % part == 0:
+            reads[i // part].wait()
         u = 1.0 / (1.0 - void_ref[i])
         v = 1.0 / (1.0 - void_ref[i + 1])
         m0_ref[i] = u
@@ -227,9 +243,12 @@
     for i in range(A2):
         halves[i * T1 : (i + 1) * T1, :] = m1_ref[2 * i] + m1_ref[2 * i + 1]
     m2_ref[...] = 0.125 * dot(row_sums(A2, H2, 2, T1), dot(halves[...], pair_cols(R1)))
-
-
-def first_faces(p_ref, m0_ref, m1_ref, vol_ref, cnt_ref, sx, sc, sz, sy):
+    for read in reads[4:]:
+        read.wait()
+    live_ref[...] = jnp.where(iota((1, SLOTS), 1) < cnt_ref[0], vol_ref[...], 0.0)
+
+
+def first_faces(p_ref, m0_ref, m1_ref, live_ref, sx, sc, sz, sy):
     a, g = position()
     pa, pg = a % 2, g % 2
     store_faces(p_ref, sx, sc, sz, sy, 0, 0)
@@ -247,9 +266,8 @@
         at = slice(2 * NA + i, 2 * NA + i + 1)
         sz[at, 0:R1] = m1_ref[i, pl.ds(z_row, 1), :]
         sy[at, 0:R1] = m1_ref[i, pl.ds(H1 + 3 - z_row, 1), :]
-    live = jnp.where(iota((1, SLOTS), 1) < cnt_ref[0], vol_ref[...], 0.0)
     for ref in (sx, sc):
-        ref[2 * NH : 2 * NH + 1, R1 : R1 + SLOTS] = live
+        ref[2 * NH : 2 * NH + 1, R1 : R1 + SLOTS] = live_ref[...]
 
 
 def fine_mobility(m_ref, ah):
@@ -470,9 +488,6 @@
     ref[HALF + 1] = pltpu.roll(ref[1], R2 // 2, 1)
 
 
-STEP = 8
-
-
 def coarse_weights(own, oth, m2, d2, w3, sum_m, m3):
     a, g = position()
     pa = a % 2
@@ -491,21 +506,16 @@
     close_ring(m2)
     consts = level2_consts()
 
-    def diagonals(k, carry):
-        s = STEP * k + 2
-        mp, mc = both(m2, s - 1), both(m2, s)
-        face = level2_face(consts, mp, mc)
-        for d in range(STEP):
-            mn = both(m2, s + d + 1)
-            w, face = level2_plane(consts, face, mc, mn)
-            for p in range(2):
-                d2[s + d, p] = OMEGA / (total_weight(w[p]) + SIGMA * 16.0)
-            if d % 2:
-                sum_m[(STEP // 2) * k + d // 2] = (mp[0] + mp[1]) + (mc[0] + mc[1])
-            mp, mc = mc, mn
-        return carry
-
-    lax.fori_loop(0, AZ2 // STEP, diagonals, 0)
+    mp, mc = both(m2, 1), both(m2, 2)
+    face = level2_face(consts, mp, mc)
+    for d in range(AZ2):
+        mn = both(m2, d + 3)
+        w, face = level2_plane(consts, face, mc, mn)
+        for p in range(2):
+            d2[d + 2, p] = OMEGA / (total_weight(w[p]) + SIGMA * 16.0)
+        if d % 2:
+            sum_m[d // 2] = (mp[0] + mp[1]) + (mc[0] + mc[1])
+        mp, mc = mc, mn
     close_ring(d2)
     m3[1 : HALF + 1] = 0.125 * packed(sum_m)
     wrap(m3)
@@ -557,24 +567,19 @@
     close_ring(v2)
     consts = level2_consts()
 
-    def residuals(k, carry):
-        s = STEP * k + 2
-        mc = both(m2, s)
-        vp, vc = both(v2, s - 1), both(v2, s)
-        face = level2_face(consts, both(m2, s - 1), mc)
-        total = None
-        for d in range(STEP):
-            mn, vn = both(m2, s + d + 1), both(v2, s + d + 1)
-            w, face = level2_plane(consts, face, mc, mn)
-            n = level2_around(vp, vc, vn)
-            b = both(b2, s + d)
-            r = ((1.0 - OMEGA) * (b[0] + b[1]) + weighted(w[0], n[0])) + weighted(w[1], n[1])
-            if d % 2:
-                sum_r[(STEP // 2) * k + d // 2] = total + r
-            total, mc, vp, vc = r, mn, vc, vn
-        return carry
-
-    lax.fori_loop(0, AZ2 // STEP, residuals, 0)
+    mc = both(m2, 2)
+    vp, vc = both(v2, 1), both(v2, 2)
+    face = level2_face(consts, both(m2, 1), mc)
+    total = None
+    for d in range(AZ2):
+        mn, vn = both(m2, d + 3), both(v2, d + 3)
+        w, face = level2_plane(consts, face, mc, mn)
+        n = level2_around(vp, vc, vn)
+        b = both(b2, d + 2)
+        r = ((1.0 - OMEGA) * (b[0] + b[1]) + weighted(w[0], n[0])) + weighted(w[1], n[1])
+        if d % 2:
+            sum_r[d // 2] = total + r
+        total, mc, vp, vc = r, mn, vc, vn
 
     b3 = 0.5 * packed(sum_r)
     for i in range(HALF):
@@ -739,14 +744,28 @@
     pairs = vmem(A1 * NH, NR)
     halves = vmem(A2 * T1, R1)
 
-    m0, m1, m2 = call(
-        mobilities, [block, wide, struct(A2 * H2, R2)], (void_fraction,), [pairs, halves]
+    far = [
+        pltpu.with_memory_space_constraint(x, pltpu.HBM)
+        for x in (void_fraction, volume)
+    ]
+    m0, m1, m2, live = call(
+        mobilities,
+        [block, wide, struct(A2 * H2, R2), struct(1, SLOTS)],
+        (*far, bubble_count),
+        [
+            pairs,
+            halves,
+            vmem(NA, NH, NR),
+            vmem(1, SLOTS),
+            pltpu.SemaphoreType.DMA((5,)),
+        ],
+        hbm=(0, 1),
+        smem=(2,),
     )
     send = call(
         first_faces,
         faces(3 * NH, 2 * NA + A1, NR),
-        (pressure, m0, m1, volume, bubble_count),
-        smem=(4,),
+        (pressure, m0, m1, live),
     )
     ha = exchange(*send)
     rhs, v0, *send = call(

time: 94.8 us -> 91.8 us (0.968)
  local copies, waits for them, and re-layouts: 1.71 us -> 0.01 us
  Pallas kernels: 18.1 us -> 16.7 us
    unnamed x10 -> x6, local copies, waits for them, and re-layouts: 1.71 us -> 0.01 us
    pallas_call x8, Pallas kernels: 18.1 us -> 16.7 us  [call(): pl.pallas_call(kernel, out_shape=outs, in_specs=specs, out_specs=[pl.Bloc...]
where the time goes in v7:
time: 91.8 us; the launch traced here: 91.6 us
  starting transfers between devices  26.9 us (29%)
  blocking collectives  23.7 us (26%)
  waiting for transfers between devices  22.7 us (25%)
  Pallas kernels  16.7 us (18%)
  between operations  1.6 us (2%)
    ppermute x17, starting transfers between devices, swap(): return lax.ppermute(x, axis, pairs)  26.9 us
    all_to_all x1, blocking collectives, gathered(): lax.all_to_all(x, ('az', 'gz'), 0, 0, tiled=True, axis_index_groups=groups)  23.7 us
    ppermute x17, waiting for transfers between devices, swap(): return lax.ppermute(x, axis, pairs)  22.7 us
    pallas_call x8, Pallas kernels, call(): pl.pallas_call(kernel, out_shape=outs, in_specs=specs, out_specs=[pl.Bloc...  16.7 us
  transfers between devices with their start and end apart: 17, of which 7 were waited for; matrix products, arithmetic and copies ran while one was open for 0% of the time, Pallas kernels for 0%

profile of v7, /device:TPU:0, one launch (start us, length us, event | category | flops | bytes accessed | tf_op | source)
XLA Modules:
  0.0 91.6 jit_solution(13014845401142504711)
XLA Ops:
  1.3 2.0 %shard_map.77 = (f32[32,8,512]{2,1,0:T(8,128)S(1)}, f32[16,8,256]{2,1,0:T(8,128)S(1)}, f32[16,128]{1,0:T(8,128)S(1)}, f32[1,128]{1,0:T(1,128)S(1)}) custom-call(f32[32,8,512]{2,1,0:T(8,128)} %void_hbm.1, f32[1,128]{1,0:T(1,128)} %bitcast.6, s32[1]{0:T(128)S(6)} %copy.8.cnt_ref), custom_call_target="tpu_custom_call" | custom-call | tf_op jit(solution)/shard_map/pallas_call | solution.py:35
  3.5 2.1 %collective-permute-start.2 = (f32[80,512]{1,0:T(8,128)S(1)}, f32[80,512]{1,0:T(8,128)S(1)}, u32[]{:S(2)}, u32[]{:S(2)}) collective-permute-start(f32[80,512]{1,0:T(8,128)S(1)} %get-tuple-element.35), channel_id=1, source_target_pairs={{0,1},{1,0},{2,3},{3,2},{4,5},{5,4},{6,7},{7,6},{8,9},{9,8},{10,11... | collective-permute-start | bytes 491528 | tf_op jit(solution)/shard_map/ppermute | solution.py:717
  5.6 2.6 %collective-permute-start.3 = (f32[80,512]{1,0:T(8,128)S(1)}, f32[80,512]{1,0:T(8,128)S(1)}, u32[]{:S(2)}, u32[]{:S(2)}) collective-permute-start(f32[80,512]{1,0:T(8,128)S(1)} %get-tuple-element.36), channel_id=1, source_target_pairs={{0,7},{1,2},{2,1},{3,4},{4,3},{5,6},{6,5},{7,0},{8,15},{9,10},{10,... | collective-permute-start | bytes 491528 | tf_op jit(solution)/shard_map/ppermute | solution.py:717
  8.1 5.0 %collective-permute-start = (f32[24,512]{1,0:T(8,128)S(1)}, f32[24,512]{1,0:T(8,128)S(1)}, u32[]{:S(2)}, u32[]{:S(2)}) collective-permute-start(f32[24,512]{1,0:T(8,128)S(1)} %get-tuple-element.33), channel_id=1, source_target_pairs={{0,120},{8,16},{16,8},{24,32},{32,24},{40,48},{48,40},{56,64},{64,... | collective-permute-start | bytes 147464 | tf_op jit(solution)/shard_map/ppermute | solution.py:717
  13.1 2.3 %collective-permute-done.ax = f32[24,512]{1,0:T(8,128)S(1)} collective-permute-done((f32[24,512]{1,0:T(8,128)S(1)}, f32[24,512]{1,0:T(8,128)S(1)}, u32[]{:S(2)}, u32[]{:S(2)}) %collective-permute-start) | collective-permute-done | bytes 49184 | tf_op jit(solution)/shard_map/ppermute | solution.py:717
  15.4 1.2 %shard_map.79 = (f32[32,8,512]{2,1,0:T(8,128)S(1)}, f32[32,8,512]{2,1,0:T(8,128)S(1)}, f32[8,512]{1,0:T(8,128)S(1)}, f32[8,512]{1,0:T(8,128)S(1)}, f32[32,512]{1,0:T(8,128)S(1)}, /*index=5*/f32[32,512]{1,0:T(8,128)S(1)}) custom-call(f32[32,8,512]{2,1,0:T(8,128)S(1)} %copy-done, f32[32,8,512]{2,1,0:T(8,128)S(1)} %copy-done.1, ...), custom_call_target="tpu_custom_call" | custom-call | tf_op jit(solution)/shard_map/pallas_call | solution.py:35
  16.6 1.0 %collective-permute-start.6 = (f32[32,512]{1,0:T(8,128)S(1)}, f32[32,512]{1,0:T(8,128)S(1)}, u32[]{:S(2)}, u32[]{:S(2)}) collective-permute-start(f32[32,512]{1,0:T(8,128)S(1)} %get-tuple-element.41), channel_id=1, source_target_pairs={{0,1},{1,0},{2,3},{3,2},{4,5},{5,4},{6,7},{7,6},{8,9},{9,8},{10,11... | collective-permute-start | bytes 196616 | tf_op jit(solution)/shard_map/ppermute | solution.py:717
  17.6 1.8 %collective-permute-start.7 = (f32[32,512]{1,0:T(8,128)S(1)}, f32[32,512]{1,0:T(8,128)S(1)}, u32[]{:S(2)}, u32[]{:S(2)}) collective-permute-start(f32[32,512]{1,0:T(8,128)S(1)} %get-tuple-element.42), channel_id=1, source_target_pairs={{0,7},{1,2},{2,1},{3,4},{4,3},{5,6},{6,5},{7,0},{8,15},{9,10},{10,... | collective-permute-start | bytes 196616 | tf_op jit(solution)/shard_map/ppermute | solution.py:717
  19.4 4.1 %collective-permute-start.4 = (f32[8,512]{1,0:T(8,128)S(1)}, f32[8,512]{1,0:T(8,128)S(1)}, u32[]{:S(2)}, u32[]{:S(2)}) collective-permute-start(f32[8,512]{1,0:T(8,128)S(1)} %get-tuple-element.39), channel_id=1, source_target_pairs={{0,120},{8,16},{16,8},{24,32},{32,24},{40,48},{48,40},{56,64},{64,... | collective-permute-start | bytes 49160 | tf_op jit(solution)/shard_map/ppermute | solution.py:717
  23.5 2.7 %collective-permute-done.4.bx = f32[8,512]{1,0:T(8,128)S(1)} collective-permute-done((f32[8,512]{1,0:T(8,128)S(1)}, f32[8,512]{1,0:T(8,128)S(1)}, u32[]{:S(2)}, u32[]{:S(2)}) %collective-permute-start.4) | collective-permute-done | bytes 16416 | tf_op jit(solution)/shard_map/ppermute | solution.py:717
  26.2 1.5 %shard_map.80 = (f32[16,8,256]{2,1,0:T(8,128)S(1)}, f32[16,8,256]{2,1,0:T(8,128)S(1)}, f32[80,256]{1,0:T(8,128)S(1)}, f32[80,256]{1,0:T(8,128)S(1)}) custom-call(f32[32,8,512]{2,1,0:T(8,128)S(1)} %get-tuple-element.37.rhs_ref, f32[32,8,512]{2,1,0:T(8,128)S(1)} %get-tuple-element.38.v_ref, f32[32,8,512]{2,1,0:T(8,128)S(1)} %get-tuple-element.30.m0_ref.m_ref, ...), custom_call_target="tpu_custom_call" | custom-call | tf_op jit(solution)/shard_map/pallas_call | solution.py:35
  28.5 1.7 %collective-permute-start.9 = (f32[80,256]{1,0:T(8,128)S(1)}, f32[80,256]{1,0:T(8,128)S(1)}, u32[]{:S(2)}, u32[]{:S(2)}) collective-permute-start(f32[80,256]{1,0:T(8,128)S(1)} %get-tuple-element.46), channel_id=1, source_target_pairs={{0,7},{1,2},{2,1},{3,4},{4,3},{5,6},{6,5},{7,0},{8,15},{9,10},{10,... | collective-permute-start | bytes 245768 | tf_op jit(solution)/shard_map/ppermute | solution.py:717
  30.2 2.7 %collective-permute-done.8.z_ref = f32[80,256]{1,0:T(8,128)S(1)} collective-permute-done((f32[80,256]{1,0:T(8,128)S(1)}, f32[80,256]{1,0:T(8,128)S(1)}, u32[]{:S(2)}, u32[]{:S(2)}) %collective-permute-start.8) | collective-permute-done | bytes 81952 | tf_op jit(solution)/shard_map/ppermute | solution.py:717
  32.9 2.1 %collective-permute-done.9.y_ref = f32[80,256]{1,0:T(8,128)S(1)} collective-permute-done((f32[80,256]{1,0:T(8,128)S(1)}, f32[80,256]{1,0:T(8,128)S(1)}, u32[]{:S(2)}, u32[]{:S(2)}) %collective-permute-start.9) | collective-permute-done | bytes 81952 | tf_op jit(solution)/shard_map/ppermute | solution.py:717
  35.2 2.7 %collective-permute-start.10 = (f32[40,256]{1,0:T(8,128)S(1)}, f32[40,256]{1,0:T(8,128)S(1)}, u32[]{:S(2)}, u32[]{:S(2)}) collective-permute-start(f32[40,256]{1,0:T(8,128)S(1)} %get-tuple-element.51), channel_id=1, source_target_pairs={{0,120},{8,16},{16,8},{24,32},{32,24},{40,48},{48,40},{56,64},{64,... | collective-permute-start | bytes 122888 | tf_op jit(solution)/shard_map/ppermute | solution.py:717
  37.9 4.4 %collective-permute-done.10.cx = f32[40,256]{1,0:T(8,128)S(1)} collective-permute-done((f32[40,256]{1,0:T(8,128)S(1)}, f32[40,256]{1,0:T(8,128)S(1)}, u32[]{:S(2)}, u32[]{:S(2)}) %collective-permute-start.10) | collective-permute-done | bytes 40992 | tf_op jit(solution)/shard_map/ppermute | solution.py:717
  42.9 23.7 %all_to_all.5 = f32[64,32,128]{2,1,0:T(8,128)S(1)} all-to-all(f32[64,32,128]{2,1,0:T(8,128)S(1)} %shard_map.82), channel_id=1, replica_groups={{0,1,2,3,4,5,6,7,16,17,18,19,20,21,22,23,32,33,34,35,36,37,38,39,48,49,..., dimensions={0} | all-to-all | bytes 2097152 | tf_op jit(solution)/shard_map/all_to_all | solution.py:726
  66.5 2.7 %collective-permute-done.12.oth = f32[2048,128]{1,0:T(8,128)S(1)} collective-permute-done((f32[2048,128]{1,0:T(8,128)S(1)}, f32[2048,128]{1,0:T(8,128)S(1)}, u32[]{:S(2)}, u32[]{:S(2)}) %collective-permute-start.12) | collective-permute-done | bytes 1048608 | tf_op jit(solution)/shard_map/ppermute | solution.py:717
  69.2 9.7 %shard_map.83 = (f32[32,8,512]{2,1,0:T(8,128)S(1)}, f32[8,512]{1,0:T(8,128)S(1)}, f32[8,512]{1,0:T(8,128)S(1)}, f32[32,512]{1,0:T(8,128)S(1)}, f32[32,512]{1,0:T(8,128)S(1)}) custom-call(f32[2048,128]{1,0:T(8,128)S(1)} %bitcast.4, f32[2048,128]{1,0:T(8,128)S(1)} %collective-permute-done.12.oth, f32[16,8,256]{2,1,0:T(8,128)S(1)} %get-tuple-element.47.bw, ...), custom_call_target="tpu_custom_call" | custom-call | tf_op jit(solution)/shard_map/pallas_call | solution.py:35
  78.9 1.1 %collective-permute-start.15 = (f32[32,512]{1,0:T(8,128)S(1)}, f32[32,512]{1,0:T(8,128)S(1)}, u32[]{:S(2)}, u32[]{:S(2)}) collective-permute-start(f32[32,512]{1,0:T(8,128)S(1)} %get-tuple-element.56), channel_id=1, source_target_pairs={{0,1},{1,0},{2,3},{3,2},{4,5},{5,4},{6,7},{7,6},{8,9},{9,8},{10,11... | collective-permute-start | bytes 196616 | tf_op jit(solution)/shard_map/ppermute | solution.py:717
  80.0 3.1 %collective-permute-start.16 = (f32[32,512]{1,0:T(8,128)S(1)}, f32[32,512]{1,0:T(8,128)S(1)}, u32[]{:S(2)}, u32[]{:S(2)}) collective-permute-start(f32[32,512]{1,0:T(8,128)S(1)} %get-tuple-element.57), channel_id=1, source_target_pairs={{0,7},{1,2},{2,1},{3,4},{4,3},{5,6},{6,5},{7,0},{8,15},{9,10},{10,... | collective-permute-start | bytes 196616 | tf_op jit(solution)/shard_map/ppermute | solution.py:717
  83.1 1.0 %collective-permute-start.13 = (f32[8,512]{1,0:T(8,128)S(1)}, f32[8,512]{1,0:T(8,128)S(1)}, u32[]{:S(2)}, u32[]{:S(2)}) collective-permute-start(f32[8,512]{1,0:T(8,128)S(1)} %get-tuple-element.54), channel_id=1, source_target_pairs={{0,120},{8,16},{16,8},{24,32},{32,24},{40,48},{48,40},{56,64},{64,... | collective-permute-start | bytes 49160 | tf_op jit(solution)/shard_map/ppermute | solution.py:717
  84.1 5.7 %collective-permute-done.13.gx = f32[8,512]{1,0:T(8,128)S(1)} collective-permute-done((f32[8,512]{1,0:T(8,128)S(1)}, f32[8,512]{1,0:T(8,128)S(1)}, u32[]{:S(2)}, u32[]{:S(2)}) %collective-permute-start.13) | collective-permute-done | bytes 16416 | tf_op jit(solution)/shard_map/ppermute | solution.py:717
  89.9 1.6 %shard_map.84 = (f32[32,8,512]{2,1,0:T(8,128)}, f32[32,8,512]{2,1,0:T(8,128)}) custom-call(f32[32,8,512]{2,1,0:T(8,128)S(1)} %get-tuple-element.37.rhs_ref, f32[32,8,512]{2,1,0:T(8,128)S(1)} %get-tuple-element.53.v_ref, f32[32,8,512]{2,1,0:T(8,128)S(1)} %get-tuple-element.30.m0_ref.m_ref, f32[24,512]{1,0:T(8,128)S(1)} %collective-permute-done.ax, ...), custom_call_target="tpu_custom_call" | custom-call | tf_op jit(solution)/shard_map/pallas_call | solution.py:35
  (25 shorter events, 1.7 us)
Async XLA Ops:
  0.6 2.7 %copy-start = (f32[32,8,512]{2,1,0:T(8,128)S(1)}, f32[32,8,512]{2,1,0:T(8,128)}, u32[]{:S(2)}) copy-start(f32[32,8,512]{2,1,0:T(8,128)} %p_ref.3) | copy-start | bytes 1572868
  3.4 12.0 %copy-start.1 = (f32[32,8,512]{2,1,0:T(8,128)S(1)}, f32[32,8,512]{2,1,0:T(8,128)}, u32[]{:S(2)}) copy-start(f32[32,8,512]{2,1,0:T(8,128)} %div_ref.1) | copy-start | bytes 1572868
  3.5 11.9 %collective-permute-start.2 = (f32[80,512]{1,0:T(8,128)S(1)}, f32[80,512]{1,0:T(8,128)S(1)}, u32[]{:S(2)}, u32[]{:S(2)}) collective-permute-start(f32[80,512]{1,0:T(8,128)S(1)} %get-tuple-element.35), channel_id=1, source_target_pairs={{0,1},{1,0},{2,3},{3,2},{4,5},{5,4},{6,7},{7,6},{8,9},{9,8},{10,11... | collective-permute-start | bytes 491528 | tf_op jit(solution)/shard_map/ppermute | solution.py:717
  5.6 9.8 %collective-permute-start.3 = (f32[80,512]{1,0:T(8,128)S(1)}, f32[80,512]{1,0:T(8,128)S(1)}, u32[]{:S(2)}, u32[]{:S(2)}) collective-permute-start(f32[80,512]{1,0:T(8,128)S(1)} %get-tuple-element.36), channel_id=1, source_target_pairs={{0,7},{1,2},{2,1},{3,4},{4,3},{5,6},{6,5},{7,0},{8,15},{9,10},{10,... | collective-permute-start | bytes 491528 | tf_op jit(solution)/shard_map/ppermute | solution.py:717
  8.1 7.2 %collective-permute-start = (f32[24,512]{1,0:T(8,128)S(1)}, f32[24,512]{1,0:T(8,128)S(1)}, u32[]{:S(2)}, u32[]{:S(2)}) collective-permute-start(f32[24,512]{1,0:T(8,128)S(1)} %get-tuple-element.33), channel_id=1, source_target_pairs={{0,120},{8,16},{16,8},{24,32},{32,24},{40,48},{48,40},{56,64},{64,... | collective-permute-start | bytes 147464 | tf_op jit(solution)/shard_map/ppermute | solution.py:717
  13.1 2.3 %copy-start.2 = (s32[128]{0:T(128)S(1)}, s32[128]{0:T(128)}, u32[]{:S(2)}) copy-start(s32[128]{0:T(128)} %param.11) | copy-start | bytes 1540
  13.1 2.3 %collective-permute-start.1 = (f32[24,512]{1,0:T(8,128)S(1)}, f32[24,512]{1,0:T(8,128)S(1)}, u32[]{:S(2)}, u32[]{:S(2)}) collective-permute-start(f32[24,512]{1,0:T(8,128)S(1)} %get-tuple-element.34), channel_id=1, source_target_pairs={{0,8},{8,0},{16,24},{24,16},{32,40},{40,32},{48,56},{56,48},{64,72... | collective-permute-start | bytes 147464 | tf_op jit(solution)/shard_map/ppermute | solution.py:717
  16.6 9.6 %collective-permute-start.6 = (f32[32,512]{1,0:T(8,128)S(1)}, f32[32,512]{1,0:T(8,128)S(1)}, u32[]{:S(2)}, u32[]{:S(2)}) collective-permute-start(f32[32,512]{1,0:T(8,128)S(1)} %get-tuple-element.41), channel_id=1, source_target_pairs={{0,1},{1,0},{2,3},{3,2},{4,5},{5,4},{6,7},{7,6},{8,9},{9,8},{10,11... | collective-permute-start | bytes 196616 | tf_op jit(solution)/shard_map/ppermute | solution.py:717
  17.6 8.6 %collective-permute-start.7 = (f32[32,512]{1,0:T(8,128)S(1)}, f32[32,512]{1,0:T(8,128)S(1)}, u32[]{:S(2)}, u32[]{:S(2)}) collective-permute-start(f32[32,512]{1,0:T(8,128)S(1)} %get-tuple-element.42), channel_id=1, source_target_pairs={{0,7},{1,2},{2,1},{3,4},{4,3},{5,6},{6,5},{7,0},{8,15},{9,10},{10,... | collective-permute-start | bytes 196616 | tf_op jit(solution)/shard_map/ppermute | solution.py:717
  19.4 6.8 %collective-permute-start.4 = (f32[8,512]{1,0:T(8,128)S(1)}, f32[8,512]{1,0:T(8,128)S(1)}, u32[]{:S(2)}, u32[]{:S(2)}) collective-permute-start(f32[8,512]{1,0:T(8,128)S(1)} %get-tuple-element.39), channel_id=1, source_target_pairs={{0,120},{8,16},{16,8},{24,32},{32,24},{40,48},{48,40},{56,64},{64,... | collective-permute-start | bytes 49160 | tf_op jit(solution)/shard_map/ppermute | solution.py:717
  23.5 2.7 %collective-permute-start.5 = (f32[8,512]{1,0:T(8,128)S(1)}, f32[8,512]{1,0:T(8,128)S(1)}, u32[]{:S(2)}, u32[]{:S(2)}) collective-permute-start(f32[8,512]{1,0:T(8,128)S(1)} %get-tuple-element.40), channel_id=1, source_target_pairs={{0,8},{8,0},{16,24},{24,16},{32,40},{40,32},{48,56},{56,48},{64,72... | collective-permute-start | bytes 49160 | tf_op jit(solution)/shard_map/ppermute | solution.py:717
  27.7 5.3 %collective-permute-start.8 = (f32[80,256]{1,0:T(8,128)S(1)}, f32[80,256]{1,0:T(8,128)S(1)}, u32[]{:S(2)}, u32[]{:S(2)}) collective-permute-start(f32[80,256]{1,0:T(8,128)S(1)} %get-tuple-element.45), channel_id=1, source_target_pairs={{0,1},{1,0},{2,3},{3,2},{4,5},{5,4},{6,7},{7,6},{8,9},{9,8},{10,11... | collective-permute-start | bytes 245768 | tf_op jit(solution)/shard_map/ppermute | solution.py:717
  28.5 6.6 %collective-permute-start.9 = (f32[80,256]{1,0:T(8,128)S(1)}, f32[80,256]{1,0:T(8,128)S(1)}, u32[]{:S(2)}, u32[]{:S(2)}) collective-permute-start(f32[80,256]{1,0:T(8,128)S(1)} %get-tuple-element.46), channel_id=1, source_target_pairs={{0,7},{1,2},{2,1},{3,4},{4,3},{5,6},{6,5},{7,0},{8,15},{9,10},{10,... | collective-permute-start | bytes 245768 | tf_op jit(solution)/shard_map/ppermute | solution.py:717
  35.2 7.1 %collective-permute-start.10 = (f32[40,256]{1,0:T(8,128)S(1)}, f32[40,256]{1,0:T(8,128)S(1)}, u32[]{:S(2)}, u32[]{:S(2)}) collective-permute-start(f32[40,256]{1,0:T(8,128)S(1)} %get-tuple-element.51), channel_id=1, source_target_pairs={{0,120},{8,16},{16,8},{24,32},{32,24},{40,48},{48,40},{56,64},{64,... | collective-permute-start | bytes 122888 | tf_op jit(solution)/shard_map/ppermute | solution.py:717
  37.9 4.4 %collective-permute-start.11 = (f32[40,256]{1,0:T(8,128)S(1)}, f32[40,256]{1,0:T(8,128)S(1)}, u32[]{:S(2)}, u32[]{:S(2)}) collective-permute-start(f32[40,256]{1,0:T(8,128)S(1)} %get-tuple-element.52), channel_id=1, source_target_pairs={{0,8},{8,0},{16,24},{24,16},{32,40},{40,32},{48,56},{56,48},{64,72... | collective-permute-start | bytes 122888 | tf_op jit(solution)/shard_map/ppermute | solution.py:717
  66.5 2.7 %collective-permute-start.12 = (f32[2048,128]{1,0:T(8,128)S(1)}, f32[2048,128]{1,0:T(8,128)S(1)}, u32[]{:S(2)}, u32[]{:S(2)}) collective-permute-start(f32[2048,128]{1,0:T(8,128)S(1)} %bitcast.3), channel_id=1, source_target_pairs={{0,8},{8,0},{16,24},{24,16},{32,40},{40,32},{48,56},{56,48},{64,72... | collective-permute-start | bytes 3145736 | tf_op jit(solution)/shard_map/ppermute | solution.py:717
  78.9 11.0 %collective-permute-start.15 = (f32[32,512]{1,0:T(8,128)S(1)}, f32[32,512]{1,0:T(8,128)S(1)}, u32[]{:S(2)}, u32[]{:S(2)}) collective-permute-start(f32[32,512]{1,0:T(8,128)S(1)} %get-tuple-element.56), channel_id=1, source_target_pairs={{0,1},{1,0},{2,3},{3,2},{4,5},{5,4},{6,7},{7,6},{8,9},{9,8},{10,11... | collective-permute-start | bytes 196616 | tf_op jit(solution)/shard_map/ppermute | solution.py:717
  80.0 9.8 %collective-permute-start.16 = (f32[32,512]{1,0:T(8,128)S(1)}, f32[32,512]{1,0:T(8,128)S(1)}, u32[]{:S(2)}, u32[]{:S(2)}) collective-permute-start(f32[32,512]{1,0:T(8,128)S(1)} %get-tuple-element.57), channel_id=1, source_target_pairs={{0,7},{1,2},{2,1},{3,4},{4,3},{5,6},{6,5},{7,0},{8,15},{9,10},{10,... | collective-permute-start | bytes 196616 | tf_op jit(solution)/shard_map/ppermute | solution.py:717
  83.1 6.8 %collective-permute-start.13 = (f32[8,512]{1,0:T(8,128)S(1)}, f32[8,512]{1,0:T(8,128)S(1)}, u32[]{:S(2)}, u32[]{:S(2)}) collective-permute-start(f32[8,512]{1,0:T(8,128)S(1)} %get-tuple-element.54), channel_id=1, source_target_pairs={{0,120},{8,16},{16,8},{24,32},{32,24},{40,48},{48,40},{56,64},{64,... | collective-permute-start | bytes 49160 | tf_op jit(solution)/shard_map/ppermute | solution.py:717
  84.1 5.8 %collective-permute-start.14 = (f32[8,512]{1,0:T(8,128)S(1)}, f32[8,512]{1,0:T(8,128)S(1)}, u32[]{:S(2)}, u32[]{:S(2)}) collective-permute-start(f32[8,512]{1,0:T(8,128)S(1)} %get-tuple-element.55), channel_id=1, source_target_pairs={{0,8},{8,0},{16,24},{24,16},{32,40},{40,32},{48,56},{56,48},{64,72... | collective-permute-start | bytes 49160 | tf_op jit(solution)/shard_map/ppermute | solution.py:717

commit v8 on v7

--- a/solution.py
+++ b/solution.py
@@ -248,6 +248,11 @@
     live_ref[...] = jnp.where(iota((1, SLOTS), 1) < cnt_ref[0], vol_ref[...], 0.0)
 
 
+def packed_row(i):
+    at, lane = 2 * NA + i // 2, (i % 2) * R1
+    return slice(at, at + 1), slice(lane, lane + R1)
+
+
 def first_faces(p_ref, m0_ref, m1_ref, live_ref, sx, sc, sz, sy):
     a, g = position()
     pa, pg = a % 2, g % 2
@@ -259,13 +264,11 @@
     c_plane = jnp.where(pa == 0, A1 - 1, 0)
     sc[rest, 0:R1] = m1_ref[c_plane]
     sx[rest, 0:R1] = m1_ref[A1 - 1 - c_plane]
-    for ref in (sz, sy):
-        ref[2 * NA : 2 * NA + A1, R1:NR] = jnp.zeros((A1, NR - R1), F32)
     z_row = jnp.where(pg == 0, H1 + 1, 2)
     for i in range(A1):
-        at = slice(2 * NA + i, 2 * NA + i + 1)
-        sz[at, 0:R1] = m1_ref[i, pl.ds(z_row, 1), :]
-        sy[at, 0:R1] = m1_ref[i, pl.ds(H1 + 3 - z_row, 1), :]
+        at, lanes = packed_row(i)
+        sz[at, lanes] = m1_ref[i, pl.ds(z_row, 1), :]
+        sy[at, lanes] = m1_ref[i, pl.ds(H1 + 3 - z_row, 1), :]
     for ref in (sx, sc):
         ref[2 * NH : 2 * NH + 1, R1 : R1 + SLOTS] = live_ref[...]
 
@@ -347,8 +350,7 @@
             return ah.prev(slice(2 * NH, 3 * NH), slice(0, R1))
         if i >= A1:
             return ah.next(slice(2 * NH, 3 * NH), slice(0, R1))
-        at = slice(2 * NA + i, 2 * NA + i + 1)
-        below, above = ah.below(at, slice(0, R1)), ah.above(at, slice(0, R1))
+        below, above = ah.below(*packed_row(i)), ah.above(*packed_row(i))
         return jnp.where(sub == 1, below, jnp.where(sub == H1 + 2, above, m1_ref[i]))
 
     def emit1(i, diagonal, around, centre):
@@ -764,7 +766,7 @@
     )
     send = call(
         first_faces,
-        faces(3 * NH, 2 * NA + A1, NR),
+        faces(3 * NH, 2 * NA + A1 // 2, NR),
         (pressure, m0, m1, live),
     )
     ha = exchange(*send)

time: 91.8 us -> 91.8 us (level)
  no operation moved by 1% of the time
where the time goes in v8:
time: 91.8 us; the launch traced here: 91.6 us
  starting transfers between devices  26.7 us (29%)
  blocking collectives  23.6 us (26%)
  waiting for transfers between devices  23 us (25%)
  Pallas kernels  16.7 us (18%)
  between operations  1.6 us (2%)
    ppermute x17, starting transfers between devices, swap(): return lax.ppermute(x, axis, pairs)  26.7 us
    all_to_all x1, blocking collectives, gathered(): lax.all_to_all(x, ('az', 'gz'), 0, 0, tiled=True, axis_index_groups=groups)  23.6 us
    ppermute x17, waiting for transfers between devices, swap(): return lax.ppermute(x, axis, pairs)  23 us
    pallas_call x8, Pallas kernels, call(): pl.pallas_call(kernel, out_shape=outs, in_specs=specs, out_specs=[pl.Bloc...  16.7 us
  transfers between devices with their start and end apart: 17, of which 7 were waited for; matrix products, arithmetic and copies ran while one was open for 0% of the time, Pallas kernels for 0%

profile of v8, /device:TPU:0, one launch (start us, length us, event | category | flops | bytes accessed | tf_op | source)
XLA Modules:
  0.0 91.6 jit_solution(11443276136179711700)
XLA Ops:
  1.3 2.0 %shard_map.77 = (f32[32,8,512]{2,1,0:T(8,128)S(1)}, f32[16,8,256]{2,1,0:T(8,128)S(1)}, f32[16,128]{1,0:T(8,128)S(1)}, f32[1,128]{1,0:T(1,128)S(1)}) custom-call(f32[32,8,512]{2,1,0:T(8,128)} %void_hbm.1, f32[1,128]{1,0:T(1,128)} %bitcast.6, s32[1]{0:T(128)S(6)} %copy.8.cnt_ref), custom_call_target="tpu_custom_call" | custom-call | tf_op jit(solution)/shard_map/pallas_call | solution.py:35
  3.5 2.1 %collective-permute-start.2 = (f32[72,512]{1,0:T(8,128)S(1)}, f32[72,512]{1,0:T(8,128)S(1)}, u32[]{:S(2)}, u32[]{:S(2)}) collective-permute-start(f32[72,512]{1,0:T(8,128)S(1)} %get-tuple-element.35), channel_id=1, source_target_pairs={{0,1},{1,0},{2,3},{3,2},{4,5},{5,4},{6,7},{7,6},{8,9},{9,8},{10,11... | collective-permute-start | bytes 442376 | tf_op jit(solution)/shard_map/ppermute | solution.py:719
  5.6 2.6 %collective-permute-start.3 = (f32[72,512]{1,0:T(8,128)S(1)}, f32[72,512]{1,0:T(8,128)S(1)}, u32[]{:S(2)}, u32[]{:S(2)}) collective-permute-start(f32[72,512]{1,0:T(8,128)S(1)} %get-tuple-element.36), channel_id=1, source_target_pairs={{0,7},{1,2},{2,1},{3,4},{4,3},{5,6},{6,5},{7,0},{8,15},{9,10},{10,... | collective-permute-start | bytes 442376 | tf_op jit(solution)/shard_map/ppermute | solution.py:719
  8.1 5.0 %collective-permute-start = (f32[24,512]{1,0:T(8,128)S(1)}, f32[24,512]{1,0:T(8,128)S(1)}, u32[]{:S(2)}, u32[]{:S(2)}) collective-permute-start(f32[24,512]{1,0:T(8,128)S(1)} %get-tuple-element.33), channel_id=1, source_target_pairs={{0,120},{8,16},{16,8},{24,32},{32,24},{40,48},{48,40},{56,64},{64,... | collective-permute-start | bytes 147464 | tf_op jit(solution)/shard_map/ppermute | solution.py:719
  13.1 2.3 %collective-permute-done.ax = f32[24,512]{1,0:T(8,128)S(1)} collective-permute-done((f32[24,512]{1,0:T(8,128)S(1)}, f32[24,512]{1,0:T(8,128)S(1)}, u32[]{:S(2)}, u32[]{:S(2)}) %collective-permute-start) | collective-permute-done | bytes 49184 | tf_op jit(solution)/shard_map/ppermute | solution.py:719
  15.4 1.2 %shard_map.79 = (f32[32,8,512]{2,1,0:T(8,128)S(1)}, f32[32,8,512]{2,1,0:T(8,128)S(1)}, f32[8,512]{1,0:T(8,128)S(1)}, f32[8,512]{1,0:T(8,128)S(1)}, f32[32,512]{1,0:T(8,128)S(1)}, /*index=5*/f32[32,512]{1,0:T(8,128)S(1)}) custom-call(f32[32,8,512]{2,1,0:T(8,128)S(1)} %copy-done, f32[32,8,512]{2,1,0:T(8,128)S(1)} %copy-done.1, ...), custom_call_target="tpu_custom_call" | custom-call | tf_op jit(solution)/shard_map/pallas_call | solution.py:35
  16.6 1.0 %collective-permute-start.6 = (f32[32,512]{1,0:T(8,128)S(1)}, f32[32,512]{1,0:T(8,128)S(1)}, u32[]{:S(2)}, u32[]{:S(2)}) collective-permute-start(f32[32,512]{1,0:T(8,128)S(1)} %get-tuple-element.41), channel_id=1, source_target_pairs={{0,1},{1,0},{2,3},{3,2},{4,5},{5,4},{6,7},{7,6},{8,9},{9,8},{10,11... | collective-permute-start | bytes 196616 | tf_op jit(solution)/shard_map/ppermute | solution.py:719
  17.6 1.8 %collective-permute-start.7 = (f32[32,512]{1,0:T(8,128)S(1)}, f32[32,512]{1,0:T(8,128)S(1)}, u32[]{:S(2)}, u32[]{:S(2)}) collective-permute-start(f32[32,512]{1,0:T(8,128)S(1)} %get-tuple-element.42), channel_id=1, source_target_pairs={{0,7},{1,2},{2,1},{3,4},{4,3},{5,6},{6,5},{7,0},{8,15},{9,10},{10,... | collective-permute-start | bytes 196616 | tf_op jit(solution)/shard_map/ppermute | solution.py:719
  19.4 3.8 %collective-permute-start.4 = (f32[8,512]{1,0:T(8,128)S(1)}, f32[8,512]{1,0:T(8,128)S(1)}, u32[]{:S(2)}, u32[]{:S(2)}) collective-permute-start(f32[8,512]{1,0:T(8,128)S(1)} %get-tuple-element.39), channel_id=1, source_target_pairs={{0,120},{8,16},{16,8},{24,32},{32,24},{40,48},{48,40},{56,64},{64,... | collective-permute-start | bytes 49160 | tf_op jit(solution)/shard_map/ppermute | solution.py:719
  23.2 3.0 %collective-permute-done.4.bx = f32[8,512]{1,0:T(8,128)S(1)} collective-permute-done((f32[8,512]{1,0:T(8,128)S(1)}, f32[8,512]{1,0:T(8,128)S(1)}, u32[]{:S(2)}, u32[]{:S(2)}) %collective-permute-start.4) | collective-permute-done | bytes 16416 | tf_op jit(solution)/shard_map/ppermute | solution.py:719
  26.2 1.5 %shard_map.80 = (f32[16,8,256]{2,1,0:T(8,128)S(1)}, f32[16,8,256]{2,1,0:T(8,128)S(1)}, f32[80,256]{1,0:T(8,128)S(1)}, f32[80,256]{1,0:T(8,128)S(1)}) custom-call(f32[32,8,512]{2,1,0:T(8,128)S(1)} %get-tuple-element.37.rhs_ref, f32[32,8,512]{2,1,0:T(8,128)S(1)} %get-tuple-element.38.v_ref, f32[32,8,512]{2,1,0:T(8,128)S(1)} %get-tuple-element.30.m0_ref.m_ref, ...), custom_call_target="tpu_custom_call" | custom-call | tf_op jit(solution)/shard_map/pallas_call | solution.py:35
  28.5 1.7 %collective-permute-start.9 = (f32[80,256]{1,0:T(8,128)S(1)}, f32[80,256]{1,0:T(8,128)S(1)}, u32[]{:S(2)}, u32[]{:S(2)}) collective-permute-start(f32[80,256]{1,0:T(8,128)S(1)} %get-tuple-element.46), channel_id=1, source_target_pairs={{0,7},{1,2},{2,1},{3,4},{4,3},{5,6},{6,5},{7,0},{8,15},{9,10},{10,... | collective-permute-start | bytes 245768 | tf_op jit(solution)/shard_map/ppermute | solution.py:719
  30.2 2.5 %collective-permute-done.8.z_ref = f32[80,256]{1,0:T(8,128)S(1)} collective-permute-done((f32[80,256]{1,0:T(8,128)S(1)}, f32[80,256]{1,0:T(8,128)S(1)}, u32[]{:S(2)}, u32[]{:S(2)}) %collective-permute-start.8) | collective-permute-done | bytes 81952 | tf_op jit(solution)/shard_map/ppermute | solution.py:719
  32.7 2.4 %collective-permute-done.9.y_ref = f32[80,256]{1,0:T(8,128)S(1)} collective-permute-done((f32[80,256]{1,0:T(8,128)S(1)}, f32[80,256]{1,0:T(8,128)S(1)}, u32[]{:S(2)}, u32[]{:S(2)}) %collective-permute-start.9) | collective-permute-done | bytes 81952 | tf_op jit(solution)/shard_map/ppermute | solution.py:719
  35.2 2.7 %collective-permute-start.10 = (f32[40,256]{1,0:T(8,128)S(1)}, f32[40,256]{1,0:T(8,128)S(1)}, u32[]{:S(2)}, u32[]{:S(2)}) collective-permute-start(f32[40,256]{1,0:T(8,128)S(1)} %get-tuple-element.51), channel_id=1, source_target_pairs={{0,120},{8,16},{16,8},{24,32},{32,24},{40,48},{48,40},{56,64},{64,... | collective-permute-start | bytes 122888 | tf_op jit(solution)/shard_map/ppermute | solution.py:719
  37.9 4.4 %collective-permute-done.10.cx = f32[40,256]{1,0:T(8,128)S(1)} collective-permute-done((f32[40,256]{1,0:T(8,128)S(1)}, f32[40,256]{1,0:T(8,128)S(1)}, u32[]{:S(2)}, u32[]{:S(2)}) %collective-permute-start.10) | collective-permute-done | bytes 40992 | tf_op jit(solution)/shard_map/ppermute | solution.py:719
  42.9 23.6 %all_to_all.5 = f32[64,32,128]{2,1,0:T(8,128)S(1)} all-to-all(f32[64,32,128]{2,1,0:T(8,128)S(1)} %shard_map.82), channel_id=1, replica_groups={{0,1,2,3,4,5,6,7,16,17,18,19,20,21,22,23,32,33,34,35,36,37,38,39,48,49,..., dimensions={0} | all-to-all | bytes 2097152 | tf_op jit(solution)/shard_map/all_to_all | solution.py:728
  66.5 2.7 %collective-permute-done.12.oth = f32[2048,128]{1,0:T(8,128)S(1)} collective-permute-done((f32[2048,128]{1,0:T(8,128)S(1)}, f32[2048,128]{1,0:T(8,128)S(1)}, u32[]{:S(2)}, u32[]{:S(2)}) %collective-permute-start.12) | collective-permute-done | bytes 1048608 | tf_op jit(solution)/shard_map/ppermute | solution.py:719
  69.1 9.7 %shard_map.83 = (f32[32,8,512]{2,1,0:T(8,128)S(1)}, f32[8,512]{1,0:T(8,128)S(1)}, f32[8,512]{1,0:T(8,128)S(1)}, f32[32,512]{1,0:T(8,128)S(1)}, f32[32,512]{1,0:T(8,128)S(1)}) custom-call(f32[2048,128]{1,0:T(8,128)S(1)} %bitcast.4, f32[2048,128]{1,0:T(8,128)S(1)} %collective-permute-done.12.oth, f32[16,8,256]{2,1,0:T(8,128)S(1)} %get-tuple-element.47.bw, ...), custom_call_target="tpu_custom_call" | custom-call | tf_op jit(solution)/shard_map/pallas_call | solution.py:35
  78.8 1.0 %collective-permute-start.15 = (f32[32,512]{1,0:T(8,128)S(1)}, f32[32,512]{1,0:T(8,128)S(1)}, u32[]{:S(2)}, u32[]{:S(2)}) collective-permute-start(f32[32,512]{1,0:T(8,128)S(1)} %get-tuple-element.56), channel_id=1, source_target_pairs={{0,1},{1,0},{2,3},{3,2},{4,5},{5,4},{6,7},{7,6},{8,9},{9,8},{10,11... | collective-permute-start | bytes 196616 | tf_op jit(solution)/shard_map/ppermute | solution.py:719
  79.8 3.2 %collective-permute-start.16 = (f32[32,512]{1,0:T(8,128)S(1)}, f32[32,512]{1,0:T(8,128)S(1)}, u32[]{:S(2)}, u32[]{:S(2)}) collective-permute-start(f32[32,512]{1,0:T(8,128)S(1)} %get-tuple-element.57), channel_id=1, source_target_pairs={{0,7},{1,2},{2,1},{3,4},{4,3},{5,6},{6,5},{7,0},{8,15},{9,10},{10,... | collective-permute-start | bytes 196616 | tf_op jit(solution)/shard_map/ppermute | solution.py:719
  83.0 1.0 %collective-permute-start.13 = (f32[8,512]{1,0:T(8,128)S(1)}, f32[8,512]{1,0:T(8,128)S(1)}, u32[]{:S(2)}, u32[]{:S(2)}) collective-permute-start(f32[8,512]{1,0:T(8,128)S(1)} %get-tuple-element.54), channel_id=1, source_target_pairs={{0,120},{8,16},{16,8},{24,32},{32,24},{40,48},{48,40},{56,64},{64,... | collective-permute-start | bytes 49160 | tf_op jit(solution)/shard_map/ppermute | solution.py:719
  84.1 5.8 %collective-permute-done.13.gx = f32[8,512]{1,0:T(8,128)S(1)} collective-permute-done((f32[8,512]{1,0:T(8,128)S(1)}, f32[8,512]{1,0:T(8,128)S(1)}, u32[]{:S(2)}, u32[]{:S(2)}) %collective-permute-start.13) | collective-permute-done | bytes 16416 | tf_op jit(solution)/shard_map/ppermute | solution.py:719
  89.8 1.6 %shard_map.84 = (f32[32,8,512]{2,1,0:T(8,128)}, f32[32,8,512]{2,1,0:T(8,128)}) custom-call(f32[32,8,512]{2,1,0:T(8,128)S(1)} %get-tuple-element.37.rhs_ref, f32[32,8,512]{2,1,0:T(8,128)S(1)} %get-tuple-element.53.v_ref, f32[32,8,512]{2,1,0:T(8,128)S(1)} %get-tuple-element.30.m0_ref.m_ref, f32[24,512]{1,0:T(8,128)S(1)} %collective-permute-done.ax, ...), custom_call_target="tpu_custom_call" | custom-call | tf_op jit(solution)/shard_map/pallas_call | solution.py:35
  (25 shorter events, 1.7 us)
Async XLA Ops:
  0.6 2.7 %copy-start = (f32[32,8,512]{2,1,0:T(8,128)S(1)}, f32[32,8,512]{2,1,0:T(8,128)}, u32[]{:S(2)}) copy-start(f32[32,8,512]{2,1,0:T(8,128)} %p_ref.3) | copy-start | bytes 1572868
  3.4 12.0 %copy-start.1 = (f32[32,8,512]{2,1,0:T(8,128)S(1)}, f32[32,8,512]{2,1,0:T(8,128)}, u32[]{:S(2)}) copy-start(f32[32,8,512]{2,1,0:T(8,128)} %div_ref.1) | copy-start | bytes 1572868
  3.5 11.9 %collective-permute-start.2 = (f32[72,512]{1,0:T(8,128)S(1)}, f32[72,512]{1,0:T(8,128)S(1)}, u32[]{:S(2)}, u32[]{:S(2)}) collective-permute-start(f32[72,512]{1,0:T(8,128)S(1)} %get-tuple-element.35), channel_id=1, source_target_pairs={{0,1},{1,0},{2,3},{3,2},{4,5},{5,4},{6,7},{7,6},{8,9},{9,8},{10,11... | collective-permute-start | bytes 442376 | tf_op jit(solution)/shard_map/ppermute | solution.py:719
  5.6 9.8 %collective-permute-start.3 = (f32[72,512]{1,0:T(8,128)S(1)}, f32[72,512]{1,0:T(8,128)S(1)}, u32[]{:S(2)}, u32[]{:S(2)}) collective-permute-start(f32[72,512]{1,0:T(8,128)S(1)} %get-tuple-element.36), channel_id=1, source_target_pairs={{0,7},{1,2},{2,1},{3,4},{4,3},{5,6},{6,5},{7,0},{8,15},{9,10},{10,... | collective-permute-start | bytes 442376 | tf_op jit(solution)/shard_map/ppermute | solution.py:719
  8.1 7.2 %collective-permute-start = (f32[24,512]{1,0:T(8,128)S(1)}, f32[24,512]{1,0:T(8,128)S(1)}, u32[]{:S(2)}, u32[]{:S(2)}) collective-permute-start(f32[24,512]{1,0:T(8,128)S(1)} %get-tuple-element.33), channel_id=1, source_target_pairs={{0,120},{8,16},{16,8},{24,32},{32,24},{40,48},{48,40},{56,64},{64,... | collective-permute-start | bytes 147464 | tf_op jit(solution)/shard_map/ppermute | solution.py:719
  13.1 2.3 %copy-start.2 = (s32[128]{0:T(128)S(1)}, s32[128]{0:T(128)}, u32[]{:S(2)}) copy-start(s32[128]{0:T(128)} %param.11) | copy-start | bytes 1540
  13.1 2.3 %collective-permute-start.1 = (f32[24,512]{1,0:T(8,128)S(1)}, f32[24,512]{1,0:T(8,128)S(1)}, u32[]{:S(2)}, u32[]{:S(2)}) collective-permute-start(f32[24,512]{1,0:T(8,128)S(1)} %get-tuple-element.34), channel_id=1, source_target_pairs={{0,8},{8,0},{16,24},{24,16},{32,40},{40,32},{48,56},{56,48},{64,72... | collective-permute-start | bytes 147464 | tf_op jit(solution)/shard_map/ppermute | solution.py:719
  16.6 9.6 %collective-permute-start.6 = (f32[32,512]{1,0:T(8,128)S(1)}, f32[32,512]{1,0:T(8,128)S(1)}, u32[]{:S(2)}, u32[]{:S(2)}) collective-permute-start(f32[32,512]{1,0:T(8,128)S(1)} %get-tuple-element.41), channel_id=1, source_target_pairs={{0,1},{1,0},{2,3},{3,2},{4,5},{5,4},{6,7},{7,6},{8,9},{9,8},{10,11... | collective-permute-start | bytes 196616 | tf_op jit(solution)/shard_map/ppermute | solution.py:719
  17.6 8.6 %collective-permute-start.7 = (f32[32,512]{1,0:T(8,128)S(1)}, f32[32,512]{1,0:T(8,128)S(1)}, u32[]{:S(2)}, u32[]{:S(2)}) collective-permute-start(f32[32,512]{1,0:T(8,128)S(1)} %get-tuple-element.42), channel_id=1, source_target_pairs={{0,7},{1,2},{2,1},{3,4},{4,3},{5,6},{6,5},{7,0},{8,15},{9,10},{10,... | collective-permute-start | bytes 196616 | tf_op jit(solution)/shard_map/ppermute | solution.py:719
  19.4 6.8 %collective-permute-start.4 = (f32[8,512]{1,0:T(8,128)S(1)}, f32[8,512]{1,0:T(8,128)S(1)}, u32[]{:S(2)}, u32[]{:S(2)}) collective-permute-start(f32[8,512]{1,0:T(8,128)S(1)} %get-tuple-element.39), channel_id=1, source_target_pairs={{0,120},{8,16},{16,8},{24,32},{32,24},{40,48},{48,40},{56,64},{64,... | collective-permute-start | bytes 49160 | tf_op jit(solution)/shard_map/ppermute | solution.py:719
  23.2 3.0 %collective-permute-start.5 = (f32[8,512]{1,0:T(8,128)S(1)}, f32[8,512]{1,0:T(8,128)S(1)}, u32[]{:S(2)}, u32[]{:S(2)}) collective-permute-start(f32[8,512]{1,0:T(8,128)S(1)} %get-tuple-element.40), channel_id=1, source_target_pairs={{0,8},{8,0},{16,24},{24,16},{32,40},{40,32},{48,56},{56,48},{64,72... | collective-permute-start | bytes 49160 | tf_op jit(solution)/shard_map/ppermute | solution.py:719
  27.7 5.0 %collective-permute-start.8 = (f32[80,256]{1,0:T(8,128)S(1)}, f32[80,256]{1,0:T(8,128)S(1)}, u32[]{:S(2)}, u32[]{:S(2)}) collective-permute-start(f32[80,256]{1,0:T(8,128)S(1)} %get-tuple-element.45), channel_id=1, source_target_pairs={{0,1},{1,0},{2,3},{3,2},{4,5},{5,4},{6,7},{7,6},{8,9},{9,8},{10,11... | collective-permute-start | bytes 245768 | tf_op jit(solution)/shard_map/ppermute | solution.py:719
  28.5 6.6 %collective-permute-start.9 = (f32[80,256]{1,0:T(8,128)S(1)}, f32[80,256]{1,0:T(8,128)S(1)}, u32[]{:S(2)}, u32[]{:S(2)}) collective-permute-start(f32[80,256]{1,0:T(8,128)S(1)} %get-tuple-element.46), channel_id=1, source_target_pairs={{0,7},{1,2},{2,1},{3,4},{4,3},{5,6},{6,5},{7,0},{8,15},{9,10},{10,... | collective-permute-start | bytes 245768 | tf_op jit(solution)/shard_map/ppermute | solution.py:719
  35.2 7.1 %collective-permute-start.10 = (f32[40,256]{1,0:T(8,128)S(1)}, f32[40,256]{1,0:T(8,128)S(1)}, u32[]{:S(2)}, u32[]{:S(2)}) collective-permute-start(f32[40,256]{1,0:T(8,128)S(1)} %get-tuple-element.51), channel_id=1, source_target_pairs={{0,120},{8,16},{16,8},{24,32},{32,24},{40,48},{48,40},{56,64},{64,... | collective-permute-start | bytes 122888 | tf_op jit(solution)/shard_map/ppermute | solution.py:719
  37.9 4.4 %collective-permute-start.11 = (f32[40,256]{1,0:T(8,128)S(1)}, f32[40,256]{1,0:T(8,128)S(1)}, u32[]{:S(2)}, u32[]{:S(2)}) collective-permute-start(f32[40,256]{1,0:T(8,128)S(1)} %get-tuple-element.52), channel_id=1, source_target_pairs={{0,8},{8,0},{16,24},{24,16},{32,40},{40,32},{48,56},{56,48},{64,72... | collective-permute-start | bytes 122888 | tf_op jit(solution)/shard_map/ppermute | solution.py:719
  66.5 2.7 %collective-permute-start.12 = (f32[2048,128]{1,0:T(8,128)S(1)}, f32[2048,128]{1,0:T(8,128)S(1)}, u32[]{:S(2)}, u32[]{:S(2)}) collective-permute-start(f32[2048,128]{1,0:T(8,128)S(1)} %bitcast.3), channel_id=1, source_target_pairs={{0,8},{8,0},{16,24},{24,16},{32,40},{40,32},{48,56},{56,48},{64,72... | collective-permute-start | bytes 3145736 | tf_op jit(solution)/shard_map/ppermute | solution.py:719
  78.8 11.0 %collective-permute-start.15 = (f32[32,512]{1,0:T(8,128)S(1)}, f32[32,512]{1,0:T(8,128)S(1)}, u32[]{:S(2)}, u32[]{:S(2)}) collective-permute-start(f32[32,512]{1,0:T(8,128)S(1)} %get-tuple-element.56), channel_id=1, source_target_pairs={{0,1},{1,0},{2,3},{3,2},{4,5},{5,4},{6,7},{7,6},{8,9},{9,8},{10,11... | collective-permute-start | bytes 196616 | tf_op jit(solution)/shard_map/ppermute | solution.py:719
  79.8 10.0 %collective-permute-start.16 = (f32[32,512]{1,0:T(8,128)S(1)}, f32[32,512]{1,0:T(8,128)S(1)}, u32[]{:S(2)}, u32[]{:S(2)}) collective-permute-start(f32[32,512]{1,0:T(8,128)S(1)} %get-tuple-element.57), channel_id=1, source_target_pairs={{0,7},{1,2},{2,1},{3,4},{4,3},{5,6},{6,5},{7,0},{8,15},{9,10},{10,... | collective-permute-start | bytes 196616 | tf_op jit(solution)/shard_map/ppermute | solution.py:719
  83.0 6.8 %collective-permute-start.13 = (f32[8,512]{1,0:T(8,128)S(1)}, f32[8,512]{1,0:T(8,128)S(1)}, u32[]{:S(2)}, u32[]{:S(2)}) collective-permute-start(f32[8,512]{1,0:T(8,128)S(1)} %get-tuple-element.54), channel_id=1, source_target_pairs={{0,120},{8,16},{16,8},{24,32},{32,24},{40,48},{48,40},{56,64},{64,... | collective-permute-start | bytes 49160 | tf_op jit(solution)/shard_map/ppermute | solution.py:719
  84.1 5.8 %collective-permute-start.14 = (f32[8,512]{1,0:T(8,128)S(1)}, f32[8,512]{1,0:T(8,128)S(1)}, u32[]{:S(2)}, u32[]{:S(2)}) collective-permute-start(f32[8,512]{1,0:T(8,128)S(1)} %get-tuple-element.55), channel_id=1, source_target_pairs={{0,8},{8,0},{16,24},{24,16},{32,40},{40,32},{48,56},{56,48},{64,72... | collective-permute-start | bytes 49160 | tf_op jit(solution)/shard_map/ppermute | solution.py:719
